TPU v7x, 32 devices: a whole 2x2x4 slice. The times are simulated.
32 devices in a mesh: frames: 2 (over x), slab: 16 (over z, y, core).
Axes of the slice: x: 2, y: 2, z: 4, core: 2. Of those that a mesh axis runs over, the one named last changes fastest.
Arguments:
- x_image: float32 [2, 384, 128, 384], P(None, 'slab', 'frames'), parts along dimension 2, may hold values from -6 to 6
- residual: float32 [2, 384, 128, 384], P(None, 'slab', 'frames'), parts along dimension 2, may hold values from -6 to 6
- direction: float32 [2, 384, 128, 384], P(None, 'slab', 'frames'), parts along dimension 2, may hold values from -6 to 6
- sensitivity: float32 [2, 2, 384, 64, 384], P(None, None, 'slab'), may hold values from -5 to 5
- tile_block: int32 [256], P('slab'), may hold values from 0 to 1799
- tile_count: int32 [256], P('slab'), may hold values from 1 to 128
- tile_weight: bfloat16 [256, 128, 512], P('slab'), may hold values from -1 to 1
Outputs:
- x_next: float32 [2, 384, 128, 384], P(None, 'slab', 'frames'), parts along dimension 2
- residual_next: float32 [2, 384, 128, 384], P(None, 'slab', 'frames'), parts along dimension 2
- direction_next: float32 [2, 384, 128, 384], P(None, 'slab', 'frames'), parts along dimension 2
There are 2 independent parts, one for each index of `frames`. A program takes and returns all parts, laid end to end along the dimension named above; an argument that names none is the same for every part. Nothing has to cross between parts.
Inputs may be any that keep to these rules, and one draw needn't show every extreme that they name: `tile_block`: tile t belongs to slab t // 16 and names a block of that slab; several tiles may name one block. `tile_count`: samples of a tile at and beyond its count are unused.
All inputs are finite; a program needn't handle non-finite values.
Results may differ from a plain program's by a relative error of at most 0.00065.
The roundings to bfloat16 on the way count: a program that leaves them out, or rounds other values in their place, can miss the bound.
Values sent between devices are 32-bit elements; how exact they have to be, the bound alone decides.
No kernel may reach another device: no remote copies, remote signals or barrier semaphores. Data moves between devices by JAX's collectives and lax.ppermute only.
A program may use at most 192 MiB of HBM per device.

v0:
```python
import math

import jax
import jax.numpy as jnp
from jax import lax
from jax.sharding import PartitionSpec as P

NX = 384
NY = 384
GX = 480
GY = 480


DAMPING = 0.1
HIGHEST = lax.Precision.HIGHEST


def dft_table(size_in, size_out):
    out_index = jnp.arange(size_out, dtype=jnp.int32)[:, None]
    in_index = jnp.arange(size_in, dtype=jnp.int32)[None, :]
    phase_angle = (out_index * in_index % size_out).astype(jnp.float32) * (2.0 * math.pi / size_out)
    scaling = 1.0 / math.sqrt(size_out)
    cosine = jnp.cos(phase_angle) * scaling
    sine_part = jnp.sin(phase_angle) * scaling
    upper_rows = jnp.stack([cosine, sine_part], axis=1)
    lower_rows = jnp.stack([-sine_part, cosine], axis=1)
    return jnp.stack([upper_rows, lower_rows], axis=0)


def grid_tiles(cell_rows, block_ids, sample_count, weights):
    block_total = cell_rows.shape[1]
    samples_tile = weights.shape[1]
    picked = jnp.take(cell_rows, block_ids, axis=1).astype(jnp.bfloat16)
    samples = jnp.einsum("tsc,ktc->kts", weights, picked, preferred_element_type=jnp.float32)
    live_mask = jnp.arange(samples_tile, dtype=jnp.int32)[None, :] < sample_count[:, None]
    samples = jnp.where(live_mask[None], samples, 0.0).astype(jnp.bfloat16)
    spread_back = jnp.einsum("tsc,kts->ktc", weights, samples, preferred_element_type=jnp.float32)
    block_hit = (block_ids[:, None] == jnp.arange(block_total, dtype=jnp.int32)[None, :]).astype(
        jnp.float32
    )
    return jnp.einsum("tb,ktc->kbc", block_hit, spread_back, precision=HIGHEST)


def body(x_image, residual, direction, sensitivity, tile_block, tile_count, tile_weight):
    coil_count = sensitivity.shape[1]
    rows_local = sensitivity.shape[2]
    plane_count = sensitivity.shape[3]
    cells_tile = tile_weight.shape[2]
    slab_count = lax.axis_size("slab")
    lines_local = plane_count * GY // slab_count
    fold_count = max(GY // lines_local, 1)
    line_width = min(lines_local, GY)
    deep_count = plane_count * fold_count // slab_count
    y_table = dft_table(NY, GY).reshape(2, fold_count, line_width, 2, NY)
    y_table = y_table.transpose(3, 4, 1, 0, 2).reshape(2 * NY, 2 * GY)
    x_table = dft_table(NX, GX).transpose(0, 1, 3, 2).reshape(2 * GX, NX * 2)
    sens_re, sens_im = (sensitivity[0], sensitivity[1])
    dir_re, dir_im = (direction[0][None], direction[1][None])
    coil_image = jnp.stack(
        [sens_re * dir_re - sens_im * dir_im, sens_re * dir_im + sens_im * dir_re], axis=3
    )
    coil_image = coil_image.reshape(coil_count * rows_local * plane_count, 2 * NY)
    y_done = jnp.dot(coil_image, y_table, precision=HIGHEST)
    y_done = y_done.reshape(coil_count, rows_local, slab_count, deep_count, 2, line_width)
    pieces = []
    for coil_pos in range(coil_count):
        single = y_done[coil_pos : coil_pos + 1]
        arrived = lax.all_to_all(single, "slab", split_axis=2, concat_axis=1, tiled=True)
        many = arrived.shape[0]
        total_rows = arrived.shape[1]
        lined = arrived.reshape(many, total_rows, deep_count, 2, line_width)
        lined = jnp.swapaxes(lined, 2, 3).reshape(many, total_rows * 2, lines_local)
        grid_data = jnp.einsum("gn,cnl->cgl", x_table, lined, precision=HIGHEST)
        cell_rows = grid_data.reshape(2 * many, -1, cells_tile)
        spread = grid_tiles(cell_rows, tile_block, tile_count, tile_weight)
        spread = spread.reshape(many, 2 * GX, lines_local)
        adjoint = jnp.einsum("gn,cgl->cnl", x_table, spread, precision=HIGHEST)
        adjoint = adjoint.reshape(many, total_rows, 2, deep_count, line_width)
        adjoint = jnp.swapaxes(adjoint, 2, 3)
        pieces.append(
            lax.all_to_all(
                adjoint.reshape(many, total_rows, 1, deep_count, 2, line_width),
                "slab",
                split_axis=1,
                concat_axis=2,
                tiled=True,
            )
        )
    returned = jnp.concatenate(pieces, axis=0)
    returned = returned.reshape(coil_count * rows_local * plane_count, 2 * GY)
    back = lax.dot_general(returned, y_table, (((1,), (1,)), ((), ())), precision=HIGHEST)
    back = back.reshape(coil_count, rows_local, plane_count, 2, NY)
    val_re, val_im = (back[:, :, :, 0], back[:, :, :, 1])
    comb_re = jnp.sum(sens_re * val_re + sens_im * val_im, axis=0)
    comb_im = jnp.sum(sens_re * val_im - sens_im * val_re, axis=0)
    image_ap = jnp.stack([comb_re, comb_im]) + DAMPING * direction
    norm_old, curvature, cross_term, power_term = lax.psum(
        (
            jnp.sum(residual * residual),
            jnp.sum(direction * image_ap),
            jnp.sum(residual * image_ap),
            jnp.sum(image_ap * image_ap),
        ),
        "slab",
    )
    step_size = norm_old / curvature
    x_next = x_image + step_size * direction
    residual_next = residual - step_size * image_ap
    norm_new = norm_old - 2.0 * step_size * cross_term + step_size * step_size * power_term
    direction_next = residual_next + norm_new / norm_old * direction
    return (x_next, residual_next, direction_next)


def solution(mesh):
    placed = (
        P(None, "slab", "frames", None),
        P(None, "slab", "frames", None),
        P(None, "slab", "frames", None),
        P(None, None, "slab", None, None),
        P("slab"),
        P("slab"),
        P("slab", None, None),
    )
    return jax.shard_map(
        body,
        mesh=mesh,
        in_specs=placed,
        out_specs=(
            P(None, "slab", "frames", None),
            P(None, "slab", "frames", None),
            P(None, "slab", "frames", None),
        ),
        check_vma=False,
    )
```

profile of v0, /device:TPU:0, one launch (start us, length us, event | category | flops | bytes accessed | tf_op | source)
XLA Modules:
  0.0 837.5 jit_solution(4427068549957621303)
XLA Ops:
  14.1 14.9 %fusion.7 = (f32[2,24,64,1,384]{4,2,1,0,3:T(8,128)S(1)}, f32[2,24,64,1,384]{4,2,1,0,3:T(8,128)}) fusion(f32[2,2,24,64,384]{4,3,2,1,0:T(8,128)S(1)} %bitcast.181, f32[24,64,384]{2,1,0:T(8,128)S(1)} %get-tuple-element.22, f32[24,64,384]{2,1,0:T(8,128)S(1)} %get-tuple-element.21), kind=kLoop, calls=%fused_computation.20 | loop fusion | flops 7077888 | bytes 23592960 | tf_op jit(solution)/shard_map/sub | solution.py:60
  44.3 31.1 %fusion.44 = f32[3072,960]{0,1:T(8,128)} fusion(f32[3072,768]{1,0:T(8,128)S(1)} %bitcast.193, f32[768,960]{0,1:T(8,128)S(1)} %bitcast.194), kind=kOutput, calls=%fused_computation.88 | convolution fusion | flops 27179089920 | bytes 24182784 | tf_op jit(solution)/shard_map/dot_general | solution.py:63
  75.4 9.8 %fusion.43 = (f32[1536,960]{0,1:T(8,128)}, f32[1536,960]{0,1:T(8,128)}) fusion(f32[3072,960]{0,1:T(8,128)} %fusion.44), kind=kLoop, calls=%fused_computation.87 | loop fusion | bytes 23592960 | tf_op jit(solution)/shard_map/slice | solution.py:67
  91.8 10.3 %slice.35 = f32[1,24,16,4,2,480]{5,4,3,2,1,0:T(2,128)} reshape(f32[1536,960]{1,0:T(8,128)} %copy.52) | data formatting | bytes 11796480 | tf_op jit(solution)/shard_map/slice | solution.py:67
  102.0 9.8 %copy.53 = f32[1,24,16,4,2,480]{5,4,3,1,0,2:T(2,128)} copy(f32[1,24,16,4,2,480]{5,4,3,2,1,0:T(2,128)} %slice.35) | data formatting | bytes 11796480 | tf_op jit(solution)/shard_map/slice | solution.py:67
  125.7 10.3 %slice.37 = f32[1,24,16,4,2,480]{5,4,3,2,1,0:T(2,128)} reshape(f32[1536,960]{1,0:T(8,128)} %copy.62) | data formatting | bytes 11796480 | tf_op jit(solution)/shard_map/slice | solution.py:67
  136.0 9.7 %copy.63 = f32[1,24,16,4,2,480]{5,4,3,1,0,2:T(2,128)} copy(f32[1,24,16,4,2,480]{5,4,3,2,1,0:T(2,128)} %slice.37) | data formatting | bytes 11796480 | tf_op jit(solution)/shard_map/slice | solution.py:67
  145.7 87.8 %all-to-all-done = f32[1,24,16,4,2,480]{5,4,3,1,0,2:T(2,128)} async-done(((f32[1,24,16,4,2,480]{5,4,3,1,0,2:T(2,128)}), f32[1,24,16,4,2,480]{5,4,3,1,0,2:T(2,128)}, u32[]{:S(2)}, u32[]{:S(2)}) %all-to-all-start) | async-done | bytes 5898272 | tf_op jit(solution)/shard_map/all_to_all | solution.py:68
  233.5 28.3 %all-to-all-start.2 = ((f32[1,24,16,4,2,480]{5,4,3,1,0,2:T(2,128)}), f32[1,24,16,4,2,480]{5,4,3,1,0,2:T(2,128)}, u32[]{:S(2)}, u32[]{:S(2)}) async-start(f32[1,24,16,4,2,480]{5,4,3,1,0,2:T(2,128)} %copy.63), calls=%async_computation.2 | async-start | bytes 12582912 | tf_op jit(solution)/shard_map/all_to_all | solution.py:68
  295.6 24.6 %convolution_bitcast_fusion.3 = bf16[1,960,1920]{2,1,0:T(8,128)(2,1)} fusion(f32[768,1920]{1,0:T(8,128)} %reshape.221, f32[960,768]{0,1:T(8,128)} %reshape.222), kind=kOutput, calls=%fused_computation.36 | convolution fusion | flops 16986931200 | bytes 12533760 | tf_op jit(solution)/shard_map/gn,cnl->cgl/dot_general | solution.py:73
  327.6 21.1 %copy.57 = bf16[2,1800,512]{2,0,1:T(2,128)(2,1)} copy(bf16[2,1800,512]{2,1,0:T(8,128)(2,1)} %reshape.223) | data formatting | bytes 7372800 | tf_op jit(solution)/shard_map/reshape | solution.py:74
  366.3 41.6 %convolution_bitcast_fusion.5 = f32[1,768,1920]{1,2,0:T(8,128)} fusion(f32[960,1920]{1,0:T(8,128)} %reshape.224, f32[960,768]{0,1:T(8,128)} %reshape.222), kind=kOutput, calls=%fused_computation.38 | convolution fusion | flops 16986931200 | bytes 16220160 | tf_op jit(solution)/shard_map/gn,cgl->cnl/dot_general | solution.py:77
  414.4 9.8 %reshape.225 = f32[1,384,2,4,480]{4,3,2,1,0:T(4,128)} reshape(f32[1,768,1920]{2,1,0:T(8,128)} %copy.59) | data formatting | bytes 11796480 | tf_op jit(solution)/shard_map/reshape | solution.py:78
  452.1 24.8 %convolution_bitcast_fusion.2 = bf16[1,960,1920]{2,1,0:T(8,128)(2,1)} fusion(f32[768,1920]{1,0:T(8,128)} %reshape.228, f32[960,768]{0,1:T(8,128)} %reshape.222), kind=kOutput, calls=%fused_computation.35 | convolution fusion | flops 16986931200 | bytes 12533760 | tf_op jit(solution)/shard_map/gn,cnl->cgl/dot_general | solution.py:73
  484.3 21.1 %copy.66 = bf16[2,1800,512]{2,0,1:T(2,128)(2,1)} copy(bf16[2,1800,512]{2,1,0:T(8,128)(2,1)} %reshape.229) | data formatting | bytes 7372800 | tf_op jit(solution)/shard_map/reshape | solution.py:74
  523.0 41.6 %convolution_bitcast_fusion.4 = f32[1,768,1920]{1,2,0:T(8,128)} fusion(f32[960,1920]{1,0:T(8,128)} %reshape.230, f32[960,768]{0,1:T(8,128)} %reshape.222), kind=kOutput, calls=%fused_computation.37 | convolution fusion | flops 16986931200 | bytes 16220160 | tf_op jit(solution)/shard_map/gn,cgl->cnl/dot_general | solution.py:77
  571.0 9.8 %reshape.231 = f32[1,384,2,4,480]{4,3,2,1,0:T(4,128)} reshape(f32[1,768,1920]{2,1,0:T(8,128)} %copy.68) | data formatting | bytes 11796480 | tf_op jit(solution)/shard_map/reshape | solution.py:78
  590.4 8.9 %copy.85 = f32[1,16,24,1,4,2,480]{6,5,4,1,2,3,0:T(2,128)} copy(f32[1,16,24,1,4,2,480]{6,4,5,2,1,3,0:T(4,128)} %bitcast.26) | data formatting | bytes 11796480 | tf_op jit(solution)/shard_map/all_to_all | solution.py:81
  599.3 10.3 %concatenate.8 = f32[1,24,64,960]{3,2,1,0:T(8,128)} reshape(f32[1,24,16,1,4,2,480]{6,5,4,2,1,3,0:T(2,128)} %bitcast.186) | data formatting | bytes 11796480 | tf_op jit(solution)/shard_map/concatenate | solution.py:89
  609.6 91.4 %all-to-all-done.3 = f32[1,384,1,4,2,480]{5,3,4,2,0,1:T(4,128)} async-done(((f32[1,384,1,4,2,480]{5,3,4,2,0,1:T(4,128)}), f32[1,384,1,4,2,480]{5,3,4,2,0,1:T(4,128)}, u32[]{:S(2)}, u32[]{:S(2)}) %all-to-all-start.3) | async-done | bytes 5898272 | tf_op jit(solution)/shard_map/all_to_all | solution.py:81
  709.9 10.3 %concatenate.9 = f32[1,24,64,960]{3,2,1,0:T(8,128)} reshape(f32[1,24,16,1,4,2,480]{6,5,4,2,1,3,0:T(2,128)} %bitcast.187) | data formatting | bytes 11796480 | tf_op jit(solution)/shard_map/concatenate | solution.py:89
  720.2 34.7 %fusion = f32[2,24,64,2,384]{4,2,3,1,0:T(8,128)S(1)} fusion(f32[2,384,960,1,1]{1,2,0,4,3:T(8,128)} %bitcast.195, f32[1,24,64,960]{3,2,1,0:T(8,128)} %concatenate.9, f32[1,24,64,960]{3,2,1,0:T(8,128)} %concatenate.8), kind=kOutput, calls=%fused_computation.3 | convolution fusion | flops 27182039040 | bytes 24182784 | tf_op jit(solution)/shard_map/dot_general | solution.py:91
  765.9 56.7 %all-reduce = (f32[]{:T(128)}, f32[]{:T(128)}, f32[]{:T(128)}, f32[]{:T(128)}) all-reduce(f32[]{:T(128)} %get-tuple-element.9, f32[]{:T(128)} %get-tuple-element.8, f32[]{:T(128)} %get-tuple-element.7, f32[]{:T(128)} %get-tuple-element.6), channel_id=1, replica_groups=mesh['frames'=2,'slab'=16] {'slab'}, use_global_device_ids=true, to_apply=%region_1.2 | all-reduce | flops 4 | bytes 32 | tf_op jit(solution)/shard_map/psum | solution.py:97
  826.3 11.0 %multiply_add_fusion = (f32[2,24,64,384]{3,2,1,0:T(8,128)}, f32[2,24,64,384]{3,2,1,0:T(8,128)}, f32[2,24,64,384]{3,2,1,0:T(8,128)}) fusion(f32[2,24,64,384]{3,2,1,0:T(8,128)} %param.11, f32[]{:T(128)S(6)} %div.7, f32[2,24,64,384]{3,2,1,0:T(8,128)} %param.10, f32[1,24,64,384]{3,2,1,0:T(8,128)} %bitcast.191, f32[1,24,64,384]{3,2,1,0:T(8,128)} %bitcast.189, ...), kind=kLoop, calls=%fused_computation.26 | loop fusion | flops 10616832 | bytes 33030152 | tf_op jit(solution)/shard_map/add | solution.py:110
  (74 shorter events, 203.2 us)
Async XLA Ops:
  0.6 350.7 %copy-start = (bf16[16,128,512]{2,1,0:T(8,128)(2,1)S(1)}, bf16[16,128,512]{2,1,0:T(8,128)(2,1)}, u32[]{:S(2)}) copy-start(bf16[16,128,512]{2,1,0:T(8,128)(2,1)} %param.15) | copy-start | bytes 6291460
  6.7 4.5 slice-start
  8.7 2.5 copy-start.1
  8.7 2.5 slice-start.1
  8.7 3.8 slice-start.4
  11.0 2.9 slice-start.5
  11.2 2.9 slice-start.6
  111.8 121.6 %all-to-all-start = ((f32[1,24,16,4,2,480]{5,4,3,1,0,2:T(2,128)}), f32[1,24,16,4,2,480]{5,4,3,1,0,2:T(2,128)}, u32[]{:S(2)}, u32[]{:S(2)}) async-start(f32[1,24,16,4,2,480]{5,4,3,1,0,2:T(2,128)} %copy.53), calls=%async_computation | async-start | bytes 12582912 | tf_op jit(solution)/shard_map/all_to_all | solution.py:68
  233.5 190.7 %all-to-all-start.2 = ((f32[1,24,16,4,2,480]{5,4,3,1,0,2:T(2,128)}), f32[1,24,16,4,2,480]{5,4,3,1,0,2:T(2,128)}, u32[]{:S(2)}, u32[]{:S(2)}) async-start(f32[1,24,16,4,2,480]{5,4,3,1,0,2:T(2,128)} %copy.63), calls=%async_computation.2 | async-start | bytes 12582912 | tf_op jit(solution)/shard_map/all_to_all | solution.py:68
  261.8 11.9 %copy-start.4 = (s32[16]{0:T(128)S(1)}, s32[16]{0:T(128)}, u32[]{:S(2)}) copy-start(s32[16]{0:T(128)} %param.13) | copy-start | bytes 196
  261.8 11.9 %copy-start.5 = (s32[16]{0:T(128)S(1)}, s32[16]{0:T(128)}, u32[]{:S(2)}) copy-start(s32[16]{0:T(128)} %param.14) | copy-start | bytes 196
  424.2 156.6 %all-to-all-start.1 = ((f32[1,384,1,4,2,480]{5,3,4,2,0,1:T(4,128)}), f32[1,384,1,4,2,480]{5,3,4,2,0,1:T(4,128)}, u32[]{:S(2)}, u32[]{:S(2)}) async-start(f32[1,384,1,4,2,480]{5,3,4,2,0,1:T(4,128)} %bitcast.182), calls=%async_computation.1 | async-start | bytes 12582912 | tf_op jit(solution)/shard_map/all_to_all | solution.py:81
  580.8 120.2 %all-to-all-start.3 = ((f32[1,384,1,4,2,480]{5,3,4,2,0,1:T(4,128)}), f32[1,384,1,4,2,480]{5,3,4,2,0,1:T(4,128)}, u32[]{:S(2)}, u32[]{:S(2)}) async-start(f32[1,384,1,4,2,480]{5,3,4,2,0,1:T(4,128)} %bitcast.183), calls=%async_computation.3 | async-start | bytes 12582912 | tf_op jit(solution)/shard_map/all_to_all | solution.py:81
  709.9 50.5 %slice-start.2 = ((s8[4718592]{0:T(1024)(128)(4,1)}), s8[524288]{0:T(1024)(128)(4,1)S(1)}, s32[]{:S(2)}) async-start(s8[4718592]{0:T(1024)(128)(4,1)} %bitcast.177), calls=%async_computation.6 | async-start | bytes 1048576
  720.2 40.1 %slice-start.3 = ((s8[4718592]{0:T(1024)(128)(4,1)}), s8[4194304]{0:T(1024)(128)(4,1)S(1)}, s32[]{:S(2)}) async-start(s8[4718592]{0:T(1024)(128)(4,1)} %bitcast.177), calls=%async_computation.7 | async-start | bytes 8388608
  760.3 5.6 copy-start.2
  760.3 5.6 copy-start.3
where the time goes:
time: 848 us; the launch traced here: 837 us
  local copies, waits for them, and re-layouts  290 us (34%)
  matrix products  211 us (25%)
  waiting for transfers between devices  179 us (21%)
  blocking collectives  56.7 us (7%)
  other arithmetic  48.2 us (6%)
  starting transfers between devices  47.9 us (6%)
    all_to_all x2, waiting for transfers between devices, body(): lax.all_to_all(adjoint.reshape(many, total_rows, 1, deep_count, 2, line_w...  91.4 us
    all_to_all x2, waiting for transfers between devices, body(): lax.all_to_all(single, 'slab', split_axis=2, concat_axis=1, tiled=True)  87.8 us
    dot_general x2, matrix products, body(): adjoint = jnp.einsum('gn,cgl->cnl', x_table, spread, precision=HIGHEST)  83.2 us
    slice x7, local copies, waits for them, and re-layouts, body(): single = y_done[coil_pos:coil_pos + 1]  62.8 us
    reshape x4, local copies, waits for them, and re-layouts, body(): cell_rows = grid_data.reshape(2 * many, -1, cells_tile)  57 us
    psum x1, blocking collectives, body(): lax.psum((jnp.sum(residual * residual), jnp.sum(direction * image_ap), jn...  56.7 us
    dot_general x2, matrix products, body(): grid_data = jnp.einsum('gn,cnl->cgl', x_table, lined, precision=HIGHEST)  49.4 us
    all_to_all x2, starting transfers between devices, body(): lax.all_to_all(single, 'slab', split_axis=2, concat_axis=1, tiled=True)  35.7 us
  transfers between devices with their start and end apart: 4, of which 2 were waited for; matrix products, arithmetic and copies ran while one was open for 43% of the time, Pallas kernels for 0%

commit v1 on v0

v1 whole, which is shorter than its diff:
```python
import math

import jax
import jax.numpy as jnp
import ml_dtypes
import numpy as np
from jax import lax
from jax.experimental import pallas as pl
from jax.experimental.pallas import tpu as pltpu
from jax.sharding import PartitionSpec as P

GX = 480
GY = 480
DAMPING = 0.1
HIGHEST = lax.Precision.HIGHEST
F32 = jnp.float32
BF16 = jnp.bfloat16
VMEM_LIMIT = 56 * 1024 * 1024
FIELDS = 8


def dft(out_index, in_index, size, scaled=True):
    angle = (out_index[:, None] * in_index[None, :] % size) * (2.0 * math.pi / size)
    scale = 1.0 / math.sqrt(size) if scaled else 1.0
    return np.cos(angle) * scale, np.sin(angle) * scale


def table_parts(table, count):
    parts = []
    for _ in range(count):
        part = table.astype(ml_dtypes.bfloat16)
        parts.append(part)
        table = table - part.astype(np.float64)
    return np.stack(parts)


def split(value, count):
    parts = []
    for step in range(count):
        part = value.astype(BF16)
        parts.append(part)
        if step + 1 < count:
            value = value - part.astype(F32)
    return parts


def dot(a, b):
    return lax.dot_general(a, b, (((1,), (0,)), ((), ())), preferred_element_type=F32)


def six_products(lhs, rhs):
    rows = lhs[0].shape[0]
    first = dot(jnp.concatenate(lhs, axis=0), rhs[0])
    second = dot(jnp.concatenate(lhs[:2], axis=0), rhs[1])
    third = dot(lhs[0], rhs[2])
    small = first[2 * rows :] + second[rows:] + third
    return first[:rows] + (first[rows : 2 * rows] + second[:rows] + small)


def params():
    return pltpu.CompilerParams(vmem_limit_bytes=VMEM_LIMIT)


def coil_kernel(sens_ref, dir_ref, res_ref, out_ref, sums_ref):
    coils, rows, planes, width = sens_ref.shape[1:]
    half = rows * planes
    chunk = max(16 // planes, 1)

    @pl.when(pl.program_id(0) == 0)
    def _():
        sums_ref[...] = jnp.zeros(sums_ref.shape, F32)

    def step(index, carry):
        at = pl.ds(index * chunk, chunk)
        to = index * chunk * planes
        d_re, d_im = dir_ref[0, at], dir_ref[1, at]
        r_re, r_im = res_ref[0, at], res_ref[1, at]
        sums_ref[0] += jnp.sum(r_re * r_re + r_im * r_im, axis=0)
        sums_ref[1] += jnp.sum(d_re * d_re + d_im * d_im, axis=0)
        for coil in range(coils):
            s_re, s_im = sens_ref[0, coil, at], sens_ref[1, coil, at]
            pair = (s_re * d_re - s_im * d_im, s_re * d_im + s_im * d_re)
            for ri, value in enumerate(pair):
                value = value.reshape(chunk * planes, width)
                where = pl.ds(pl.multiple_of(ri * half + to, 16), chunk * planes)
                for number, part in enumerate(split(value, 3)):
                    out_ref[0, number, where, coil * width : (coil + 1) * width] = part
        return carry

    lax.fori_loop(0, rows // chunk, step, 0)


def coil_images(sens, direction, residual, planes):
    _, coils, rows, total, width = sens.shape
    groups = total // planes
    depth = 2 * rows * planes
    return pl.pallas_call(
        coil_kernel,
        grid=(groups,),
        in_specs=[
            pl.BlockSpec((2, coils, rows, planes, width), lambda i: (0, 0, 0, i, 0)),
            pl.BlockSpec((2, rows, planes, width), lambda i: (0, 0, i, 0)),
            pl.BlockSpec((2, rows, planes, width), lambda i: (0, 0, i, 0)),
        ],
        out_specs=[
            pl.BlockSpec((1, 3, depth, coils * width), lambda i: (i, 0, 0, 0)),
            pl.BlockSpec((2, planes, width), lambda i: (0, 0, 0)),
        ],
        out_shape=[
            jax.ShapeDtypeStruct((groups, 3, depth, coils * width), BF16),
            jax.ShapeDtypeStruct((2, planes, width), F32),
        ],
        compiler_params=params(),
        name="coil_images",
    )(sens, direction, residual)


def row_matrix(info, table_ref, planes, parts):
    rows = info.shape[0]
    half = rows // 2
    depth = table_ref.shape[3]
    hot = lax.broadcasted_iota(jnp.int32, (rows, GX), 1) == info[:, 0:1]
    hot = jnp.where(hot, 1.0, 0.0)
    hot_low = hot.astype(BF16)
    live = lax.broadcasted_iota(jnp.int32, (rows, depth), 1) % planes == info[:, 1:2]
    matrix = []
    for part in range(parts):
        upper = jnp.where(live, dot(hot_low, table_ref[part, 0]), 0.0)
        lower = jnp.where(live, dot(hot_low, table_ref[part, 1]), 0.0)
        stack = [upper[:half], lower[:half], upper[half:], lower[half:]]
        matrix.append(jnp.concatenate(stack, axis=0).astype(BF16))
    return matrix, hot


def rows_kernel(planes, me_ref, info_ref, image_ref, table_ref, turn_ref, keep_ref, send_ref):
    count = info_ref.shape[2]
    info = info_ref[0].reshape(2 * count, FIELDS)
    matrix, hot = row_matrix(info, table_ref, planes, 3)
    turn = jnp.dot(hot, turn_ref[...], precision=HIGHEST, preferred_element_type=F32)
    cos, sin = turn[:, 0:1], turn[:, 1:2]
    out = six_products(matrix, [image_ref[0, part] for part in range(3)])
    for slab, ref in enumerate((keep_ref, send_ref)):
        re = out[2 * slab * count : (2 * slab + 1) * count]
        im = out[(2 * slab + 1) * count : (2 * slab + 2) * count]
        c = cos[slab * count : (slab + 1) * count]
        s = sin[slab * count : (slab + 1) * count]
        ref[0, :count] = c * re + s * im
        ref[0, count:] = c * im - s * re


def partial_rows(me, info, images, table, turn, planes, slabs_group):
    pairs, _, count, _ = info.shape
    _, _, depth, width = images.shape
    whole = jax.ShapeDtypeStruct((pairs, 2 * count, width), F32)
    block = pl.BlockSpec((1, 2 * count, width), lambda q, me: (q, 0, 0))
    return pl.pallas_call(
        lambda *refs: rows_kernel(planes, *refs),
        grid_spec=pltpu.PrefetchScalarGridSpec(
            num_scalar_prefetch=1,
            grid=(pairs,),
            in_specs=[
                pl.BlockSpec((1, 2, count, FIELDS), lambda q, me: (q, 0, 0, 0)),
                pl.BlockSpec(
                    (1, 3, depth, width),
                    lambda q, me: (lax.bitwise_xor(2 * q, me[0]) // slabs_group, 0, 0, 0),
                ),
                pl.BlockSpec(table.shape, lambda q, me: (0, 0, 0, 0)),
                pl.BlockSpec(turn.shape, lambda q, me: (0, 0)),
            ],
            out_specs=[block, block],
        ),
        out_shape=[whole, whole],
        compiler_params=params(),
        name="partial_rows",
    )(me, info, images, table, turn)


def start_turn(info_ref, start_ref):
    pairs, _, count, _ = info_ref.shape
    info = info_ref[...].reshape(pairs * count, FIELDS)
    starts = start_ref.shape[0]
    hot = lax.broadcasted_iota(jnp.int32, (pairs * count, starts), 1) == info[:, 2:3]
    turn = jnp.dot(
        jnp.where(hot, 1.0, 0.0), start_ref[...], precision=HIGHEST, preferred_element_type=F32
    )
    width = turn.shape[1] // 2
    return info, turn[:, :width], turn[:, width:]


def segment_mask(info, cells, segment):
    at = lax.broadcasted_iota(jnp.int32, (info.shape[0], 2 * cells), 1) % cells
    return (at >= info[:, 3:4]) & (at < info[:, 3:4] + segment)


def cells_kernel(tiles, segment, keep_ref, got_ref, info_ref, start_ref, table_ref, *out_refs):
    pairs, count, _ = keep_ref.shape
    count = count // 2
    cells = out_refs[0].shape[2] // 2
    info, cos, sin = start_turn(info_ref, start_ref)
    width = cos.shape[1]
    values = []
    for coil in range(len(out_refs)):
        lanes = slice(coil * width, (coil + 1) * width)
        both = keep_ref[:, :, lanes] + got_ref[:, :, lanes]
        re = both[:, :count].reshape(pairs * count, width)
        im = both[:, count:].reshape(pairs * count, width)
        values.append(jnp.concatenate([cos * re + sin * im, cos * im - sin * re], axis=1))
    value = split(jnp.concatenate(values, axis=0), 3)
    out = six_products(value, [table_ref[part] for part in range(3)])
    mask = segment_mask(info, cells, segment)
    for coil, ref in enumerate(out_refs):
        mine = jnp.where(mask, out[coil * pairs * count : (coil + 1) * pairs * count], 0.0)
        mine = mine.reshape(pairs, count // tiles, tiles, 2 * cells)
        ref[...] = jnp.sum(mine, axis=1)


def row_cells(keep, got, info, start, table, tiles, segment, coils, chunk):
    pairs, double, width = keep.shape
    lines = table.shape[2]
    rows = pl.BlockSpec((chunk, double, width), lambda i: (i, 0, 0))
    whole = jax.ShapeDtypeStruct((pairs, tiles, lines), F32)
    return pl.pallas_call(
        lambda *refs: cells_kernel(tiles, segment, *refs),
        grid=(pairs // chunk,),
        in_specs=[
            rows,
            rows,
            pl.BlockSpec((chunk, 1, double // 2, FIELDS), lambda i: (i, 0, 0, 0)),
            pl.BlockSpec(start.shape, lambda i: (0, 0)),
            pl.BlockSpec(table.shape, lambda i: (0, 0, 0), pipeline_mode=pl.Buffered(1)),
        ],
        out_specs=[pl.BlockSpec((chunk, tiles, lines), lambda i: (i, 0, 0))] * coils,
        out_shape=[whole] * coils,
        compiler_params=params(),
        name="row_cells",
    )(keep, got, info, start, table)


def adjoint_kernel(tiles, segment, coils, *refs):
    cell_refs, (info_ref, start_ref, table_ref, out_ref) = refs[:coils], refs[coils:]
    pairs, _, count, _ = info_ref.shape
    cells = cell_refs[0].shape[2] // 2
    info, cos, sin = start_turn(info_ref, start_ref)
    width = cos.shape[1]
    mask = segment_mask(info, cells, segment)
    values = []
    for ref in cell_refs:
        wide = jnp.concatenate([ref[...][:, None]] * (count // tiles), axis=1)
        values.append(jnp.where(mask, wide.reshape(pairs * count, 2 * cells), 0.0))
    rows = coils * pairs * count
    high, low = split(jnp.concatenate(values, axis=0), 2)
    first = dot(jnp.concatenate([high, low], axis=0), table_ref[0])
    out = first[:rows] + (first[rows:] + dot(high, table_ref[1]))
    for coil in range(coils):
        mine = out[coil * pairs * count : (coil + 1) * pairs * count]
        re, im = mine[:, :width], mine[:, width:]
        lanes = slice(coil * width, (coil + 1) * width)
        out_ref[:, :count, lanes] = (cos * re - sin * im).reshape(pairs, count, width)
        out_ref[:, count:, lanes] = (cos * im + sin * re).reshape(pairs, count, width)


def adjoint_rows(spread, info, start, table, tiles, segment, chunk):
    coils = len(spread)
    pairs, _, lines = spread[0].shape
    count = info.shape[2]
    width = coils * table.shape[2] // 2
    return pl.pallas_call(
        lambda *refs: adjoint_kernel(tiles, segment, coils, *refs),
        grid=(pairs // chunk,),
        in_specs=[pl.BlockSpec((chunk, tiles, lines), lambda i: (i, 0, 0))] * coils
        + [
            pl.BlockSpec((chunk, 1, count, FIELDS), lambda i: (i, 0, 0, 0)),
            pl.BlockSpec(start.shape, lambda i: (0, 0)),
            pl.BlockSpec(table.shape, lambda i: (0, 0, 0), pipeline_mode=pl.Buffered(1)),
        ],
        out_specs=pl.BlockSpec((chunk, 2 * count, width), lambda i: (i, 0, 0)),
        out_shape=jax.ShapeDtypeStruct((pairs, 2 * count, width), F32),
        compiler_params=params(),
        name="adjoint_rows",
    )(*spread, info, start, table)


def tiles_kernel(coils, *refs):
    count_ref, cell_refs = refs[0], refs[1 : 1 + coils]
    weight_ref, out_refs, dot_ref = refs[1 + coils], refs[2 + coils : 2 + 2 * coils], refs[-1]
    tiles, samples, cells = weight_ref.shape
    total = jnp.zeros((2 * coils, cells), F32)
    for tile in range(tiles):
        grid = jnp.concatenate(
            [
                ref[tile : tile + 1, ri * cells : (ri + 1) * cells]
                for ref in cell_refs
                for ri in range(2)
            ],
            axis=0,
        )
        weight = weight_ref[tile]
        found = lax.dot_general(
            grid.astype(BF16), weight, (((1,), (1,)), ((), ())), preferred_element_type=F32
        )
        live = lax.broadcasted_iota(jnp.int32, found.shape, 1) < count_ref[tile]
        found = jnp.where(live, found, 0.0).astype(BF16)
        spread = dot(found, weight)
        total += grid * spread
        for coil, ref in enumerate(out_refs):
            for ri in range(2):
                row = 2 * coil + ri
                ref[tile : tile + 1, ri * cells : (ri + 1) * cells] = spread[row : row + 1]
    dot_ref[...] = total


def run_tiles(count, cells, weight):
    coils = len(cells)
    lines = cells[0].shape[1]
    vmem = pl.BlockSpec(memory_space=pltpu.VMEM)
    whole = jax.ShapeDtypeStruct(cells[0].shape, F32)
    *spread, total = pl.pallas_call(
        lambda *refs: tiles_kernel(coils, *refs),
        in_specs=[pl.BlockSpec(memory_space=pltpu.SMEM)] + [vmem] * (coils + 1),
        out_specs=[vmem] * (coils + 1),
        out_shape=[whole] * coils + [jax.ShapeDtypeStruct((2 * coils, lines // 2), F32)],
        compiler_params=params(),
        name="tiles",
    )(count, *cells, weight)
    return spread, total


def finish_kernel(
    planes, depth_pairs, me_ref, step_ref, info_ref, mine_ref, got_ref, sens_ref, dir_ref, res_ref,
    table_ref, turn_ref, out_ref, norm_ref, *scratch,
):
    count = info_ref.shape[2]
    coils, rows, _, width = sens_ref.shape[1:]
    half = rows * planes
    group, pair = pl.program_id(0), pl.program_id(1)
    info = info_ref[0].reshape(2 * count, FIELDS)
    matrix, hot = row_matrix(info, table_ref, planes, 2)
    turn = jnp.dot(hot, turn_ref[...], precision=HIGHEST, preferred_element_type=F32)
    values = []
    for slab, ref in enumerate((mine_ref, got_ref)):
        re, im = ref[0, :count], ref[0, count:]
        c = turn[slab * count : (slab + 1) * count, 0:1]
        s = turn[slab * count : (slab + 1) * count, 1:2]
        values += [c * re - s * im, c * im + s * re]
    high, low = split(jnp.concatenate(values, axis=0), 2)
    left = jnp.concatenate([matrix[0], matrix[1], matrix[0]], axis=0)
    right = jnp.concatenate([high, high, low], axis=0)
    back = lax.dot_general(left, right, (((0,), (0,)), ((), ())), preferred_element_type=F32)

    @pl.when((group == 0) & (pair == 0))
    def _():
        norm_ref[...] = jnp.zeros(norm_ref.shape, F32)

    def combine(back):
        direction = [dir_ref[ri].reshape(half, width) for ri in range(2)]
        total = [DAMPING * direction[0], DAMPING * direction[1]]
        for coil in range(coils):
            lanes = slice(coil * width, (coil + 1) * width)
            v_re, v_im = back[:half, lanes], back[half:, lanes]
            s_re = sens_ref[0, coil].reshape(half, width)
            s_im = sens_ref[1, coil].reshape(half, width)
            total[0] += s_re * v_re + s_im * v_im
            total[1] += s_re * v_im - s_im * v_re
        squares = 0.0
        for ri in range(2):
            value = res_ref[ri].reshape(half, width) - step_ref[0] * total[ri]
            out_ref[ri] = value.reshape(rows, planes, width)
            squares = squares + jnp.sum((value * value).reshape(rows, planes, width), axis=0)
        norm_ref[...] += squares

    if depth_pairs == 1:
        combine(back)
    else:
        sum_ref = scratch[0]

        @pl.when(pair == 0)
        def _():
            sum_ref[...] = back

        @pl.when(pair > 0)
        def _():
            sum_ref[...] += back

        @pl.when(pair == depth_pairs - 1)
        def _():
            combine(sum_ref[...])


def finish(me, step, info, mine, got, sens, direction, residual, table, turn, planes, slabs_group):
    _, coils, rows, total, width = sens.shape
    pairs, _, count, _ = info.shape
    groups, deep = total // planes, slabs_group // 2
    wide = coils * width

    def place(i, j, me):
        return lax.bitwise_xor(i * slabs_group, me[0]) // slabs_group

    row_block = pl.BlockSpec((1, 2 * count, wide), lambda i, j, me: (i * deep + j, 0, 0))
    image = pl.BlockSpec((2, rows, planes, width), lambda i, j, me: (0, 0, place(i, j, me), 0))
    return pl.pallas_call(
        lambda *refs: finish_kernel(planes, deep, *refs),
        grid_spec=pltpu.PrefetchScalarGridSpec(
            num_scalar_prefetch=1,
            grid=(groups, deep),
            in_specs=[
                pl.BlockSpec(memory_space=pltpu.SMEM),
                pl.BlockSpec(
                    (1, 2, count, FIELDS), lambda i, j, me: (i * deep + j, 0, 0, 0)
                ),
                row_block,
                row_block,
                pl.BlockSpec(
                    (2, coils, rows, planes, width),
                    lambda i, j, me: (0, 0, 0, place(i, j, me), 0),
                ),
                image,
                image,
                pl.BlockSpec(table.shape, lambda i, j, me: (0, 0, 0, 0)),
                pl.BlockSpec(turn.shape, lambda i, j, me: (0, 0)),
            ],
            out_specs=[image, pl.BlockSpec((planes, width), lambda i, j, me: (0, 0))],
            scratch_shapes=[pltpu.VMEM((2 * rows * planes, wide), F32)] if deep > 1 else [],
        ),
        out_shape=[
            jax.ShapeDtypeStruct(residual.shape, F32),
            jax.ShapeDtypeStruct((planes, width), F32),
        ],
        compiler_params=params(),
        name="finish",
    )(me, step, info, mine, got, sens, direction, residual, table, turn)


def swap(value, bit, slabs):
    return lax.ppermute(value, "slab", [(i, i ^ bit) for i in range(slabs)])


def sum_scatter(value, bits, slabs):
    dims = value.shape[1:]
    value = value.reshape((2,) * len(bits) + dims)
    left = sorted(bits, reverse=True)
    for bit in bits:
        axis = left.index(bit)
        left.pop(axis)
        keep = lax.index_in_dim(value, 0, axis, keepdims=False)
        send = lax.index_in_dim(value, 1, axis, keepdims=False)
        value = keep + swap(send, bit, slabs)
    return value


def gather(value, bits, slabs):
    dims = value.shape
    have = []
    for bit in bits:
        other = swap(value, bit, slabs)
        axis = sum(1 for b in have if b > bit)
        value = jnp.stack([value, other], axis=axis)
        have.append(bit)
    return value.reshape((2 ** len(bits),) + dims)


def body(x_image, residual, direction, sensitivity, tile_block, tile_count, tile_weight):
    _, coils, rows, plane_count, ny = sensitivity.shape
    tiles, _, cells = tile_weight.shape
    slabs = lax.axis_size("slab")
    me = lax.axis_index("slab")
    lines = plane_count * GY // slabs
    segment = min(lines, GY)
    per_gx = lines // segment
    unit = math.gcd(cells, segment)
    segments = -(-(segment - unit + cells) // segment)
    planes = 8 if rows % 2 == 0 else 16
    slabs_group = planes * GY // lines
    pairs = slabs // 2
    bits = [1 << i for i in range(slabs.bit_length() - 1)]

    first = tile_block * cells
    start = first % segment
    base = (me * lines) % GY
    info = []
    for k in range(segments):
        row = jnp.minimum(first // segment + k, GX * per_gx - 1)
        plane = (me * lines + (row % per_gx) * segment) // GY
        turn = (base + start - segment * k) % GY // unit
        fields = [row // per_gx, plane % planes, turn, segment * k - start]
        info.append(jnp.stack(fields + [jnp.zeros_like(row)] * (FIELDS - len(fields)), axis=1))
    info = jnp.concatenate(info, axis=0)
    info = gather(info, bits, slabs).reshape(pairs, 2, segments * tiles, FIELDS)

    x_cos, x_sin = dft(np.arange(GX), np.repeat(np.arange(rows), planes), GX)
    x_table = np.stack([np.hstack([x_cos, x_sin]), np.hstack([-x_sin, x_cos])])
    x_table = jnp.asarray(table_parts(x_table, 3))
    y_cos, y_sin = dft(np.arange(ny), np.arange(cells), GY)
    y_table = np.vstack([np.hstack([y_cos, -y_sin]), np.hstack([y_sin, y_cos])])
    y_forward = jnp.asarray(table_parts(y_table, 3))
    y_back = jnp.asarray(table_parts(y_table.T, 2))
    start_table = np.hstack(dft(np.arange(GY // unit) * unit, np.arange(ny), GY, False))
    start_table = np.pad(start_table, ((0, -start_table.shape[0] % 8), (0, 0)))
    start_table = jnp.asarray(start_table.astype(np.float32))
    angle = (jnp.arange(GX, dtype=jnp.int32) * (me * rows) % GX).astype(F32) * (2 * math.pi / GX)
    turn = jnp.stack([jnp.cos(angle), jnp.sin(angle)], axis=1)
    turn = jnp.pad(turn, ((0, 0), (0, 126)))
    me_array = me.astype(jnp.int32)[None]

    images, sums = coil_images(sensitivity, direction, residual, planes)
    keep, send = partial_rows(me_array, info, images, x_table, turn, planes, slabs_group)
    got = swap(send, 1, slabs)
    chunk = min(pairs, 4)
    grid = row_cells(
        keep, got, info, start_table, y_forward, tiles, segment, coils, chunk
    )
    high_bits = bits[1:]
    orders = [high_bits[c % len(high_bits) :] + high_bits[: c % len(high_bits)] for c in range(coils)]
    grid = [sum_scatter(value, order, slabs) for value, order in zip(grid, orders)]

    spread, products = run_tiles(tile_count, grid, tile_weight)

    local = jnp.sum(sums, axis=(1, 2))
    scalars = jnp.stack([local[0], jnp.sum(products) + DAMPING * local[1]])
    for bit in bits:
        scalars = scalars + swap(scalars, bit, slabs)
    norm_old = scalars[0]
    step_size = norm_old / scalars[1]

    spread = [gather(value, order[::-1], slabs) for value, order in zip(spread, orders)]
    mine = adjoint_rows(spread, info, start_table, y_back, tiles, segment, chunk)
    other = swap(mine, 1, slabs)
    residual_next, squares = finish(
        me_array, step_size[None], info, mine, other, sensitivity, direction, residual, x_table, turn,
        planes, slabs_group,
    )
    norm_new = jnp.sum(squares)[None]
    for bit in bits:
        norm_new = norm_new + swap(norm_new, bit, slabs)
    x_next = x_image + step_size * direction
    direction_next = residual_next + norm_new[0] / norm_old * direction
    return (x_next, residual_next, direction_next)


def solution(mesh):
    image = P(None, "slab", "frames", None)
    placed = (image, image, image, P(None, None, "slab", None, None)) + (
        P("slab"),
        P("slab"),
        P("slab", None, None),
    )
    return jax.shard_map(
        body, mesh=mesh, in_specs=placed, out_specs=(image, image, image), check_vma=False
    )
```

time: 848 us -> 191 us (0.23); the launches traced: 837 us -> 190 us
  local copies, waits for them, and re-layouts: 290 us -> 8.96 us
  matrix products: 211 us -> 0 us
  waiting for transfers between devices: 179 us -> 47 us
  Pallas kernels: 0 us -> 69.8 us
  blocking collectives: 56.7 us -> 0 us
  other arithmetic: 48.2 us -> 20.8 us
  starting transfers between devices: 47.9 us -> 35.9 us
    dot_general x10 -> x0, matrix products: 211 us -> none  [the longest x2 83.2 us: body(): adjoint = jnp.einsum('gn,cgl->cnl', x_table, spread, precision=HIGHEST)]
    all_to_all x4 -> x0, waiting for transfers between devices: 179 us -> none  [the longest x2 91.4 us: body(): lax.all_to_all(adjoint.reshape(many, total_rows, 1, deep_count, 2, line_w...]
    reshape x7 -> x0, local copies, waits for them, and re-layouts: 82.7 us -> none  [the longest x4 57 us: body(): cell_rows = grid_data.reshape(2 * many, -1, cells_tile)]
    pallas_call x0 -> x6, Pallas kernels: none -> 69.8 us  [the longest x1 17.9 us: finish(): pl.pallas_call(lambda *refs: finish_kernel(planes, deep, *refs), grid_spe...]
    slice x7 -> x3, local copies, waits for them, and re-layouts: 62.8 us -> 2.24 us  [the longest x1 1.06 us: sum_scatter(): keep = lax.index_in_dim(value, 0, axis, keepdims=False)]
    psum x1 -> x0, blocking collectives: 56.7 us -> none  [body(): lax.psum((jnp.sum(residual * residual), jnp.sum(direction * image_ap), jn...]
    all_to_all x4 -> x0, starting transfers between devices: 47.9 us -> none  [the longest x2 35.7 us: body(): lax.all_to_all(single, 'slab', split_axis=2, concat_axis=1, tiled=True)]
    ppermute x0 -> x26, waiting for transfers between devices: none -> 47 us  [swap(): return lax.ppermute(value, 'slab', [(i, i ^ bit) for i in range(slabs)])]
  transfers between devices with their start and end apart: 4 -> 26, of which waited for: 2 -> 22; matrix products, arithmetic and copies ran while one was open for 43% -> 6% of each run, Pallas kernels for 0% -> 8%
where the time goes in v1:
time: 191 us; the launch traced here: 190 us
  Pallas kernels  69.8 us (37%)
  waiting for transfers between devices  47 us (25%)
  starting transfers between devices  35.9 us (19%)
  other arithmetic  20.8 us (11%)
  local copies, waits for them, and re-layouts  8.96 us (5%)
  between operations  7.42 us (4%)
    ppermute x26, waiting for transfers between devices, swap(): return lax.ppermute(value, 'slab', [(i, i ^ bit) for i in range(slabs)])  47 us
    ppermute x26, starting transfers between devices, swap(): return lax.ppermute(value, 'slab', [(i, i ^ bit) for i in range(slabs)])  35.9 us
    pallas_call x1, Pallas kernels, finish(): pl.pallas_call(lambda *refs: finish_kernel(planes, deep, *refs), grid_spe...  17.9 us
    pallas_call x1, Pallas kernels, partial_rows(): pl.pallas_call(lambda *refs: rows_kernel(planes, *refs), grid_spec=pltpu....  14.7 us
    pallas_call x1, Pallas kernels, coil_images(): pl.pallas_call(coil_kernel, grid=(groups,), in_specs=[pl.BlockSpec((2, co...  14.7 us
    add x1, other arithmetic, body(): direction_next = residual_next + norm_new[0] / norm_old * direction  11.4 us
    pallas_call x1, Pallas kernels, row_cells(): pl.pallas_call(lambda *refs: cells_kernel(tiles, segment, *refs), grid=(p...  10.3 us
    pallas_call x1, Pallas kernels, adjoint_rows(): pl.pallas_call(lambda *refs: adjoint_kernel(tiles, segment, coils, *refs)...  6.56 us
  transfers between devices with their start and end apart: 26, of which 22 were waited for; matrix products, arithmetic and copies ran while one was open for 6% of the time, Pallas kernels for 8%

profile of v1, /device:TPU:0, one launch (start us, length us, event | category | flops | bytes accessed | tf_op | source)
XLA Modules:
  0.0 189.8 jit_solution(13766406281044100024)
XLA Ops:
  2.8 2.9 %collective-permute-start.1 = (s32[2,32,8]{1,2,0:T(8,128)S(1)}, s32[2,32,8]{1,2,0:T(8,128)S(1)}, u32[]{:S(2)}, u32[]{:S(2)}) collective-permute-start(s32[2,32,8]{1,2,0:T(8,128)S(1)} %get-tuple-element.48), channel_id=1, source_target_pairs={{0,2},{1,3},{2,0},{3,1},{4,6},{5,7},{6,4},{7,5},{8,10},{9,11},{10,... | collective-permute-start | bytes 6152 | tf_op jit(solution)/shard_map/ppermute | solution.py:434
  7.3 2.1 %collective-permute-start.2 = (s32[2,2,32,8]{2,3,1,0:T(8,128)S(1)}, s32[2,2,32,8]{2,3,1,0:T(8,128)S(1)}, u32[]{:S(2)}, u32[]{:S(2)}) collective-permute-start(s32[2,2,32,8]{2,3,1,0:T(8,128)S(1)} %get-tuple-element.46), channel_id=1, source_target_pairs={{0,4},{1,5},{2,6},{3,7},{4,0},{5,1},{6,2},{7,3},{8,12},{9,13},{10,... | collective-permute-start | bytes 12296 | tf_op jit(solution)/shard_map/ppermute | solution.py:434
  11.1 3.1 %collective-permute-start.3 = (s32[2,2,2,32,8]{3,4,2,1,0:T(8,128)S(1)}, s32[2,2,2,32,8]{3,4,2,1,0:T(8,128)S(1)}, u32[]{:S(2)}, u32[]{:S(2)}) collective-permute-start(s32[2,2,2,32,8]{3,4,2,1,0:T(8,128)S(1)} %get-tuple-element.44), channel_id=1, source_target_pairs={{0,8},{1,9},{2,10},{3,11},{4,12},{5,13},{6,14},{7,15},{8,0},{9,1},... | collective-permute-start | bytes 24584 | tf_op jit(solution)/shard_map/ppermute | solution.py:434
  15.1 14.7 %coil_images.1 = (bf16[8,3,384,768]{3,2,1,0:T(8,128)(2,1)}, f32[2,8,384]{2,1,0:T(8,128)}) custom-call(f32[2,2,24,64,384]{4,3,2,1,0:T(8,128)} %refs_5_.1, f32[2,24,64,384]{3,2,1,0:T(8,128)} %refs_6_.1, f32[2,24,64,384]{3,2,1,0:T(8,128)} %refs_7_.1), custom_call_target="tpu_custom_call" | custom-call | tf_op jit(solution)/shard_map/coil_images/pallas_call | solution.py:97
  30.6 14.7 %partial_rows.1 = (f32[8,64,768]{2,1,0:T(8,128)}, f32[8,64,768]{2,1,0:T(8,128)}) custom-call(s32[1]{0:T(128)} %bitcast.refs_0_, s32[8,2,32,8]{3,2,1,0:T(8,128)} %bitcast.96, bf16[8,3,384,768]{3,2,1,0:T(8,128)(2,1)} %get-tuple-element.15.refs_2_, bf16[3,2,480,384]{3,2,1,0:T(8,128)(2,1)} %constant.145.clone.refs_3_.refs_8_, f32[480,128]{1,0:T(8,128)} %pad.4.refs_4_.refs_9_), custom_call_target="tpu_custom_call" | custom-call | tf_op jit(solution)/shard_map/partial_rows/pallas_call | solution.py:156
  45.3 3.6 %collective-permute-done.4.refs_1_ = f32[8,64,768]{2,1,0:T(8,128)S(1)} collective-permute-done((f32[8,64,768]{2,1,0:T(8,128)}, f32[8,64,768]{2,1,0:T(8,128)S(1)}, u32[]{:S(2)}, u32[]{:S(2)}) %collective-permute-start.4) | collective-permute-done | bytes 1572896 | tf_op jit(solution)/shard_map/ppermute | solution.py:434
  50.1 10.3 %row_cells.1 = (f32[8,16,1024]{2,1,0:T(8,128)}, f32[8,16,1024]{2,1,0:T(8,128)}) custom-call(f32[8,64,768]{2,1,0:T(8,128)} %get-tuple-element.16.refs_0_, f32[8,64,768]{2,1,0:T(8,128)} %copy-done.1, s32[8,2,32,8]{3,2,1,0:T(8,128)} %bitcast.97, f32[16,768]{1,0:T(8,128)} %constant.148.clone.refs_3_, bf16[3,768,1024]{2,1,0:T(8,128)(2,1)} %constant.146.clone.refs_4_), custom_call_target="tpu_custom_call" | custom-call | tf_op jit(solution)/shard_map/row_cells/pallas_call | solution.py:222
  65.7 4.1 %collective-permute-done.8 = f32[2,2,16,1024]{3,2,1,0:T(8,128)S(1)} collective-permute-done((f32[2,2,16,1024]{3,2,1,0:T(8,128)S(1)}, f32[2,2,16,1024]{3,2,1,0:T(8,128)S(1)}, u32[]{:S(2)}, u32[]{:S(2)}) %collective-permute-start.8) | collective-permute-done | bytes 262176 | tf_op jit(solution)/shard_map/ppermute | solution.py:434
  72.9 6.4 %collective-permute-done.9 = f32[2,16,1024]{2,1,0:T(8,128)S(1)} collective-permute-done((f32[2,16,1024]{2,1,0:T(8,128)S(1)}, f32[2,16,1024]{2,1,0:T(8,128)S(1)}, u32[]{:S(2)}, u32[]{:S(2)}) %collective-permute-start.9) | collective-permute-done | bytes 131104 | tf_op jit(solution)/shard_map/ppermute | solution.py:434
  81.0 2.6 %collective-permute-done.10 = f32[16,1024]{1,0:T(8,128)S(1)} collective-permute-done((f32[16,1024]{1,0:T(8,128)S(1)}, f32[16,1024]{1,0:T(8,128)S(1)}, u32[]{:S(2)}, u32[]{:S(2)}) %collective-permute-start.10) | collective-permute-done | bytes 65568 | tf_op jit(solution)/shard_map/ppermute | solution.py:434
  84.3 2.2 %collective-permute-done.7 = f32[16,1024]{1,0:T(8,128)S(1)} collective-permute-done((f32[16,1024]{1,0:T(8,128)S(1)}, f32[16,1024]{1,0:T(8,128)S(1)}, u32[]{:S(2)}, u32[]{:S(2)}) %collective-permute-start.7) | collective-permute-done | bytes 65568 | tf_op jit(solution)/shard_map/ppermute | solution.py:434
  87.1 5.7 %tiles.1 = (f32[16,1024]{1,0:T(8,128)}, f32[16,1024]{1,0:T(8,128)}, f32[4,512]{1,0:T(4,128)}) custom-call(s32[16]{0:T(128)} %refs_0_.1, f32[16,1024]{1,0:T(8,128)} %fusion.5.refs_1_, f32[16,1024]{1,0:T(8,128)} %fusion.4.refs_2_, bf16[16,128,512]{2,1,0:T(8,128)(2,1)} %refs_3_.4), custom_call_target="tpu_custom_call" | custom-call | tf_op jit(solution)/shard_map/tiles/pallas_call | solution.py:317
  94.0 4.2 %collective-permute-done.15 = f32[16,1024]{1,0:T(8,128)S(1)} collective-permute-done((f32[16,1024]{1,0:T(8,128)}, f32[16,1024]{1,0:T(8,128)S(1)}, u32[]{:S(2)}, u32[]{:S(2)}) %collective-permute-start.15) | collective-permute-done | bytes 65568 | tf_op jit(solution)/shard_map/ppermute | solution.py:434
  100.0 2.2 %collective-permute-start.19 = (f32[2,16,1024]{2,1,0:T(8,128)S(1)}, f32[2,16,1024]{2,1,0:T(8,128)S(1)}, u32[]{:S(2)}, u32[]{:S(2)}) collective-permute-start(f32[2,16,1024]{2,1,0:T(8,128)S(1)} %get-tuple-element.40), channel_id=1, source_target_pairs={{0,8},{1,9},{2,10},{3,11},{4,12},{5,13},{6,14},{7,15},{8,0},{9,1},... | collective-permute-start | bytes 393224 | tf_op jit(solution)/shard_map/ppermute | solution.py:434
  106.1 3.3 %collective-permute-start.20 = (f32[2,2,16,1024]{3,2,1,0:T(8,128)S(1)}, f32[2,2,16,1024]{3,2,1,0:T(8,128)S(1)}, u32[]{:S(2)}, u32[]{:S(2)}) collective-permute-start(f32[2,2,16,1024]{3,2,1,0:T(8,128)S(1)} %get-tuple-element.36), channel_id=1, source_target_pairs={{0,4},{1,5},{2,6},{3,7},{4,0},{5,1},{6,2},{7,3},{8,12},{9,13},{10,... | collective-permute-start | bytes 786440 | tf_op jit(solution)/shard_map/ppermute | solution.py:434
  111.5 2.3 %collective-permute-done.20 = f32[2,2,16,1024]{3,2,1,0:T(8,128)S(1)} collective-permute-done((f32[2,2,16,1024]{3,2,1,0:T(8,128)S(1)}, f32[2,2,16,1024]{3,2,1,0:T(8,128)S(1)}, u32[]{:S(2)}, u32[]{:S(2)}) %collective-permute-start.20) | collective-permute-done | bytes 262176 | tf_op jit(solution)/shard_map/ppermute | solution.py:434
  114.7 6.6 %adjoint_rows.1.refs_3_ = f32[8,64,768]{2,1,0:T(8,128)} custom-call(f32[8,16,1024]{2,1,0:T(8,128)} %bitcast.100, f32[8,16,1024]{2,1,0:T(8,128)} %bitcast.101, s32[8,2,32,8]{3,2,1,0:T(8,128)} %bitcast.98, f32[16,768]{1,0:T(8,128)} %constant.148.clone.refs_3_, bf16[2,1024,768]{2,1,0:T(8,128)(2,1)} %constant.147.clone.refs_4_), custom_call_target="tpu_custom_call" | custom-call | tf_op jit(solution)/shard_map/adjoint_rows/pallas_call | solution.py:267
  127.3 2.9 %collective-permute-done.12 = f32[2]{0:T(128)S(1)} collective-permute-done((f32[2]{0:T(128)S(1)}, f32[2]{0:T(128)S(1)}, u32[]{:S(2)}, u32[]{:S(2)}) %collective-permute-start.12) | collective-permute-done | bytes 40 | tf_op jit(solution)/shard_map/ppermute | solution.py:434
  134.4 2.2 %collective-permute-start.14 = (f32[2]{0:T(128)S(1)}, f32[2]{0:T(128)S(1)}, u32[]{:S(2)}, u32[]{:S(2)}) collective-permute-start(f32[2]{0:T(128)S(1)} %add.157), channel_id=1, source_target_pairs={{0,8},{1,9},{2,10},{3,11},{4,12},{5,13},{6,14},{7,15},{8,0},{9,1},... | collective-permute-start | bytes 32 | tf_op jit(solution)/shard_map/ppermute | solution.py:434
  136.6 2.3 %collective-permute-done.14 = f32[2]{0:T(128)S(1)} collective-permute-done((f32[2]{0:T(128)S(1)}, f32[2]{0:T(128)S(1)}, u32[]{:S(2)}, u32[]{:S(2)}) %collective-permute-start.14) | collective-permute-done | bytes 40 | tf_op jit(solution)/shard_map/ppermute | solution.py:434
  141.9 17.9 %finish.1 = (f32[2,24,64,384]{3,2,1,0:T(8,128)}, f32[8,384]{1,0:T(8,128)}) custom-call(s32[1]{0:T(128)} %bitcast.refs_0_, f32[1]{0:T(128)} %div.81.refs_1_, s32[8,2,32,8]{3,2,1,0:T(8,128)} %bitcast.99, f32[8,64,768]{2,1,0:T(8,128)} %adjoint_rows.1.refs_3_, f32[8,64,768]{2,1,0:T(8,128)} %copy-done, f32[2,2,24,64,384]{4,3,2,1,0:T(8,128)} %refs_5_.1, ...), custom_call_target="tpu_custom_call" | custom-call | tf_op jit(solution)/shard_map/finish/pallas_call | solution.py:400
  168.2 3.4 %collective-permute-start.24 = (f32[1]{0:T(128)}, f32[1]{0:T(128)}, u32[]{:S(2)}, u32[]{:S(2)}) collective-permute-start(f32[1]{0:T(128)} %add.161), channel_id=1, source_target_pairs={{0,4},{1,5},{2,6},{3,7},{4,0},{5,1},{6,2},{7,3},{8,12},{9,13},{10,... | collective-permute-start | bytes 20 | tf_op jit(solution)/shard_map/ppermute | solution.py:434
  172.5 3.5 %collective-permute-start.25 = (f32[1]{0:T(128)}, f32[1]{0:T(128)}, u32[]{:S(2)}, u32[]{:S(2)}) collective-permute-start(f32[1]{0:T(128)} %add.162), channel_id=1, source_target_pairs={{0,8},{1,9},{2,10},{3,11},{4,12},{5,13},{6,14},{7,15},{8,0},{9,1},... | collective-permute-start | bytes 20 | tf_op jit(solution)/shard_map/ppermute | solution.py:434
  178.5 11.4 %multiply_add_fusion = (f32[2,24,64,384]{3,2,1,0:T(8,128)}, f32[2,24,64,384]{3,2,1,0:T(8,128)}) fusion(f32[2,24,64,384]{3,2,1,0:T(8,128)} %get-tuple-element.12, f32[2,24,64,384]{3,2,1,0:T(8,128)} %refs_6_.1, f32[]{:T(128)} %bitcast.50, f32[2,24,64,384]{3,2,1,0:T(8,128)} %param.11, f32[]{:T(128)} %bitcast.34), kind=kLoop, calls=%fused_computation | loop fusion | flops 4718592 | bytes 23592968 | tf_op jit(solution)/shard_map/add | solution.py:535
  (91 shorter events, 48.2 us)
Async XLA Ops:
  2.8 4.5 %collective-permute-start.1 = (s32[2,32,8]{1,2,0:T(8,128)S(1)}, s32[2,32,8]{1,2,0:T(8,128)S(1)}, u32[]{:S(2)}, u32[]{:S(2)}) collective-permute-start(s32[2,32,8]{1,2,0:T(8,128)S(1)} %get-tuple-element.48), channel_id=1, source_target_pairs={{0,2},{1,3},{2,0},{3,1},{4,6},{5,7},{6,4},{7,5},{8,10},{9,11},{10,... | collective-permute-start | bytes 6152 | tf_op jit(solution)/shard_map/ppermute | solution.py:434
  7.3 3.8 %collective-permute-start.2 = (s32[2,2,32,8]{2,3,1,0:T(8,128)S(1)}, s32[2,2,32,8]{2,3,1,0:T(8,128)S(1)}, u32[]{:S(2)}, u32[]{:S(2)}) collective-permute-start(s32[2,2,32,8]{2,3,1,0:T(8,128)S(1)} %get-tuple-element.46), channel_id=1, source_target_pairs={{0,4},{1,5},{2,6},{3,7},{4,0},{5,1},{6,2},{7,3},{8,12},{9,13},{10,... | collective-permute-start | bytes 12296 | tf_op jit(solution)/shard_map/ppermute | solution.py:434
  11.1 18.6 %collective-permute-start.3 = (s32[2,2,2,32,8]{3,4,2,1,0:T(8,128)S(1)}, s32[2,2,2,32,8]{3,4,2,1,0:T(8,128)S(1)}, u32[]{:S(2)}, u32[]{:S(2)}) collective-permute-start(s32[2,2,2,32,8]{3,4,2,1,0:T(8,128)S(1)} %get-tuple-element.44), channel_id=1, source_target_pairs={{0,8},{1,9},{2,10},{3,11},{4,12},{5,13},{6,14},{7,15},{8,0},{9,1},... | collective-permute-start | bytes 24584 | tf_op jit(solution)/shard_map/ppermute | solution.py:434
  45.3 3.6 %collective-permute-start.4 = (f32[8,64,768]{2,1,0:T(8,128)}, f32[8,64,768]{2,1,0:T(8,128)S(1)}, u32[]{:S(2)}, u32[]{:S(2)}) collective-permute-start(f32[8,64,768]{2,1,0:T(8,128)} %get-tuple-element.17), channel_id=1, source_target_pairs={{0,1},{1,0},{2,3},{3,2},{4,5},{5,4},{6,7},{7,6},{8,9},{9,8},{10,11... | collective-permute-start | bytes 4718600 | tf_op jit(solution)/shard_map/ppermute | solution.py:434
  61.3 8.4 %collective-permute-start.8 = (f32[2,2,16,1024]{3,2,1,0:T(8,128)S(1)}, f32[2,2,16,1024]{3,2,1,0:T(8,128)S(1)}, u32[]{:S(2)}, u32[]{:S(2)}) collective-permute-start(f32[2,2,16,1024]{3,2,1,0:T(8,128)S(1)} %slice_bitcast_fusion), channel_id=1, source_target_pairs={{0,4},{1,5},{2,6},{3,7},{4,0},{5,1},{6,2},{7,3},{8,12},{9,13},{10,... | collective-permute-start | bytes 786440 | tf_op jit(solution)/shard_map/ppermute | solution.py:434
  64.1 8.1 %collective-permute-start.5 = (f32[2,2,16,1024]{3,2,0,1:T(8,128)S(1)}, f32[2,2,16,1024]{3,2,0,1:T(8,128)S(1)}, u32[]{:S(2)}, u32[]{:S(2)}) collective-permute-start(f32[2,2,16,1024]{3,2,0,1:T(8,128)S(1)} %bitcast.105), channel_id=1, source_target_pairs={{0,2},{1,3},{2,0},{3,1},{4,6},{5,7},{6,4},{7,5},{8,10},{9,11},{10,... | collective-permute-start | bytes 786440 | tf_op jit(solution)/shard_map/ppermute | solution.py:434
  70.8 8.5 %collective-permute-start.9 = (f32[2,16,1024]{2,1,0:T(8,128)S(1)}, f32[2,16,1024]{2,1,0:T(8,128)S(1)}, u32[]{:S(2)}, u32[]{:S(2)}) collective-permute-start(f32[2,16,1024]{2,1,0:T(8,128)S(1)} %slice_bitcast_fusion.2), channel_id=1, source_target_pairs={{0,8},{1,9},{2,10},{3,11},{4,12},{5,13},{6,14},{7,15},{8,0},{9,1},... | collective-permute-start | bytes 393224 | tf_op jit(solution)/shard_map/ppermute | solution.py:434
  72.3 8.6 %collective-permute-start.6 = (f32[2,16,1024]{2,1,0:T(8,128)S(1)}, f32[2,16,1024]{2,1,0:T(8,128)S(1)}, u32[]{:S(2)}, u32[]{:S(2)}) collective-permute-start(f32[2,16,1024]{2,1,0:T(8,128)S(1)} %slice_bitcast_fusion.4), channel_id=1, source_target_pairs={{0,4},{1,5},{2,6},{3,7},{4,0},{5,1},{6,2},{7,3},{8,12},{9,13},{10,... | collective-permute-start | bytes 393224 | tf_op jit(solution)/shard_map/ppermute | solution.py:434
  79.3 4.3 %collective-permute-start.10 = (f32[16,1024]{1,0:T(8,128)S(1)}, f32[16,1024]{1,0:T(8,128)S(1)}, u32[]{:S(2)}, u32[]{:S(2)}) collective-permute-start(f32[16,1024]{1,0:T(8,128)S(1)} %slice_bitcast_fusion.6), channel_id=1, source_target_pairs={{0,2},{1,3},{2,0},{3,1},{4,6},{5,7},{6,4},{7,5},{8,10},{9,11},{10,... | collective-permute-start | bytes 196616 | tf_op jit(solution)/shard_map/ppermute | solution.py:434
  80.9 5.6 %collective-permute-start.7 = (f32[16,1024]{1,0:T(8,128)S(1)}, f32[16,1024]{1,0:T(8,128)S(1)}, u32[]{:S(2)}, u32[]{:S(2)}) collective-permute-start(f32[16,1024]{1,0:T(8,128)S(1)} %slice_bitcast_fusion.8), channel_id=1, source_target_pairs={{0,8},{1,9},{2,10},{3,11},{4,12},{5,13},{6,14},{7,15},{8,0},{9,1},... | collective-permute-start | bytes 196616 | tf_op jit(solution)/shard_map/ppermute | solution.py:434
  92.8 5.4 %collective-permute-start.15 = (f32[16,1024]{1,0:T(8,128)}, f32[16,1024]{1,0:T(8,128)S(1)}, u32[]{:S(2)}, u32[]{:S(2)}) collective-permute-start(f32[16,1024]{1,0:T(8,128)} %get-tuple-element.21), channel_id=1, source_target_pairs={{0,8},{1,9},{2,10},{3,11},{4,12},{5,13},{6,14},{7,15},{8,0},{9,1},... | collective-permute-start | bytes 196616 | tf_op jit(solution)/shard_map/ppermute | solution.py:434
  92.8 6.4 %collective-permute-start.18 = (f32[16,1024]{1,0:T(8,128)}, f32[16,1024]{1,0:T(8,128)S(1)}, u32[]{:S(2)}, u32[]{:S(2)}) collective-permute-start(f32[16,1024]{1,0:T(8,128)} %get-tuple-element.22), channel_id=1, source_target_pairs={{0,2},{1,3},{2,0},{3,1},{4,6},{5,7},{6,4},{7,5},{8,10},{9,11},{10,... | collective-permute-start | bytes 196616 | tf_op jit(solution)/shard_map/ppermute | solution.py:434
  99.1 5.0 %collective-permute-start.16 = (f32[2,16,1024]{2,1,0:T(8,128)S(1)}, f32[2,16,1024]{2,1,0:T(8,128)S(1)}, u32[]{:S(2)}, u32[]{:S(2)}) collective-permute-start(f32[2,16,1024]{2,1,0:T(8,128)S(1)} %get-tuple-element.42), channel_id=1, source_target_pairs={{0,4},{1,5},{2,6},{3,7},{4,0},{5,1},{6,2},{7,3},{8,12},{9,13},{10,... | collective-permute-start | bytes 393224 | tf_op jit(solution)/shard_map/ppermute | solution.py:434
  100.0 6.0 %collective-permute-start.19 = (f32[2,16,1024]{2,1,0:T(8,128)S(1)}, f32[2,16,1024]{2,1,0:T(8,128)S(1)}, u32[]{:S(2)}, u32[]{:S(2)}) collective-permute-start(f32[2,16,1024]{2,1,0:T(8,128)S(1)} %get-tuple-element.40), channel_id=1, source_target_pairs={{0,8},{1,9},{2,10},{3,11},{4,12},{5,13},{6,14},{7,15},{8,0},{9,1},... | collective-permute-start | bytes 393224 | tf_op jit(solution)/shard_map/ppermute | solution.py:434
  104.2 6.4 %collective-permute-start.17 = (f32[2,2,16,1024]{3,2,0,1:T(8,128)S(1)}, f32[2,2,16,1024]{3,2,0,1:T(8,128)S(1)}, u32[]{:S(2)}, u32[]{:S(2)}) collective-permute-start(f32[2,2,16,1024]{3,2,0,1:T(8,128)S(1)} %get-tuple-element.38), channel_id=1, source_target_pairs={{0,2},{1,3},{2,0},{3,1},{4,6},{5,7},{6,4},{7,5},{8,10},{9,11},{10,... | collective-permute-start | bytes 786440 | tf_op jit(solution)/shard_map/ppermute | solution.py:434
  106.1 7.7 %collective-permute-start.20 = (f32[2,2,16,1024]{3,2,1,0:T(8,128)S(1)}, f32[2,2,16,1024]{3,2,1,0:T(8,128)S(1)}, u32[]{:S(2)}, u32[]{:S(2)}) collective-permute-start(f32[2,2,16,1024]{3,2,1,0:T(8,128)S(1)} %get-tuple-element.36), channel_id=1, source_target_pairs={{0,4},{1,5},{2,6},{3,7},{4,0},{5,1},{6,2},{7,3},{8,12},{9,13},{10,... | collective-permute-start | bytes 786440 | tf_op jit(solution)/shard_map/ppermute | solution.py:434
  121.2 19.6 %collective-permute-start.21 = (f32[8,64,768]{2,1,0:T(8,128)}, f32[8,64,768]{2,1,0:T(8,128)S(1)}, u32[]{:S(2)}, u32[]{:S(2)}) collective-permute-start(f32[8,64,768]{2,1,0:T(8,128)} %adjoint_rows.1.refs_3_), channel_id=1, source_target_pairs={{0,1},{1,0},{2,3},{3,2},{4,5},{5,4},{6,7},{7,6},{8,9},{9,8},{10,11... | collective-permute-start | bytes 4718600 | tf_op jit(solution)/shard_map/ppermute | solution.py:434
  126.6 3.5 %collective-permute-start.12 = (f32[2]{0:T(128)S(1)}, f32[2]{0:T(128)S(1)}, u32[]{:S(2)}, u32[]{:S(2)}) collective-permute-start(f32[2]{0:T(128)S(1)} %fusion.32), channel_id=1, source_target_pairs={{0,2},{1,3},{2,0},{3,1},{4,6},{5,7},{6,4},{7,5},{8,10},{9,11},{10,... | collective-permute-start | bytes 32 | tf_op jit(solution)/shard_map/ppermute | solution.py:434
  130.9 3.5 %collective-permute-start.13 = (f32[2]{0:T(128)S(1)}, f32[2]{0:T(128)S(1)}, u32[]{:S(2)}, u32[]{:S(2)}) collective-permute-start(f32[2]{0:T(128)S(1)} %fusion.34), channel_id=1, source_target_pairs={{0,4},{1,5},{2,6},{3,7},{4,0},{5,1},{6,2},{7,3},{8,12},{9,13},{10,... | collective-permute-start | bytes 32 | tf_op jit(solution)/shard_map/ppermute | solution.py:434
  134.4 4.4 %collective-permute-start.14 = (f32[2]{0:T(128)S(1)}, f32[2]{0:T(128)S(1)}, u32[]{:S(2)}, u32[]{:S(2)}) collective-permute-start(f32[2]{0:T(128)S(1)} %add.157), channel_id=1, source_target_pairs={{0,8},{1,9},{2,10},{3,11},{4,12},{5,13},{6,14},{7,15},{8,0},{9,1},... | collective-permute-start | bytes 32 | tf_op jit(solution)/shard_map/ppermute | solution.py:434
  161.2 1.4 collective-permute-start.22
  163.8 3.7 %collective-permute-start.23 = (f32[1]{0:T(128)}, f32[1]{0:T(128)}, u32[]{:S(2)}, u32[]{:S(2)}) collective-permute-start(f32[1]{0:T(128)} %add.160), channel_id=1, source_target_pairs={{0,2},{1,3},{2,0},{3,1},{4,6},{5,7},{6,4},{7,5},{8,10},{9,11},{10,... | collective-permute-start | bytes 20 | tf_op jit(solution)/shard_map/ppermute | solution.py:434
  168.2 3.7 %collective-permute-start.24 = (f32[1]{0:T(128)}, f32[1]{0:T(128)}, u32[]{:S(2)}, u32[]{:S(2)}) collective-permute-start(f32[1]{0:T(128)} %add.161), channel_id=1, source_target_pairs={{0,4},{1,5},{2,6},{3,7},{4,0},{5,1},{6,2},{7,3},{8,12},{9,13},{10,... | collective-permute-start | bytes 20 | tf_op jit(solution)/shard_map/ppermute | solution.py:434
  172.5 4.6 %collective-permute-start.25 = (f32[1]{0:T(128)}, f32[1]{0:T(128)}, u32[]{:S(2)}, u32[]{:S(2)}) collective-permute-start(f32[1]{0:T(128)} %add.162), channel_id=1, source_target_pairs={{0,8},{1,9},{2,10},{3,11},{4,12},{5,13},{6,14},{7,15},{8,0},{9,1},... | collective-permute-start | bytes 20 | tf_op jit(solution)/shard_map/ppermute | solution.py:434
  (6 other events, 27.4 us)

commit v2 on v1

v2 whole, which is shorter than its diff:
```python
import math

import jax
import jax.numpy as jnp
import ml_dtypes
import numpy as np
from jax import lax
from jax.experimental import pallas as pl
from jax.experimental.pallas import tpu as pltpu
from jax.sharding import PartitionSpec as P

GX = 480
GY = 480
DAMPING = 0.1
HIGHEST = lax.Precision.HIGHEST
F32 = jnp.float32
BF16 = jnp.bfloat16
MIB = 1024 * 1024
FIELDS = 8


def dft(out_index, in_index, size, scaled=True):
    angle = (out_index[:, None] * in_index[None, :] % size) * (2.0 * math.pi / size)
    scale = 1.0 / math.sqrt(size) if scaled else 1.0
    return np.cos(angle) * scale, np.sin(angle) * scale


def table_parts(table, count):
    parts = []
    for _ in range(count):
        part = table.astype(ml_dtypes.bfloat16)
        parts.append(part)
        table = table - part.astype(np.float64)
    return np.stack(parts)


def split(value, count):
    parts = []
    for step in range(count):
        part = value.astype(BF16)
        parts.append(part)
        if step + 1 < count:
            value = value - part.astype(F32)
    return parts


def dot(a, b):
    return lax.dot_general(a, b, (((1,), (0,)), ((), ())), preferred_element_type=F32)


def six_products(lhs, rhs):
    rows = lhs[0].shape[0]
    first = dot(jnp.concatenate(lhs, axis=0), rhs[0])
    second = dot(jnp.concatenate(lhs[:2], axis=0), rhs[1])
    third = dot(lhs[0], rhs[2])
    small = first[2 * rows :] + second[rows:] + third
    return first[:rows] + (first[rows : 2 * rows] + second[:rows] + small)


def params(mib):
    return pltpu.CompilerParams(vmem_limit_bytes=mib * MIB)


def squares_kernel(value_ref, out_ref):
    @pl.when(pl.program_id(0) == 0)
    def _():
        out_ref[...] = jnp.zeros(out_ref.shape, F32)

    value = value_ref[...]
    out_ref[...] += jnp.sum(value * value, axis=0)


def squares(value):
    value = value.reshape((-1,) + value.shape[2:])
    rows, planes, width = value.shape
    step = math.gcd(rows, 8)
    return pl.pallas_call(
        squares_kernel,
        grid=(rows // step,),
        in_specs=[pl.BlockSpec((step, planes, width), lambda i: (i, 0, 0))],
        out_specs=pl.BlockSpec((planes, width), lambda i: (0, 0)),
        out_shape=jax.ShapeDtypeStruct((planes, width), F32),
        compiler_params=params(48),
        name="squares",
    )(value)


def x_kernel(sums_ref, x_ref, dir_ref, *refs):
    step = sums_ref[0:1, 0:1] / sums_ref[1:2, 0:1]
    refs[-1][...] = x_ref[...] + step * dir_ref[...]


def x_update(sums, x_image, direction, piece, pieces, before):
    dims = x_image.shape
    flat = (-1,) + dims[2:]
    rows = dims[0] * dims[1] // pieces
    step = math.gcd(rows, 4)
    given = [] if before is None else [before.reshape(flat)]
    block = pl.BlockSpec((step,) + dims[2:], lambda i: (piece * (rows // step) + i, 0, 0))
    out = pl.pallas_call(
        x_kernel,
        grid=(rows // step,),
        in_specs=[pl.BlockSpec(sums.shape, lambda i: (0, 0)), block, block]
        + [pl.BlockSpec(memory_space=pl.ANY)] * len(given),
        out_specs=block,
        out_shape=jax.ShapeDtypeStruct((dims[0] * dims[1],) + dims[2:], F32),
        input_output_aliases={3: 0} if given else {},
        compiler_params=params(48),
        name="x_update",
    )(sums, x_image.reshape(flat), direction.reshape(flat), *given)
    return out.reshape(dims)


def direction_kernel(sums_ref, one_ref, two_ref, res_ref, dir_ref, out_ref):
    ratio = (one_ref[0:1, 0:1] + two_ref[0:1, 0:1]) / sums_ref[0:1, 0:1]
    out_ref[...] = res_ref[...] + ratio * dir_ref[...]


def direction_update(sums, one, two, residual, direction):
    dims = residual.shape
    flat = (-1,) + dims[2:]
    rows = dims[0] * dims[1]
    step = math.gcd(rows, 4)
    block = pl.BlockSpec((step,) + dims[2:], lambda i: (i, 0, 0))
    small = pl.BlockSpec(sums.shape, lambda i: (0, 0))
    out = pl.pallas_call(
        direction_kernel,
        grid=(rows // step,),
        in_specs=[small, small, small, block, block],
        out_specs=block,
        out_shape=jax.ShapeDtypeStruct((rows,) + dims[2:], F32),
        compiler_params=params(32),
        name="direction_update",
    )(sums, one, two, residual.reshape(flat), direction.reshape(flat))
    return out.reshape(dims)


def row_matrix(info, table_ref, planes, parts):
    pairs, count, _ = info.shape
    half = count // 2
    info = info.reshape(pairs * count, FIELDS)
    depth = table_ref.shape[3]
    hot = lax.broadcasted_iota(jnp.int32, (pairs * count, GX), 1) == info[:, 0:1]
    hot = jnp.where(hot, 1.0, 0.0).astype(BF16)
    live = lax.broadcasted_iota(jnp.int32, (pairs * count, depth), 1) % planes == info[:, 1:2]
    matrix = []
    for part in range(parts):
        sides = [
            jnp.where(live, dot(hot, table_ref[part, side]), 0.0)
            .astype(BF16)
            .reshape(pairs, 2, 1, half, depth)
            for side in range(2)
        ]
        matrix.append(jnp.concatenate(sides, axis=2).reshape(pairs, 2 * count, depth))
    return matrix


def coil_parts(sens_ref, dir_ref, out_ref):
    coils, rows, planes, width = sens_ref.shape[1:]
    half = rows * planes
    chunk = max(16 // planes, 1)
    for index in range(0, rows, chunk):
        at = slice(index, index + chunk)
        to = index * planes
        d_re, d_im = dir_ref[0, at], dir_ref[1, at]
        for coil in range(coils):
            s_re, s_im = sens_ref[0, coil, at], sens_ref[1, coil, at]
            pair = (s_re * d_re - s_im * d_im, s_re * d_im + s_im * d_re)
            for ri, value in enumerate(pair):
                value = value.reshape(chunk * planes, width)
                where = slice(ri * half + to, ri * half + to + chunk * planes)
                for number, part in enumerate(split(value, 3)):
                    out_ref[number, where, coil * width : (coil + 1) * width] = part


def rows_kernel(
    planes, per_step, per_group, me_ref, info_ref, sens_ref, dir_ref, table_ref, keep_ref, send_ref,
    matrix_ref, all_ref, image_ref,
):
    pair = pl.program_id(0)
    count = info_ref.shape[2]

    @pl.when(pair % per_step == 0)
    def _():
        info = info_ref[...].reshape(per_step, 2 * count, FIELDS)
        for part, value in enumerate(row_matrix(info, table_ref, planes, 3)):
            all_ref[:, part] = value

    if per_group == 1:
        coil_parts(sens_ref, dir_ref, image_ref)
    else:

        @pl.when(pair % per_group == 0)
        def _():
            coil_parts(sens_ref, dir_ref, image_ref)

    matrix = [all_ref[pair % per_step, part] for part in range(3)]
    out = six_products(matrix, [image_ref[part] for part in range(3)])
    for slab, ref in enumerate((keep_ref, send_ref)):
        ref[0] = out[2 * slab * count : 2 * (slab + 1) * count]
    for part in range(2):
        matrix_ref[0, part] = matrix[part]


def partial_rows(me, info, sens, direction, table, planes, slabs_group):
    pairs, _, count, _ = info.shape
    _, coils, rows, _, width = sens.shape
    depth = 2 * rows * planes
    per_step = min(pairs, 8)
    whole = jax.ShapeDtypeStruct((pairs, 2 * count, coils * width), F32)
    block = pl.BlockSpec((1, 2 * count, coils * width), lambda q, me: (q, 0, 0))

    def place(q, me):
        return lax.bitwise_xor(2 * q, me[0]) // slabs_group

    return pl.pallas_call(
        lambda *refs: rows_kernel(planes, per_step, slabs_group // 2, *refs),
        grid_spec=pltpu.PrefetchScalarGridSpec(
            num_scalar_prefetch=1,
            grid=(pairs,),
            in_specs=[
                pl.BlockSpec((per_step, 2, count, FIELDS), lambda q, me: (q // per_step, 0, 0, 0)),
                pl.BlockSpec(
                    (2, coils, rows, planes, width), lambda q, me: (0, 0, 0, place(q, me), 0)
                ),
                pl.BlockSpec((2, rows, planes, width), lambda q, me: (0, 0, place(q, me), 0)),
                pl.BlockSpec(table.shape, lambda q, me: (0, 0, 0, 0)),
            ],
            out_specs=[
                block,
                block,
                pl.BlockSpec((1, 2, 4 * count, depth), lambda q, me: (q, 0, 0, 0)),
            ],
            scratch_shapes=[
                pltpu.VMEM((per_step, 3, 4 * count, depth), BF16),
                pltpu.VMEM((3, depth, coils * width), BF16),
            ],
        ),
        out_shape=[whole, whole, jax.ShapeDtypeStruct((pairs, 2, 4 * count, depth), BF16)],
        compiler_params=params(48),
        name="partial_rows",
    )(me, info, sens, direction, table)


def start_turn(info_ref, start_ref):
    chunk, _, count, _ = info_ref.shape
    info = info_ref[...].reshape(chunk * count, FIELDS)
    starts = start_ref.shape[0]
    hot = lax.broadcasted_iota(jnp.int32, (chunk * count, starts), 1) == info[:, 2:3]
    turn = jnp.dot(
        jnp.where(hot, 1.0, 0.0), start_ref[...], precision=HIGHEST, preferred_element_type=F32
    )
    width = turn.shape[1] // 2
    return info, turn[:, :width], turn[:, width:]


def segment_mask(info, cells, segment):
    at = lax.broadcasted_iota(jnp.int32, (info.shape[0], cells), 1)
    return (at >= info[:, 3:4]) & (at < info[:, 3:4] + segment)


def side_of(value, bit):
    step = 2**bit
    return value // step % 2, value // (2 * step) * step + value % step


def cells_kernel(tiles, segment, keep_ref, got_ref, info_ref, start_ref, table_ref, *out_refs):
    pairs, count, _ = keep_ref.shape
    count = count // 2
    cells = out_refs[0].shape[2] // 2
    coils = len(out_refs) // 2
    info, cos, sin = start_turn(info_ref, start_ref)
    width = cos.shape[1]
    values = []
    for coil in range(coils):
        lanes = slice(coil * width, (coil + 1) * width)
        both = keep_ref[:, :, lanes] + got_ref[:, :, lanes]
        re = both[:, :count].reshape(pairs * count, width)
        im = both[:, count:].reshape(pairs * count, width)
        re, im = cos * re + sin * im, cos * im - sin * re
        values.append(jnp.concatenate([re, im], axis=1))
        values.append(jnp.concatenate([im, -re], axis=1))
    value = split(jnp.concatenate(values, axis=0), 3)
    out = six_products(value, [table_ref[part] for part in range(3)])
    rows = pairs * count
    mask = segment_mask(info, cells, segment)
    for coil in range(coils):
        for ri in range(2):
            mine = out[(2 * coil + ri) * rows : (2 * coil + ri + 1) * rows]
            mine = jnp.where(mask, mine, 0.0).reshape(pairs, count // tiles, tiles, cells)
            mine = jnp.sum(mine, axis=1)
            for pair in range(pairs):
                side, place = side_of(pair, coil % 2)
                out_refs[2 * coil + side][place, :, ri * cells : (ri + 1) * cells] = mine[pair]


def row_cells(keep, got, info, start, table, tiles, segment, coils, chunk):
    pairs, double, width = keep.shape
    lines = 2 * table.shape[2]
    rows = pl.BlockSpec((chunk, double, width), lambda i: (i, 0, 0))
    half = jax.ShapeDtypeStruct((pairs // 2, tiles, lines), F32)
    return pl.pallas_call(
        lambda *refs: cells_kernel(tiles, segment, *refs),
        grid=(pairs // chunk,),
        in_specs=[
            rows,
            rows,
            pl.BlockSpec((chunk, 1, double // 2, FIELDS), lambda i: (i, 0, 0, 0)),
            pl.BlockSpec(start.shape, lambda i: (0, 0)),
            pl.BlockSpec(table.shape, lambda i: (0, 0, 0), pipeline_mode=pl.Buffered(1)),
        ],
        out_specs=[pl.BlockSpec((chunk // 2, tiles, lines), lambda i: (i, 0, 0))] * (2 * coils),
        out_shape=[half] * (2 * coils),
        compiler_params=params(40),
        name="row_cells",
    )(keep, got, info, start, table)


def adjoint_kernel(segment, coils, chunk, *refs):
    cell_refs, (info_ref, start_ref, table_ref, out_ref) = refs[: 2 * coils], refs[2 * coils :]
    count = info_ref.shape[2]
    _, tiles, cells = cell_refs[0].shape
    cells = cells // 2
    info, cos, sin = start_turn(info_ref, start_ref)
    width = cos.shape[1]
    mask = segment_mask(info, cells, segment)
    values = []
    for coil in range(coils):
        both = []
        for ri in range(2):
            wide = []
            for pair in range(chunk):
                side, place = side_of(pair, coil % 2)
                value = cell_refs[2 * coil + side][place, :, ri * cells : (ri + 1) * cells]
                wide += [value] * (count // tiles)
            both.append(jnp.where(mask, jnp.concatenate(wide, axis=0), 0.0))
        re, im = both
        values.append(jnp.concatenate([re, -im], axis=1))
        values.append(jnp.concatenate([im, re], axis=1))
    rows = chunk * count
    high, low = split(jnp.concatenate(values, axis=0), 2)
    first = dot(jnp.concatenate([high, low], axis=0), table_ref[0])
    total = high.shape[0]
    out = first[:total] + (first[total:] + dot(high, table_ref[1]))
    for coil in range(coils):
        re = out[2 * coil * rows : (2 * coil + 1) * rows]
        im = out[(2 * coil + 1) * rows : (2 * coil + 2) * rows]
        lanes = slice(coil * width, (coil + 1) * width)
        out_ref[:, :count, lanes] = (cos * re - sin * im).reshape(chunk, count, width)
        out_ref[:, count:, lanes] = (cos * im + sin * re).reshape(chunk, count, width)


def adjoint_rows(spread, info, start, table, segment, chunk):
    coils = len(spread) // 2
    half, tiles, lines = spread[0].shape
    pairs, _, count, _ = info.shape
    width = coils * table.shape[2]
    return pl.pallas_call(
        lambda *refs: adjoint_kernel(segment, coils, chunk, *refs),
        grid=(pairs // chunk,),
        in_specs=[pl.BlockSpec((chunk // 2, tiles, lines), lambda i: (i, 0, 0))] * (2 * coils)
        + [
            pl.BlockSpec((chunk, 1, count, FIELDS), lambda i: (i, 0, 0, 0)),
            pl.BlockSpec(start.shape, lambda i: (0, 0)),
            pl.BlockSpec(table.shape, lambda i: (0, 0, 0), pipeline_mode=pl.Buffered(1)),
        ],
        out_specs=pl.BlockSpec((chunk, 2 * count, width), lambda i: (i, 0, 0)),
        out_shape=jax.ShapeDtypeStruct((pairs, 2 * count, width), F32),
        compiler_params=params(32),
        name="adjoint_rows",
    )(*spread, info, start, table)


def tiles_kernel(coils, *refs):
    count_ref, res_ref, dir_ref, *refs = refs
    cell_refs, weight_ref = refs[: 2 * coils], refs[2 * coils]
    out_refs, sums_ref = refs[2 * coils + 1 : -1], refs[-1]
    tiles, samples, cells = weight_ref.shape
    rows = [
        ref[:, ri * cells : (ri + 1) * cells] + got[:, ri * cells : (ri + 1) * cells]
        for ref, got in zip(cell_refs[::2], cell_refs[1::2])
        for ri in range(2)
    ]
    found = []
    for tile in range(tiles):
        grid = jnp.concatenate([row[tile : tile + 1] for row in rows], axis=0)
        found.append(
            lax.dot_general(
                grid.astype(BF16),
                weight_ref[tile],
                (((1,), (1,)), ((), ())),
                preferred_element_type=F32,
            )
        )
    spread = []
    for tile in range(tiles):
        live = lax.broadcasted_iota(jnp.int32, found[tile].shape, 1) < count_ref[tile]
        spread.append(dot(jnp.where(live, found[tile], 0.0).astype(BF16), weight_ref[tile]))
    total = 0.0
    for number, row in enumerate(rows):
        value = jnp.concatenate([piece[number : number + 1] for piece in spread], axis=0)
        total = total + row * value
        ri = number % 2
        out_refs[number // 2][:, ri * cells : (ri + 1) * cells] = value
    norm = jnp.sum(res_ref[...], keepdims=True)
    curvature = jnp.sum(total, keepdims=True) + DAMPING * jnp.sum(dir_ref[...], keepdims=True)
    first = lax.broadcasted_iota(jnp.int32, sums_ref.shape, 0) == 0
    sums_ref[...] = jnp.where(first, norm, curvature)


def run_tiles(count, norms, cells, weight):
    coils = len(cells) // 2
    vmem = pl.BlockSpec(memory_space=pltpu.VMEM)
    whole = jax.ShapeDtypeStruct(cells[0].shape, F32)
    *spread, sums = pl.pallas_call(
        lambda *refs: tiles_kernel(coils, *refs),
        in_specs=[pl.BlockSpec(memory_space=pltpu.SMEM)] + [vmem] * (2 * coils + 3),
        out_specs=[vmem] * (coils + 1),
        out_shape=[whole] * coils + [jax.ShapeDtypeStruct((8, 128), F32)],
        compiler_params=params(16),
        name="tiles",
    )(count, *norms, *cells, weight)
    return spread, sums


def turn_kernel(matrix_ref, out_ref):
    for part in range(matrix_ref.shape[1]):
        out_ref[0, part] = jnp.transpose(matrix_ref[0, part].astype(F32)).astype(BF16)


def transposed(matrix):
    pairs, parts, rows, depth = matrix.shape
    return pl.pallas_call(
        turn_kernel,
        grid=(pairs,),
        in_specs=[pl.BlockSpec((1, parts, rows, depth), lambda q: (q, 0, 0, 0))],
        out_specs=pl.BlockSpec((1, parts, depth, rows), lambda q: (q, 0, 0, 0)),
        out_shape=jax.ShapeDtypeStruct((pairs, parts, depth, rows), BF16),
        compiler_params=params(8),
        name="transposed",
    )(matrix)


def finish_kernel(
    planes, depth_pairs, me_ref, sums_ref, mine_ref, got_ref, sens_ref, dir_ref, res_ref, matrix_ref,
    out_ref, norm_ref, squares_ref, *scratch,
):
    coils, rows, _, width = sens_ref.shape[1:]
    half = rows * planes
    group, pair = pl.program_id(0), pl.program_id(1)
    high, low = split(jnp.concatenate([mine_ref[0], got_ref[0]], axis=0), 2)
    left = jnp.concatenate([matrix_ref[0, 0], matrix_ref[0, 1], matrix_ref[0, 0]], axis=1)
    back = dot(left, jnp.concatenate([high, high, low], axis=0))

    @pl.when((group == 0) & (pair == 0))
    def _():
        squares_ref[...] = jnp.zeros(squares_ref.shape, F32)

    def combine(back):
        direction = [dir_ref[ri].reshape(half, width) for ri in range(2)]
        total = [DAMPING * direction[0], DAMPING * direction[1]]
        for coil in range(coils):
            lanes = slice(coil * width, (coil + 1) * width)
            v_re, v_im = back[:half, lanes], back[half:, lanes]
            s_re = sens_ref[0, coil].reshape(half, width)
            s_im = sens_ref[1, coil].reshape(half, width)
            total[0] += s_re * v_re + s_im * v_im
            total[1] += s_re * v_im - s_im * v_re
        squares = 0.0
        step = sums_ref[0:1, 0:1] / sums_ref[1:2, 0:1]
        for ri in range(2):
            value = res_ref[ri].reshape(half, width) - step * total[ri]
            out_ref[ri] = value.reshape(rows, planes, width)
            squares = squares + jnp.sum((value * value).reshape(rows, planes, width), axis=0)
        squares_ref[...] += squares

        @pl.when(group == pl.num_programs(0) - 1)
        def _():
            total = jnp.sum(squares_ref[...], keepdims=True)
            norm_ref[...] = jnp.broadcast_to(total, norm_ref.shape)

    if depth_pairs == 1:
        combine(back)
    else:
        sum_ref = scratch[0]

        @pl.when(pair == 0)
        def _():
            sum_ref[...] = back

        @pl.when(pair > 0)
        def _():
            sum_ref[...] += back

        @pl.when(pair == depth_pairs - 1)
        def _():
            combine(sum_ref[...])


def finish(me, sums, mine, got, sens, direction, residual, matrix, planes, slabs_group):
    _, coils, rows, total, width = sens.shape
    pairs, double, wide = mine.shape
    groups, deep = total // planes, slabs_group // 2

    def place(i, me):
        return lax.bitwise_xor(i * slabs_group, me[0]) // slabs_group

    row_block = pl.BlockSpec((1, double, wide), lambda i, j, me: (i * deep + j, 0, 0))
    image = pl.BlockSpec((2, rows, planes, width), lambda i, j, me: (0, 0, place(i, me), 0))
    return pl.pallas_call(
        lambda *refs: finish_kernel(planes, deep, *refs),
        grid_spec=pltpu.PrefetchScalarGridSpec(
            num_scalar_prefetch=1,
            grid=(groups, deep),
            in_specs=[
                pl.BlockSpec(sums.shape, lambda i, j, me: (0, 0)),
                row_block,
                row_block,
                pl.BlockSpec(
                    (2, coils, rows, planes, width), lambda i, j, me: (0, 0, 0, place(i, me), 0)
                ),
                image,
                image,
                pl.BlockSpec((1,) + matrix.shape[1:], lambda i, j, me: (i * deep + j, 0, 0, 0)),
            ],
            out_specs=[image, pl.BlockSpec(sums.shape, lambda i, j, me: (0, 0))],
            scratch_shapes=[pltpu.VMEM((planes, width), F32)]
            + ([pltpu.VMEM((2 * rows * planes, wide), F32)] if deep > 1 else []),
        ),
        out_shape=[
            jax.ShapeDtypeStruct(residual.shape, F32),
            jax.ShapeDtypeStruct(sums.shape, F32),
        ],
        compiler_params=params(56),
        name="finish",
    )(me, sums, mine, got, sens, direction, residual, matrix)


def swap(value, bit, slabs):
    return lax.ppermute(value, "slab", [(i, i ^ bit) for i in range(slabs)])


def sum_scatter(keep, send, bits, slabs):
    dims = keep.shape[1:]
    left = sorted(bits, reverse=True)
    for number, bit in enumerate(bits):
        axis = left.index(bit)
        left.pop(axis)
        if number > 0:
            value = (keep + got).reshape((2,) * (len(left) + 1) + dims)
            keep = lax.index_in_dim(value, 0, axis, keepdims=False)
            send = lax.index_in_dim(value, 1, axis, keepdims=False)
        got = swap(send, bit, slabs)
    return keep, got


def gather(value, bits, slabs):
    have = []
    for bit in bits:
        other = swap(value, bit, slabs)
        value = jnp.stack([value, other], axis=sum(1 for b in have if b > bit))
        have.append(bit)
    return value


def body(x_image, residual, direction, sensitivity, tile_block, tile_count, tile_weight):
    _, coils, rows, plane_count, ny = sensitivity.shape
    tiles, _, cells = tile_weight.shape
    slabs = lax.axis_size("slab")
    me = lax.axis_index("slab")
    lines = plane_count * GY // slabs
    segment = min(lines, GY)
    per_gx = lines // segment
    unit = math.gcd(cells, segment)
    segments = -(-(segment - unit + cells) // segment)
    planes = 8 if rows % 2 == 0 else 16
    slabs_group = planes * GY // lines
    pairs = slabs // 2
    bits = [1 << i for i in range(slabs.bit_length() - 1)]

    first = tile_block * cells
    start = first % segment
    base = (me * lines) % GY
    info = []
    for k in range(segments):
        row = jnp.minimum(first // segment + k, GX * per_gx - 1)
        plane = (me * lines + (row % per_gx) * segment) // GY
        turn = (base + start - segment * k) % GY // unit
        fields = [row // per_gx, plane % planes, turn, segment * k - start]
        info.append(jnp.stack(fields + [jnp.zeros_like(row)] * (FIELDS - len(fields)), axis=1))
    info = jnp.concatenate(info, axis=0)

    fillers = [lambda: squares(residual), lambda: squares(direction)]
    norms, have = [], []
    for number, bit in enumerate(reversed(bits)):
        other = swap(info, bit, slabs)
        if number < len(fillers):
            norms.append(fillers[number]())
        info = jnp.stack([info, other], axis=sum(1 for b in have if b > bit))
        have.append(bit)
        info, *norms = lax.optimization_barrier((info, *norms))
    info = info.reshape(pairs, 2, segments * tiles, FIELDS)

    x_cos, x_sin = dft(np.arange(GX), np.repeat(np.arange(rows), planes), GX)
    angle = (jnp.arange(GX, dtype=jnp.int32) * (me * rows) % GX).astype(F32) * (2 * math.pi / GX)
    turn_cos, turn_sin = jnp.cos(angle)[:, None], jnp.sin(angle)[:, None]
    x_upper = jnp.asarray(np.hstack([x_cos, x_sin]).astype(np.float32))
    x_lower = jnp.asarray(np.hstack([-x_sin, x_cos]).astype(np.float32))
    x_table = jnp.stack(
        [x_upper * turn_cos + x_lower * turn_sin, x_lower * turn_cos - x_upper * turn_sin]
    )
    x_parts = []
    for _ in range(3):
        part = lax.reduce_precision(x_table, 8, 7)
        x_parts.append(part.astype(BF16))
        x_table = x_table - part
    x_table = jnp.stack(x_parts)
    y_cos, y_sin = dft(np.arange(ny), np.arange(cells), GY)
    y_forward = jnp.asarray(table_parts(np.vstack([y_cos, y_sin]), 3))
    y_back = jnp.asarray(table_parts(np.vstack([y_cos.T, y_sin.T]), 2))
    start_table = np.hstack(dft(np.arange(GY // unit) * unit, np.arange(ny), GY, False))
    start_table = np.pad(start_table, ((0, -start_table.shape[0] % 8), (0, 0)))
    start_table = jnp.asarray(start_table.astype(np.float32))
    me_array = me.astype(jnp.int32)[None]

    keep, send, x_matrix = partial_rows(
        me_array, info, sensitivity, direction, x_table, planes, slabs_group
    )
    got = swap(send, 1, slabs)
    chunk = min(pairs, 4)
    grid = row_cells(
        keep, got, info, start_table, y_forward, tiles, segment, coils, chunk
    )
    high_bits = bits[1:]
    *grid, x_matrix = lax.optimization_barrier((*grid, x_matrix))
    x_matrix = transposed(x_matrix)
    orders = [high_bits[c % 2 :] + high_bits[: c % 2] for c in range(coils)]
    grid = [
        value
        for c, order in enumerate(orders)
        for value in sum_scatter(grid[2 * c], grid[2 * c + 1], order, slabs)
    ]

    *grid, x_matrix = lax.optimization_barrier((*grid, x_matrix))
    spread, sums = run_tiles(tile_count, norms, grid, tile_weight)

    dims = spread[0].shape
    had, have = [[] for _ in spread], [[] for _ in spread]
    for number, bit in enumerate(high_bits):
        sums = sums + swap(sums, bit, slabs)
        for c, order in enumerate(orders):
            way = order[len(order) - 1 - number]
            other = swap(spread[c], way, slabs)
            if number == len(order) - 1:
                had[c] = [spread[c].reshape((-1,) + dims), other.reshape((-1,) + dims)]
            else:
                axis = sum(1 for b in have[c] if b > way)
                spread[c] = jnp.stack([spread[c], other], axis=axis)
                have[c].append(way)
        if number < len(high_bits) - 1:
            sums, *spread = lax.optimization_barrier((sums, *spread))
    sums, *had = lax.optimization_barrier((sums, *had))
    mine = adjoint_rows(had[0] + had[1], info, start_table, y_back, segment, chunk)
    other = swap(mine, 1, slabs)
    sums, mine = lax.optimization_barrier((sums, mine))
    sums = sums + swap(sums, 1, slabs)
    residual_next, norm = finish(
        me_array, sums, mine, other, sensitivity, direction, residual, x_matrix, planes, slabs_group
    )

    pieces = 3
    x_next = None
    for number, bit in enumerate(reversed(bits)):
        norm, x_image = lax.optimization_barrier((norm, x_image))
        other = swap(norm, bit, slabs)
        if number < pieces:
            x_next = x_update(sums, x_image, direction, number, pieces, x_next)
            x_next, x_image = lax.optimization_barrier((x_next, x_image))
        if bit > 1:
            norm, x_next = lax.optimization_barrier((norm + other, x_next))
    direction_next = direction_update(sums, norm, other, residual_next, direction)
    return (x_next, residual_next, direction_next)


def solution(mesh):
    image = P(None, "slab", "frames", None)
    placed = (image, image, image, P(None, None, "slab", None, None)) + (
        P("slab"),
        P("slab"),
        P("slab", None, None),
    )
    return jax.shard_map(
        body, mesh=mesh, in_specs=placed, out_specs=(image, image, image), check_vma=False
    )
```

time: 191 us -> 137 us (0.72)
  other arithmetic: 20.8 us -> 5.34 us
  waiting for transfers between devices: 47 us -> 32.6 us
  Pallas kernels: 69.8 us -> 60.5 us
  between operations: 7.42 us -> 1.02 us
  local copies, waits for them, and re-layouts: 8.96 us -> 3.79 us
  starting transfers between devices: 35.9 us -> 33.2 us
    add x11, other arithmetic: 15.1 us -> 0.73 us  [the longest x1 0.59 us: body(): sums = sums + swap(sums, 1, slabs)]
    ppermute x26, waiting for transfers between devices: 47 us -> 32.6 us  [swap(): return lax.ppermute(value, 'slab', [(i, i ^ bit) for i in range(slabs)])]
    pallas_call x1, Pallas kernels: 5.66 us -> 1.61 us  [run_tiles(): pl.pallas_call(lambda *refs: tiles_kernel(coils, *refs), in_specs=[pl.Blo...]
    pallas_call x1, Pallas kernels: 10.3 us -> 6.77 us  [row_cells(): pl.pallas_call(lambda *refs: cells_kernel(tiles, segment, *refs), grid=(p...]
    pallas_call x1, Pallas kernels: 17.9 us -> 15 us  [finish(): pl.pallas_call(lambda *refs: finish_kernel(planes, deep, *refs), grid_spe...]
    ppermute x26, starting transfers between devices: 35.9 us -> 33.2 us  [swap(): return lax.ppermute(value, 'slab', [(i, i ^ bit) for i in range(slabs)])]
    another operation x5 -> x1, local copies, waits for them, and re-layouts: 2.65 us -> 0.01 us  [the longest x3 2.51 us: gather(): value = jnp.stack([value, other], axis=axis)]
    slice x3 -> x1, local copies, waits for them, and re-layouts: 2.24 us -> 0.01 us  [sum_scatter(): send = lax.index_in_dim(value, 1, axis, keepdims=False)]
  transfers between devices with their start and end apart: 26 -> 26, of which waited for: 22 -> 14; matrix products, arithmetic and copies ran while one was open for 6% -> 3% of each run, Pallas kernels for 8% -> 10%
where the time goes in v2:
time: 137 us; the launch traced here: 136 us
  Pallas kernels  60.5 us (44%)
  starting transfers between devices  33.2 us (24%)
  waiting for transfers between devices  32.6 us (24%)
  other arithmetic  5.34 us (4%)
  local copies, waits for them, and re-layouts  3.79 us (3%)
    ppermute x26, starting transfers between devices, swap(): return lax.ppermute(value, 'slab', [(i, i ^ bit) for i in range(slabs)])  33.2 us
    ppermute x26, waiting for transfers between devices, swap(): return lax.ppermute(value, 'slab', [(i, i ^ bit) for i in range(slabs)])  32.6 us
    pallas_call x1, Pallas kernels, finish(): pl.pallas_call(lambda *refs: finish_kernel(planes, deep, *refs), grid_spe...  15 us
    pallas_call x1, Pallas kernels, partial_rows(): pl.pallas_call(lambda *refs: rows_kernel(planes, per_step, slabs_group //...  13.5 us
    pallas_call x3, Pallas kernels, x_update(): pl.pallas_call(x_kernel, grid=(rows // step,), in_specs=[pl.BlockSpec(sum...  12.1 us
    pallas_call x1, Pallas kernels, row_cells(): pl.pallas_call(lambda *refs: cells_kernel(tiles, segment, *refs), grid=(p...  6.77 us
    pallas_call x1, Pallas kernels, direction_update(): pl.pallas_call(direction_kernel, grid=(rows // step,), in_specs=[small, s...  5.23 us
    pallas_call x1, Pallas kernels, adjoint_rows(): pl.pallas_call(lambda *refs: adjoint_kernel(segment, coils, chunk, *refs)...  4.4 us
  transfers between devices with their start and end apart: 26, of which 14 were waited for; matrix products, arithmetic and copies ran while one was open for 3% of the time, Pallas kernels for 10%

profile of v2, /device:TPU:0, one launch (start us, length us, event | category | flops | bytes accessed | tf_op | source)
XLA Modules:
  0.0 136.5 jit_solution(8372238715525319924)
XLA Ops:
  1.6 4.0 %collective-permute-start = (s32[32,8]{0,1:T(8,128)S(1)}, s32[32,8]{0,1:T(8,128)S(1)}, u32[]{:S(2)}, u32[]{:S(2)}) collective-permute-start(s32[32,8]{0,1:T(8,128)S(1)} %pad_add_fusion.4), channel_id=1, source_target_pairs={{0,8},{1,9},{2,10},{3,11},{4,12},{5,13},{6,14},{7,15},{8,0},{9,1},... | collective-permute-start | bytes 3080 | tf_op jit(solution)/shard_map/ppermute | solution.py:540
  5.7 2.3 %copy-done.1 = f32[2,24,64,384]{3,2,1,0:T(8,128)S(1)} copy-done((f32[2,24,64,384]{3,2,1,0:T(8,128)S(1)}, f32[2,24,64,384]{3,2,1,0:T(8,128)}, u32[]{:S(2)}) %copy-start.1) | copy-done | bytes 4718616
  14.2 1.9 %collective-permute-done.2 = s32[2,2,32,8]{2,3,1,0:T(8,128)S(1)} collective-permute-done((s32[2,2,32,8]{2,3,1,0:T(8,128)S(1)}, s32[2,2,32,8]{2,3,1,0:T(8,128)S(1)}, u32[]{:S(2)}, u32[]{:S(2)}) %collective-permute-start.2) | collective-permute-done | bytes 4128 | tf_op jit(solution)/shard_map/ppermute | solution.py:540
  16.0 1.7 %pad_maximum_fusion.refs_4_ = bf16[3,2,480,384]{3,2,1,0:T(8,128)(2,1)} fusion(bf16[1,2,480,384]{3,2,1,0:T(8,128)(2,1)S(1)} %get-tuple-element.139, bf16[1,2,480,384]{3,2,1,0:T(8,128)(2,1)S(1)} %get-tuple-element.138, bf16[1,2,480,384]{3,2,1,0:T(8,128)(2,1)S(1)} %get-tuple-element.137), kind=kLoop, calls=%fused_computation | loop fusion | flops 2211840 | bytes 4423680 | tf_op jit(solution)/shard_map/stack | solution.py:617
  17.9 13.5 %partial_rows.1 = (f32[8,64,768]{2,1,0:T(8,128)S(1)}, f32[8,64,768]{2,1,0:T(8,128)S(1)}, bf16[8,2,128,384]{3,2,1,0:T(8,128)(2,1)S(1)}) custom-call(s32[1]{0:T(128)} %bitcast.refs_0_, s32[8,2,32,8]{3,2,1,0:T(8,128)S(1)} %bitcast.102, f32[2,2,24,64,384]{4,3,2,1,0:T(8,128)} %refs_4_.2, f32[2,24,64,384]{3,2,1,0:T(8,128)} %refs_5_.2, ...), custom_call_target="tpu_custom_call" | custom-call | tf_op jit(solution)/shard_map/partial_rows/pallas_call | solution.py:216
  31.9 3.0 %collective-permute-done.4.refs_1_ = f32[8,64,768]{2,1,0:T(8,128)S(1)} collective-permute-done((f32[8,64,768]{2,1,0:T(8,128)S(1)}, f32[8,64,768]{2,1,0:T(8,128)S(1)}, u32[]{:S(2)}, u32[]{:S(2)}) %collective-permute-start.4) | collective-permute-done | bytes 1572896 | tf_op jit(solution)/shard_map/ppermute | solution.py:540
  35.0 6.8 %row_cells.1 = (f32[4,16,1024]{2,1,0:T(8,128)S(1)}, f32[4,16,1024]{2,1,0:T(8,128)S(1)}, f32[4,16,1024]{2,1,0:T(8,128)S(1)}, f32[4,16,1024]{2,1,0:T(8,128)S(1)}) custom-call(f32[8,64,768]{2,1,0:T(8,128)S(1)} %get-tuple-element.77.refs_0_, f32[8,64,768]{2,1,0:T(8,128)S(1)} %collective-permute-done.4.refs_1_, s32[8,2,32,8]{3,2,1,0:T(8,128)S(1)} %bitcast.103, ...), custom_call_target="tpu_custom_call" | custom-call | tf_op jit(solution)/shard_map/row_cells/pallas_call | solution.py:302
  44.9 5.5 %collective-permute-done.5 = f32[4,16,1024]{2,1,0:T(8,128)S(1)} collective-permute-done((f32[4,16,1024]{2,1,0:T(8,128)S(1)}, f32[4,16,1024]{2,1,0:T(8,128)S(1)}, u32[]{:S(2)}, u32[]{:S(2)}) %collective-permute-start.5) | collective-permute-done | bytes 262176 | tf_op jit(solution)/shard_map/ppermute | solution.py:540
  53.7 2.8 %collective-permute-done.6 = f32[2,16,1024]{2,1,0:T(8,128)S(1)} collective-permute-done((f32[2,16,1024]{2,1,0:T(8,128)S(1)}, f32[2,16,1024]{2,1,0:T(8,128)S(1)}, u32[]{:S(2)}, u32[]{:S(2)}) %collective-permute-start.6) | collective-permute-done | bytes 131104 | tf_op jit(solution)/shard_map/ppermute | solution.py:540
  58.2 3.8 %collective-permute-done.9 = f32[2,16,1024]{2,1,0:T(8,128)S(1)} collective-permute-done((f32[2,16,1024]{2,1,0:T(8,128)S(1)}, f32[2,16,1024]{2,1,0:T(8,128)S(1)}, u32[]{:S(2)}, u32[]{:S(2)}) %collective-permute-start.9) | collective-permute-done | bytes 131104 | tf_op jit(solution)/shard_map/ppermute | solution.py:540
  71.7 2.1 %collective-permute-done.12 = f32[16,1024]{1,0:T(8,128)S(1)} collective-permute-done((f32[16,1024]{1,0:T(8,128)S(1)}, f32[16,1024]{1,0:T(8,128)S(1)}, u32[]{:S(2)}, u32[]{:S(2)}) %collective-permute-start.12) | collective-permute-done | bytes 65568 | tf_op jit(solution)/shard_map/ppermute | solution.py:540
  73.9 1.8 %collective-permute-start.15 = (f32[2,16,1024]{2,1,0:T(8,128)S(1)}, f32[2,16,1024]{2,1,0:T(8,128)S(1)}, u32[]{:S(2)}, u32[]{:S(2)}) collective-permute-start(f32[2,16,1024]{2,1,0:T(8,128)S(1)} %pad_maximum_fusion.4), channel_id=1, source_target_pairs={{0,4},{1,5},{2,6},{3,7},{4,0},{5,1},{6,2},{7,3},{8,12},{9,13},{10,... | collective-permute-start | bytes 393224 | tf_op jit(solution)/shard_map/ppermute | solution.py:540
  76.9 1.9 %collective-permute-start.14 = (f32[8,128]{1,0:T(8,128)S(1)}, f32[8,128]{1,0:T(8,128)S(1)}, u32[]{:S(2)}, u32[]{:S(2)}) collective-permute-start(f32[8,128]{1,0:T(8,128)S(1)} %add.132), channel_id=1, source_target_pairs={{0,4},{1,5},{2,6},{3,7},{4,0},{5,1},{6,2},{7,3},{8,12},{9,13},{10,... | collective-permute-start | bytes 12296 | tf_op jit(solution)/shard_map/ppermute | solution.py:540
  78.9 2.7 %collective-permute-done.14 = f32[8,128]{1,0:T(8,128)S(1)} collective-permute-done((f32[8,128]{1,0:T(8,128)S(1)}, f32[8,128]{1,0:T(8,128)S(1)}, u32[]{:S(2)}, u32[]{:S(2)}) %collective-permute-start.14) | collective-permute-done | bytes 4128 | tf_op jit(solution)/shard_map/ppermute | solution.py:540
  82.2 2.6 %collective-permute-start.18 = (f32[2,2,16,1024]{3,2,0,1:T(8,128)S(1)}, f32[2,2,16,1024]{3,2,0,1:T(8,128)S(1)}, u32[]{:S(2)}, u32[]{:S(2)}) collective-permute-start(f32[2,2,16,1024]{3,2,0,1:T(8,128)S(1)} %pad_maximum_fusion.2), channel_id=1, source_target_pairs={{0,2},{1,3},{2,0},{3,1},{4,6},{5,7},{6,4},{7,5},{8,10},{9,11},{10,... | collective-permute-start | bytes 786440 | tf_op jit(solution)/shard_map/ppermute | solution.py:540
  86.8 3.8 %collective-permute-done.17 = f32[8,128]{1,0:T(8,128)S(1)} collective-permute-done((f32[8,128]{1,0:T(8,128)S(1)}, f32[8,128]{1,0:T(8,128)S(1)}, u32[]{:S(2)}, u32[]{:S(2)}) %collective-permute-start.17) | collective-permute-done | bytes 4128 | tf_op jit(solution)/shard_map/ppermute | solution.py:540
  91.2 4.4 %adjoint_rows.1.refs_2_ = f32[8,64,768]{2,1,0:T(8,128)S(1)} custom-call(f32[4,16,1024]{2,1,0:T(8,128)S(1)} %bitcast.106, f32[4,16,1024]{2,1,0:T(8,128)S(1)} %bitcast.107, f32[4,16,1024]{2,1,0:T(8,128)S(1)} %bitcast.105, f32[4,16,1024]{2,1,0:T(8,128)S(1)} %bitcast.108, s32[8,2,32,8]{3,2,1,0:T(8,128)S(1)} %bitcast.104, f32[16,768]{1,0:T(8,128)S(1)} %copy-done.7, ...), custom_call_target="tpu_custom_call" | custom-call | tf_op jit(solution)/shard_map/adjoint_rows/pallas_call | solution.py:358
  96.2 2.5 %collective-permute-done.20 = f32[8,128]{1,0:T(8,128)S(1)} collective-permute-done((f32[8,128]{1,0:T(8,128)S(1)}, f32[8,128]{1,0:T(8,128)S(1)}, u32[]{:S(2)}, u32[]{:S(2)}) %collective-permute-start.20) | collective-permute-done | bytes 4128 | tf_op jit(solution)/shard_map/ppermute | solution.py:540
  99.3 15.0 %finish.1 = (f32[2,24,64,384]{3,2,1,0:T(8,128)}, f32[8,128]{1,0:T(8,128)}) custom-call(s32[1]{0:T(128)} %bitcast.refs_0_, f32[8,128]{1,0:T(8,128)} %add.135.refs_1_.sums_ref, f32[8,64,768]{2,1,0:T(8,128)} %copy-done.3, f32[8,64,768]{2,1,0:T(8,128)} %collective-permute-done.21.refs_3_, f32[2,2,24,64,384]{4,3,2,1,0:T(8,128)} %refs_4_.2, ...), custom_call_target="tpu_custom_call" | custom-call | tf_op jit(solution)/shard_map/finish/pallas_call | solution.py:510
  114.3 2.2 %collective-permute-start.22 = (f32[8,128]{1,0:T(8,128)}, f32[8,128]{1,0:T(8,128)S(1)}, u32[]{:S(2)}, u32[]{:S(2)}) collective-permute-start(f32[8,128]{1,0:T(8,128)} %get-tuple-element.111), channel_id=1, source_target_pairs={{0,8},{1,9},{2,10},{3,11},{4,12},{5,13},{6,14},{7,15},{8,0},{9,1},... | collective-permute-start | bytes 12296 | tf_op jit(solution)/shard_map/ppermute | solution.py:540
  116.6 3.7 %x_update.3 = f32[48,64,384]{2,1,0:T(8,128)} custom-call(f32[8,128]{1,0:T(8,128)S(1)} %copy-done.8, f32[48,64,384]{2,1,0:T(8,128)S(1)} %bitcast.95, f32[48,64,384]{2,1,0:T(8,128)} %bitcast.86), custom_call_target="tpu_custom_call" | custom-call | tf_op jit(solution)/shard_map/x_update/pallas_call | solution.py:100
  121.1 3.7 %x_update.4 = f32[48,64,384]{2,1,0:T(8,128)} custom-call(f32[8,128]{1,0:T(8,128)S(1)} %copy-done.8, f32[48,64,384]{2,1,0:T(8,128)S(1)} %bitcast.96, f32[48,64,384]{2,1,0:T(8,128)} %bitcast.87, f32[48,64,384]{2,1,0:T(8,128)} %x_update.3), custom_call_target="tpu_custom_call", output_to_operand_aliasing={{}: (3, {})} | custom-call | tf_op jit(solution)/shard_map/x_update/pallas_call | solution.py:100
  125.4 4.6 %x_update.5 = f32[48,64,384]{2,1,0:T(8,128)} custom-call(f32[8,128]{1,0:T(8,128)S(1)} %copy-done.8, f32[48,64,384]{2,1,0:T(8,128)S(1)} %bitcast.97, f32[48,64,384]{2,1,0:T(8,128)} %bitcast.88, f32[48,64,384]{2,1,0:T(8,128)} %x_update.4), custom_call_target="tpu_custom_call", output_to_operand_aliasing={{}: (3, {})} | custom-call | tf_op jit(solution)/shard_map/x_update/pallas_call | solution.py:100
  131.3 5.2 %direction_update.1 = f32[48,64,384]{2,1,0:T(8,128)} custom-call(f32[8,128]{1,0:T(8,128)S(1)} %copy-done.8, f32[8,128]{1,0:T(8,128)S(1)} %add.138.one_ref, f32[8,128]{1,0:T(8,128)S(1)} %collective-permute-done.25.two_ref, f32[48,64,384]{2,1,0:T(8,128)S(1)} %bitcast.101, f32[48,64,384]{2,1,0:T(8,128)S(1)} %bitcast.92), custom_call_target="tpu_custom_call" | custom-call | tf_op jit(solution)/shard_map/direction_update/pallas_call | solution.py:126
  (115 shorter events, 33.8 us)
Async XLA Ops:
  1.6 6.9 %collective-permute-start = (s32[32,8]{0,1:T(8,128)S(1)}, s32[32,8]{0,1:T(8,128)S(1)}, u32[]{:S(2)}, u32[]{:S(2)}) collective-permute-start(s32[32,8]{0,1:T(8,128)S(1)} %pad_add_fusion.4), channel_id=1, source_target_pairs={{0,8},{1,9},{2,10},{3,11},{4,12},{5,13},{6,14},{7,15},{8,0},{9,1},... | collective-permute-start | bytes 3080 | tf_op jit(solution)/shard_map/ppermute | solution.py:540
  8.5 3.7 %collective-permute-start.1 = (s32[2,32,8]{1,2,0:T(8,128)S(1)}, s32[2,32,8]{1,2,0:T(8,128)S(1)}, u32[]{:S(2)}, u32[]{:S(2)}) collective-permute-start(s32[2,32,8]{1,2,0:T(8,128)S(1)} %pad_add_fusion.3), channel_id=1, source_target_pairs={{0,4},{1,5},{2,6},{3,7},{4,0},{5,1},{6,2},{7,3},{8,12},{9,13},{10,... | collective-permute-start | bytes 6152 | tf_op jit(solution)/shard_map/ppermute | solution.py:540
  12.2 3.8 %collective-permute-start.2 = (s32[2,2,32,8]{2,3,1,0:T(8,128)S(1)}, s32[2,2,32,8]{2,3,1,0:T(8,128)S(1)}, u32[]{:S(2)}, u32[]{:S(2)}) collective-permute-start(s32[2,2,32,8]{2,3,1,0:T(8,128)S(1)} %pad_add_fusion.2), channel_id=1, source_target_pairs={{0,2},{1,3},{2,0},{3,1},{4,6},{5,7},{6,4},{7,5},{8,10},{9,11},{10,... | collective-permute-start | bytes 12296 | tf_op jit(solution)/shard_map/ppermute | solution.py:540
  31.3 3.6 %collective-permute-start.4 = (f32[8,64,768]{2,1,0:T(8,128)S(1)}, f32[8,64,768]{2,1,0:T(8,128)S(1)}, u32[]{:S(2)}, u32[]{:S(2)}) collective-permute-start(f32[8,64,768]{2,1,0:T(8,128)S(1)} %get-tuple-element.78), channel_id=1, source_target_pairs={{0,1},{1,0},{2,3},{3,2},{4,5},{5,4},{6,7},{7,6},{8,9},{9,8},{10,11... | collective-permute-start | bytes 4718600 | tf_op jit(solution)/shard_map/ppermute | solution.py:540
  41.7 8.7 %collective-permute-start.5 = (f32[4,16,1024]{2,1,0:T(8,128)S(1)}, f32[4,16,1024]{2,1,0:T(8,128)S(1)}, u32[]{:S(2)}, u32[]{:S(2)}) collective-permute-start(f32[4,16,1024]{2,1,0:T(8,128)S(1)} %get-tuple-element.85), channel_id=1, source_target_pairs={{0,2},{1,3},{2,0},{3,1},{4,6},{5,7},{6,4},{7,5},{8,10},{9,11},{10,... | collective-permute-start | bytes 786440 | tf_op jit(solution)/shard_map/ppermute | solution.py:540
  43.3 8.7 %collective-permute-start.8 = (f32[4,16,1024]{2,1,0:T(8,128)S(1)}, f32[4,16,1024]{2,1,0:T(8,128)S(1)}, u32[]{:S(2)}, u32[]{:S(2)}) collective-permute-start(f32[4,16,1024]{2,1,0:T(8,128)S(1)} %get-tuple-element.87), channel_id=1, source_target_pairs={{0,4},{1,5},{2,6},{3,7},{4,0},{5,1},{6,2},{7,3},{8,12},{9,13},{10,... | collective-permute-start | bytes 786440 | tf_op jit(solution)/shard_map/ppermute | solution.py:540
  50.4 6.0 %collective-permute-start.6 = (f32[2,16,1024]{2,1,0:T(8,128)S(1)}, f32[2,16,1024]{2,1,0:T(8,128)S(1)}, u32[]{:S(2)}, u32[]{:S(2)}) collective-permute-start(f32[2,16,1024]{2,1,0:T(8,128)S(1)} %slice_bitcast_fusion), channel_id=1, source_target_pairs={{0,4},{1,5},{2,6},{3,7},{4,0},{5,1},{6,2},{7,3},{8,12},{9,13},{10,... | collective-permute-start | bytes 393224 | tf_op jit(solution)/shard_map/ppermute | solution.py:540
  52.1 9.9 %collective-permute-start.9 = (f32[2,16,1024]{2,1,0:T(8,128)S(1)}, f32[2,16,1024]{2,1,0:T(8,128)S(1)}, u32[]{:S(2)}, u32[]{:S(2)}) collective-permute-start(f32[2,16,1024]{2,1,0:T(8,128)S(1)} %slice.39), channel_id=1, source_target_pairs={{0,8},{1,9},{2,10},{3,11},{4,12},{5,13},{6,14},{7,15},{8,0},{9,1},... | collective-permute-start | bytes 393224 | tf_op jit(solution)/shard_map/ppermute | solution.py:540
  56.5 9.4 %collective-permute-start.7 = (f32[16,1024]{1,0:T(8,128)S(1)}, f32[16,1024]{1,0:T(8,128)S(1)}, u32[]{:S(2)}, u32[]{:S(2)}) collective-permute-start(f32[16,1024]{1,0:T(8,128)S(1)} %get-tuple-element.142), channel_id=1, source_target_pairs={{0,8},{1,9},{2,10},{3,11},{4,12},{5,13},{6,14},{7,15},{8,0},{9,1},... | collective-permute-start | bytes 196616 | tf_op jit(solution)/shard_map/ppermute | solution.py:540
  62.0 4.3 %collective-permute-start.10 = (f32[16,1024]{1,0:T(8,128)S(1)}, f32[16,1024]{1,0:T(8,128)S(1)}, u32[]{:S(2)}, u32[]{:S(2)}) collective-permute-start(f32[16,1024]{1,0:T(8,128)S(1)} %get-tuple-element.140), channel_id=1, source_target_pairs={{0,2},{1,3},{2,0},{3,1},{4,6},{5,7},{6,4},{7,5},{8,10},{9,11},{10,... | collective-permute-start | bytes 196616 | tf_op jit(solution)/shard_map/ppermute | solution.py:540
  68.0 5.9 %collective-permute-start.12 = (f32[16,1024]{1,0:T(8,128)S(1)}, f32[16,1024]{1,0:T(8,128)S(1)}, u32[]{:S(2)}, u32[]{:S(2)}) collective-permute-start(f32[16,1024]{1,0:T(8,128)S(1)} %get-tuple-element.94), channel_id=1, source_target_pairs={{0,8},{1,9},{2,10},{3,11},{4,12},{5,13},{6,14},{7,15},{8,0},{9,1},... | collective-permute-start | bytes 196616 | tf_op jit(solution)/shard_map/ppermute | solution.py:540
  68.0 3.7 %collective-permute-start.11 = (f32[8,128]{1,0:T(8,128)S(1)}, f32[8,128]{1,0:T(8,128)S(1)}, u32[]{:S(2)}, u32[]{:S(2)}) collective-permute-start(f32[8,128]{1,0:T(8,128)S(1)} %get-tuple-element.93), channel_id=1, source_target_pairs={{0,2},{1,3},{2,0},{3,1},{4,6},{5,7},{6,4},{7,5},{8,10},{9,11},{10,... | collective-permute-start | bytes 12296 | tf_op jit(solution)/shard_map/ppermute | solution.py:540
  69.6 4.3 %collective-permute-start.13 = (f32[16,1024]{1,0:T(8,128)S(1)}, f32[16,1024]{1,0:T(8,128)S(1)}, u32[]{:S(2)}, u32[]{:S(2)}) collective-permute-start(f32[16,1024]{1,0:T(8,128)S(1)} %get-tuple-element.95), channel_id=1, source_target_pairs={{0,2},{1,3},{2,0},{3,1},{4,6},{5,7},{6,4},{7,5},{8,10},{9,11},{10,... | collective-permute-start | bytes 196616 | tf_op jit(solution)/shard_map/ppermute | solution.py:540
  73.9 7.6 %collective-permute-start.15 = (f32[2,16,1024]{2,1,0:T(8,128)S(1)}, f32[2,16,1024]{2,1,0:T(8,128)S(1)}, u32[]{:S(2)}, u32[]{:S(2)}) collective-permute-start(f32[2,16,1024]{2,1,0:T(8,128)S(1)} %pad_maximum_fusion.4), channel_id=1, source_target_pairs={{0,4},{1,5},{2,6},{3,7},{4,0},{5,1},{6,2},{7,3},{8,12},{9,13},{10,... | collective-permute-start | bytes 393224 | tf_op jit(solution)/shard_map/ppermute | solution.py:540
  75.7 6.4 %collective-permute-start.16 = (f32[2,16,1024]{2,1,0:T(8,128)S(1)}, f32[2,16,1024]{2,1,0:T(8,128)S(1)}, u32[]{:S(2)}, u32[]{:S(2)}) collective-permute-start(f32[2,16,1024]{2,1,0:T(8,128)S(1)} %pad_maximum_fusion.5), channel_id=1, source_target_pairs={{0,8},{1,9},{2,10},{3,11},{4,12},{5,13},{6,14},{7,15},{8,0},{9,1},... | collective-permute-start | bytes 393224 | tf_op jit(solution)/shard_map/ppermute | solution.py:540
  76.9 4.6 %collective-permute-start.14 = (f32[8,128]{1,0:T(8,128)S(1)}, f32[8,128]{1,0:T(8,128)S(1)}, u32[]{:S(2)}, u32[]{:S(2)}) collective-permute-start(f32[8,128]{1,0:T(8,128)S(1)} %add.132), channel_id=1, source_target_pairs={{0,4},{1,5},{2,6},{3,7},{4,0},{5,1},{6,2},{7,3},{8,12},{9,13},{10,... | collective-permute-start | bytes 12296 | tf_op jit(solution)/shard_map/ppermute | solution.py:540
  82.2 8.4 %collective-permute-start.18 = (f32[2,2,16,1024]{3,2,0,1:T(8,128)S(1)}, f32[2,2,16,1024]{3,2,0,1:T(8,128)S(1)}, u32[]{:S(2)}, u32[]{:S(2)}) collective-permute-start(f32[2,2,16,1024]{3,2,0,1:T(8,128)S(1)} %pad_maximum_fusion.2), channel_id=1, source_target_pairs={{0,2},{1,3},{2,0},{3,1},{4,6},{5,7},{6,4},{7,5},{8,10},{9,11},{10,... | collective-permute-start | bytes 786440 | tf_op jit(solution)/shard_map/ppermute | solution.py:540
  84.8 6.4 %collective-permute-start.19 = (f32[2,2,16,1024]{3,2,1,0:T(8,128)S(1)}, f32[2,2,16,1024]{3,2,1,0:T(8,128)S(1)}, u32[]{:S(2)}, u32[]{:S(2)}) collective-permute-start(f32[2,2,16,1024]{3,2,1,0:T(8,128)S(1)} %pad_maximum_fusion.3), channel_id=1, source_target_pairs={{0,4},{1,5},{2,6},{3,7},{4,0},{5,1},{6,2},{7,3},{8,12},{9,13},{10,... | collective-permute-start | bytes 786440 | tf_op jit(solution)/shard_map/ppermute | solution.py:540
  86.0 4.6 %collective-permute-start.17 = (f32[8,128]{1,0:T(8,128)S(1)}, f32[8,128]{1,0:T(8,128)S(1)}, u32[]{:S(2)}, u32[]{:S(2)}) collective-permute-start(f32[8,128]{1,0:T(8,128)S(1)} %add.133), channel_id=1, source_target_pairs={{0,8},{1,9},{2,10},{3,11},{4,12},{5,13},{6,14},{7,15},{8,0},{9,1},... | collective-permute-start | bytes 12296 | tf_op jit(solution)/shard_map/ppermute | solution.py:540
  95.6 3.7 %collective-permute-start.21 = (f32[8,64,768]{2,1,0:T(8,128)S(1)}, f32[8,64,768]{2,1,0:T(8,128)}, u32[]{:S(2)}, u32[]{:S(2)}) collective-permute-start(f32[8,64,768]{2,1,0:T(8,128)S(1)} %adjoint_rows.1.refs_2_), channel_id=1, source_target_pairs={{0,1},{1,0},{2,3},{3,2},{4,5},{5,4},{6,7},{7,6},{8,9},{9,8},{10,11... | collective-permute-start | bytes 4718600 | tf_op jit(solution)/shard_map/ppermute | solution.py:540
  95.7 3.0 %collective-permute-start.20 = (f32[8,128]{1,0:T(8,128)S(1)}, f32[8,128]{1,0:T(8,128)S(1)}, u32[]{:S(2)}, u32[]{:S(2)}) collective-permute-start(f32[8,128]{1,0:T(8,128)S(1)} %add.134), channel_id=1, source_target_pairs={{0,1},{1,0},{2,3},{3,2},{4,5},{5,4},{6,7},{7,6},{8,9},{9,8},{10,11... | collective-permute-start | bytes 12296 | tf_op jit(solution)/shard_map/ppermute | solution.py:540
  114.3 5.9 %collective-permute-start.22 = (f32[8,128]{1,0:T(8,128)}, f32[8,128]{1,0:T(8,128)S(1)}, u32[]{:S(2)}, u32[]{:S(2)}) collective-permute-start(f32[8,128]{1,0:T(8,128)} %get-tuple-element.111), channel_id=1, source_target_pairs={{0,8},{1,9},{2,10},{3,11},{4,12},{5,13},{6,14},{7,15},{8,0},{9,1},... | collective-permute-start | bytes 12296 | tf_op jit(solution)/shard_map/ppermute | solution.py:540
  120.3 4.5 %collective-permute-start.23 = (f32[8,128]{1,0:T(8,128)S(1)}, f32[8,128]{1,0:T(8,128)S(1)}, u32[]{:S(2)}, u32[]{:S(2)}) collective-permute-start(f32[8,128]{1,0:T(8,128)S(1)} %add.136), channel_id=1, source_target_pairs={{0,4},{1,5},{2,6},{3,7},{4,0},{5,1},{6,2},{7,3},{8,12},{9,13},{10,... | collective-permute-start | bytes 12296 | tf_op jit(solution)/shard_map/ppermute | solution.py:540
  124.9 5.1 %collective-permute-start.24 = (f32[8,128]{1,0:T(8,128)S(1)}, f32[8,128]{1,0:T(8,128)S(1)}, u32[]{:S(2)}, u32[]{:S(2)}) collective-permute-start(f32[8,128]{1,0:T(8,128)S(1)} %add.137), channel_id=1, source_target_pairs={{0,2},{1,3},{2,0},{3,1},{4,6},{5,7},{6,4},{7,5},{8,10},{9,11},{10,... | collective-permute-start | bytes 12296 | tf_op jit(solution)/shard_map/ppermute | solution.py:540
  (19 other events, 172.1 us)

commit v3 on v2

v3 whole, which is shorter than its diff:
```python
import math

import jax
import jax.numpy as jnp
import ml_dtypes
import numpy as np
from jax import lax
from jax.experimental import pallas as pl
from jax.experimental.pallas import tpu as pltpu
from jax.sharding import PartitionSpec as P

GX = 480
GY = 480
DAMPING = 0.1
HIGHEST = lax.Precision.HIGHEST
F32 = jnp.float32
BF16 = jnp.bfloat16
MIB = 1024 * 1024
FIELDS = 8


def dft(out_index, in_index, size, scaled=True):
    angle = (out_index[:, None] * in_index[None, :] % size) * (2.0 * math.pi / size)
    scale = 1.0 / math.sqrt(size) if scaled else 1.0
    return np.cos(angle) * scale, np.sin(angle) * scale


def table_parts(table, count):
    parts = []
    for _ in range(count):
        part = table.astype(ml_dtypes.bfloat16)
        parts.append(part)
        table = table - part.astype(np.float64)
    return np.stack(parts)


def split(value, count):
    parts = []
    for step in range(count):
        part = value.astype(BF16)
        parts.append(part)
        if step + 1 < count:
            value = value - part.astype(F32)
    return parts


def dot(a, b):
    return lax.dot_general(a, b, (((1,), (0,)), ((), ())), preferred_element_type=F32)


def six_products(lhs, rhs):
    rows = lhs[0].shape[0]
    first = dot(jnp.concatenate(lhs, axis=0), rhs[0])
    second = dot(jnp.concatenate(lhs[:2], axis=0), rhs[1])
    third = dot(lhs[0], rhs[2])
    small = first[2 * rows :] + second[rows:] + third
    return first[:rows] + (first[rows : 2 * rows] + second[:rows] + small)


def params(mib):
    return pltpu.CompilerParams(vmem_limit_bytes=mib * MIB)


def resident():
    return pl.BlockSpec(memory_space=pltpu.VMEM)


def in_hbm():
    return pl.BlockSpec(memory_space=pltpu.HBM)


def scalars():
    return pl.BlockSpec(memory_space=pltpu.SMEM)


def blocks(shape, index, steps):
    return resident() if steps == 1 else pl.BlockSpec(shape, index)


def load_kernel(from_hbm, out_ref, sem):
    copies = [
        pltpu.make_async_copy(from_hbm.at[piece], out_ref.at[piece], sem.at[piece])
        for piece in range(out_ref.shape[0])
    ]
    for copy in copies:
        copy.start()
    for copy in copies:
        copy.wait()


def load(value):
    flat = (-1,) + value.shape[-3:]
    out = pltpu.with_memory_space_constraint(value.reshape(flat), pltpu.HBM)
    out = pl.pallas_call(
        load_kernel,
        in_specs=[in_hbm()],
        out_specs=resident(),
        out_shape=jax.ShapeDtypeStruct(out.shape, F32),
        scratch_shapes=[pltpu.SemaphoreType.DMA((out.shape[0],))],
        compiler_params=params(2),
        name="load",
    )(out)
    return out.reshape(value.shape)


def squares_kernel(res_ref, norm_ref):
    rows = res_ref.shape[1]

    def step(row, total):
        return total + res_ref[0, row] * res_ref[0, row] + res_ref[1, row] * res_ref[1, row]

    total = lax.fori_loop(0, rows, step, jnp.zeros(res_ref.shape[2:], F32))
    total = jnp.sum(total, keepdims=True)
    first = lax.broadcasted_iota(jnp.int32, norm_ref.shape, 0) == 0
    norm_ref[...] = jnp.where(first, total, 0.0)


def squares(residual):
    return pl.pallas_call(
        squares_kernel,
        in_specs=[resident()],
        out_specs=resident(),
        out_shape=jax.ShapeDtypeStruct((8, 128), F32),
        compiler_params=params(8),
        name="squares",
    )(residual)


def x_kernel(first, sums_ref, x_ref, dir_ref, *refs):
    rows = x_ref.shape[0]
    step = sums_ref[0:1, 0:1] / sums_ref[1:2, 0:1]
    at = pl.ds(first + pl.program_id(0) * rows, rows)
    refs[-1][...] = x_ref[...] + step * dir_ref[at]


def x_update(sums, x_image, direction, piece, pieces, before):
    dims = x_image.shape
    flat = (-1,) + dims[2:]
    rows = dims[0] * dims[1] // pieces
    step = rows // 2
    given = [] if before is None else [before.reshape(flat)]
    block = pl.BlockSpec((step,) + dims[2:], lambda i: (2 * piece + i, 0, 0))
    out = pl.pallas_call(
        lambda *refs: x_kernel(piece * rows, *refs),
        grid=(2,),
        in_specs=[resident(), block, resident()] + [in_hbm()] * len(given),
        out_specs=block,
        out_shape=jax.ShapeDtypeStruct((dims[0] * dims[1],) + dims[2:], F32),
        input_output_aliases={3: 0} if given else {},
        compiler_params=params(16),
        name="x_update",
    )(sums, x_image.reshape(flat), direction.reshape(flat), *given)
    return out.reshape(dims)


def direction_kernel(sums_ref, one_ref, two_ref, res_ref, dir_ref, out_ref):
    rows = out_ref.shape[0]
    ratio = (one_ref[0:1, 0:1] + two_ref[0:1, 0:1]) / sums_ref[0:1, 0:1]
    at = pl.ds(pl.program_id(0) * rows, rows)
    out_ref[...] = res_ref[at] + ratio * dir_ref[at]


def direction_update(sums, one, two, residual, direction):
    dims = residual.shape
    flat = (-1,) + dims[2:]
    rows = dims[0] * dims[1]
    steps = 3
    out = pl.pallas_call(
        direction_kernel,
        grid=(steps,),
        in_specs=[resident()] * 5,
        out_specs=pl.BlockSpec((rows // steps,) + dims[2:], lambda i: (i, 0, 0)),
        out_shape=jax.ShapeDtypeStruct((rows,) + dims[2:], F32),
        compiler_params=params(16),
        name="direction_update",
    )(sums, one, two, residual.reshape(flat), direction.reshape(flat))
    return out.reshape(dims)


def row_matrix(info, table_ref, planes, parts):
    pairs, count, _ = info.shape
    half = count // 2
    info = info.reshape(pairs * count, FIELDS)
    depth = table_ref.shape[3]
    hot = lax.broadcasted_iota(jnp.int32, (pairs * count, GX), 1) == info[:, 0:1]
    hot = jnp.where(hot, 1.0, 0.0).astype(BF16)
    live = lax.broadcasted_iota(jnp.int32, (pairs * count, depth), 1) % planes == info[:, 1:2]
    matrix = []
    for part in range(parts):
        sides = [
            jnp.where(live, dot(hot, table_ref[part, side]), 0.0)
            .astype(BF16)
            .reshape(pairs, 2, 1, half, depth)
            for side in range(2)
        ]
        matrix.append(jnp.concatenate(sides, axis=2).reshape(pairs, 2 * count, depth))
    return matrix


def coil_parts(start, planes, sens_ref, dir_ref, out_ref):
    _, coils, rows, _, width = sens_ref.shape
    half = rows * planes
    chunk = max(16 // planes, 1)
    plane = pl.ds(start, planes)
    squares = jnp.zeros((planes, width), F32)
    for index in range(0, rows, chunk):
        at = slice(index, index + chunk)
        to = index * planes
        d_re, d_im = dir_ref[0, at, plane], dir_ref[1, at, plane]
        squares += jnp.sum(d_re * d_re + d_im * d_im, axis=0)
        for coil in range(coils):
            s_re, s_im = sens_ref[0, coil, at, plane], sens_ref[1, coil, at, plane]
            pair = (s_re * d_re - s_im * d_im, s_re * d_im + s_im * d_re)
            for ri, value in enumerate(pair):
                value = value.reshape(chunk * planes, width)
                where = slice(ri * half + to, ri * half + to + chunk * planes)
                for number, part in enumerate(split(value, 3)):
                    out_ref[number, where, coil * width : (coil + 1) * width] = part
    return squares


def rows_kernel(
    planes, slabs_group, steps, me_ref, info_ref, sens_hbm, dir_hbm, table_ref, *refs
):
    pairs, _, count, _ = info_ref.shape
    coils, _, total, width = sens_hbm.shape[1:]
    keep_refs, send_refs = refs[:coils], refs[coils : 2 * coils]
    matrix_ref, norm_ref, one_ref, two_ref, sens_ref, dir_ref, sem = refs[2 * coils :]
    groups = total // planes

    def copies(group):
        at = pl.ds(pl.multiple_of(group * planes, planes), planes)
        return (
            pltpu.make_async_copy(sens_hbm.at[:, :, :, at], sens_ref.at[:, :, :, at], sem.at[group, 0]),
            pltpu.make_async_copy(dir_hbm.at[:, :, at], dir_ref.at[:, :, at], sem.at[group, 1]),
        )

    def start_copies():
        for group in range(groups):
            for copy in copies(group):
                copy.start()

    def wait_copies(group):
        for copy in copies(group):
            copy.wait()

    if steps == 1:
        start_copies()
    else:
        pl.when(pl.program_id(0) == 0)(start_copies)
    info = info_ref[...].reshape(pairs, 2 * count, FIELDS)
    for part, value in enumerate(row_matrix(info, table_ref, planes, 3)):
        matrix_ref[:, part] = value

    def coil_images(group, ref):
        start = pl.multiple_of(group * planes, planes)
        return coil_parts(start, planes, sens_ref, dir_ref, ref)

    def products(pair, image_ref):
        matrix = [matrix_ref[pair, part] for part in range(3)]
        out = six_products(matrix, [image_ref[part] for part in range(3)])
        for coil in range(coils):
            mine = out[:, coil * width : (coil + 1) * width]
            keep_refs[coil][pair] = mine[: 2 * count]
            send_refs[coil][pair] = mine[2 * count :]

    squares = jnp.zeros((planes, width), F32)
    if slabs_group == 2:
        high = me_ref[0] // 2

        def step(index, squares):
            group = 2 * index
            wait_copies(group + 1)
            squares += coil_images(group + 1, two_ref)
            products(lax.bitwise_xor(group, high), one_ref)
            wait_copies(group + 2)
            squares += coil_images(group + 2, one_ref)
            products(lax.bitwise_xor(group + 1, high), two_ref)
            return squares

        wait_copies(0)
        squares = coil_images(0, one_ref)
        squares = lax.fori_loop(0, groups // 2 - 1, step, squares)
        wait_copies(groups - 1)
        squares += coil_images(groups - 1, two_ref)
        products(lax.bitwise_xor(groups - 2, high), one_ref)
        products(lax.bitwise_xor(groups - 1, high), two_ref)
    else:
        first = pl.program_id(0) * pairs

        @pl.when(first == 0)
        def _():
            for group in range(groups):
                wait_copies(group)

        group = lax.bitwise_xor(2 * first, me_ref[0]) // slabs_group
        fresh = coil_images(group, one_ref)
        squares = jnp.where(2 * first % slabs_group == 0, fresh, 0.0)
        for pair in range(pairs):
            products(pair, one_ref)
    amount = DAMPING * jnp.sum(squares, keepdims=True)
    at = lax.broadcasted_iota(jnp.int32, norm_ref.shape, 0)
    amount = jnp.where(at == 0, 0.0, amount)
    if steps == 1:
        norm_ref[...] = amount
    else:

        @pl.when(pl.program_id(0) == 0)
        def _():
            norm_ref[...] = jnp.zeros(norm_ref.shape, F32)

        norm_ref[...] += amount


def partial_rows(me, info, sens, direction, table, planes, slabs_group):
    pairs, _, count, _ = info.shape
    _, coils, rows, total, width = sens.shape
    depth = 2 * rows * planes
    step = min(pairs, 512 // (2 * count))
    steps = pairs // step
    shape = (2 * count, width)
    kept = jax.ShapeDtypeStruct((pairs,) + shape, F32)
    kept_block = blocks((step,) + shape, lambda i: (i, 0, 0), steps)
    shape = (3, 4 * count, depth)
    *values, matrix, norm = pl.pallas_call(
        lambda *refs: rows_kernel(planes, slabs_group, steps, *refs),
        grid=() if steps == 1 else (steps,),
        in_specs=[
            scalars(),
            blocks((step, 2, count, FIELDS), lambda i: (i, 0, 0, 0), steps),
            in_hbm(),
            in_hbm(),
            resident(),
        ],
        out_specs=[kept_block] * (2 * coils)
        + [
            blocks((step,) + shape, lambda i: (i, 0, 0, 0), steps),
            blocks((8, 128), lambda i: (0, 0), steps),
        ],
        out_shape=[kept] * (2 * coils)
        + [
            jax.ShapeDtypeStruct((pairs,) + shape, BF16),
            jax.ShapeDtypeStruct((8, 128), F32),
        ],
        scratch_shapes=[pltpu.VMEM((3, depth, coils * width), BF16)] * 2
        + [
            pltpu.VMEM(sens.shape, F32),
            pltpu.VMEM(direction.shape, F32),
            pltpu.SemaphoreType.DMA((total // planes, 2)),
        ],
        compiler_params=params(40),
        name="partial_rows",
    )(
        me,
        info,
        pltpu.with_memory_space_constraint(sens, pltpu.HBM),
        pltpu.with_memory_space_constraint(direction, pltpu.HBM),
        table,
    )
    return values[:coils], values[coils:], matrix, norm


def start_turn(info_ref, start_ref):
    chunk, _, count, _ = info_ref.shape
    info = info_ref[:, 0].reshape(chunk * count, FIELDS)
    starts = start_ref.shape[0]
    hot = lax.broadcasted_iota(jnp.int32, (chunk * count, starts), 1) == info[:, 2:3]
    turn = jnp.dot(
        jnp.where(hot, 1.0, 0.0), start_ref[...], precision=HIGHEST, preferred_element_type=F32
    )
    width = turn.shape[1] // 2
    return info, turn[:, :width], turn[:, width:]


def segment_mask(info, cells, segment):
    at = lax.broadcasted_iota(jnp.int32, (info.shape[0], cells), 1)
    return (at >= info[:, 3:4]) & (at < info[:, 3:4] + segment)


def side_of(value, bit):
    step = 2**bit
    return value // step % 2, value // (2 * step) * step + value % step


def cells_kernel(tiles, segment, bit, keep_ref, got_ref, info_ref, start_ref, table_ref, *out_refs):
    pairs, count, width = keep_ref.shape
    count = count // 2
    cells = table_ref.shape[2]
    info, cos, sin = start_turn(info_ref, start_ref)
    both = keep_ref[...] + got_ref[...]
    re = both[:, :count].reshape(pairs * count, width)
    im = both[:, count:].reshape(pairs * count, width)
    re, im = cos * re + sin * im, cos * im - sin * re
    value = [jnp.concatenate([re, im], axis=1), jnp.concatenate([im, -re], axis=1)]
    value = split(jnp.concatenate(value, axis=0), 3)
    out = six_products(value, [table_ref[part] for part in range(3)])
    mask = segment_mask(info, cells, segment)
    for ri in range(2):
        mine = out[ri * pairs * count : (ri + 1) * pairs * count]
        mine = jnp.where(mask, mine, 0.0).reshape(pairs, count // tiles, tiles, cells)
        mine = jnp.sum(mine, axis=1)
        for pair in range(pairs):
            side, place = side_of(pair, bit)
            out_refs[side][place, :, ri * cells : (ri + 1) * cells] = mine[pair]


def row_cells(keep, got, info, start, table, tiles, segment, bit):
    pairs, double, width = keep.shape
    lines = 2 * table.shape[2]
    chunk = pairs if pairs <= 8 else 4
    steps = pairs // chunk
    rows = blocks((chunk, double, width), lambda i: (i, 0, 0), steps)
    half = jax.ShapeDtypeStruct((pairs // 2, tiles, lines), F32)
    return pl.pallas_call(
        lambda *refs: cells_kernel(tiles, segment, bit, *refs),
        grid=() if steps == 1 else (steps,),
        in_specs=[
            rows,
            rows,
            blocks((chunk, 1, double // 2, FIELDS), lambda i: (i, 0, 0, 0), steps),
            resident(),
            resident(),
        ],
        out_specs=[blocks((chunk // 2, tiles, lines), lambda i: (i, 0, 0), steps)] * 2,
        out_shape=[half] * 2,
        compiler_params=params(24),
        name="row_cells",
    )(keep, got, info, start, table)


def adjoint_kernel(segment, bit, had_ref, got_ref, info_ref, start_ref, table_ref, out_ref):
    chunk, _, count, _ = info_ref.shape
    _, tiles, cells = had_ref.shape
    cells = cells // 2
    info, cos, sin = start_turn(info_ref, start_ref)
    mask = segment_mask(info, cells, segment)
    both = []
    for ri in range(2):
        wide = []
        for pair in range(chunk):
            side, place = side_of(pair, bit)
            value = (had_ref, got_ref)[side][place, :, ri * cells : (ri + 1) * cells]
            wide += [value] * (count // tiles)
        both.append(jnp.where(mask, jnp.concatenate(wide, axis=0), 0.0))
    re, im = both
    value = [jnp.concatenate([re, -im], axis=1), jnp.concatenate([im, re], axis=1)]
    high, low = split(jnp.concatenate(value, axis=0), 2)
    first = dot(jnp.concatenate([high, low], axis=0), table_ref[0])
    total, rows = high.shape[0], chunk * count
    out = first[:total] + (first[total:] + dot(high, table_ref[1]))
    re, im = out[:rows], out[rows:]
    out_ref[:, :count] = (cos * re - sin * im).reshape(chunk, count, -1)
    out_ref[:, count:] = (cos * im + sin * re).reshape(chunk, count, -1)


def adjoint_rows(had, got, info, start, table, segment, bit):
    half, tiles, lines = had.shape
    pairs, _, count, _ = info.shape
    width = table.shape[2]
    chunk = pairs if pairs <= 8 else 4
    steps = pairs // chunk
    cells = blocks((chunk // 2, tiles, lines), lambda i: (i, 0, 0), steps)
    return pl.pallas_call(
        lambda *refs: adjoint_kernel(segment, bit, *refs),
        grid=() if steps == 1 else (steps,),
        in_specs=[
            cells,
            cells,
            blocks((chunk, 1, count, FIELDS), lambda i: (i, 0, 0, 0), steps),
            resident(),
            resident(),
        ],
        out_specs=blocks((chunk, 2 * count, width), lambda i: (i, 0, 0), steps),
        out_shape=jax.ShapeDtypeStruct((pairs, 2 * count, width), F32),
        compiler_params=params(24),
        name="adjoint_rows",
    )(had, got, info, start, table)


def tiles_kernel(count_ref, norm_refs, keep_ref, got_ref, weight_ref, out_ref, sums_ref):
    tiles, _, cells = weight_ref.shape
    grid = keep_ref[...] + got_ref[...]
    rows = [grid[:, ri * cells : (ri + 1) * cells] for ri in range(2)]
    found = []
    for tile in range(tiles):
        both = jnp.concatenate([row[tile : tile + 1] for row in rows], axis=0).astype(BF16)
        found.append(
            lax.dot_general(
                both, weight_ref[tile], (((1,), (1,)), ((), ())), preferred_element_type=F32
            )
        )
    spread = []
    for tile in range(tiles):
        live = lax.broadcasted_iota(jnp.int32, found[tile].shape, 1) < count_ref[tile]
        spread.append(dot(jnp.where(live, found[tile], 0.0).astype(BF16), weight_ref[tile]))
    total = 0.0
    for ri, row in enumerate(rows):
        value = jnp.concatenate([piece[ri : ri + 1] for piece in spread], axis=0)
        total = total + row * value
        out_ref[:, ri * cells : (ri + 1) * cells] = value
    total = jnp.sum(total, keepdims=True)
    first = lax.broadcasted_iota(jnp.int32, sums_ref.shape, 0) == 0
    norm = norm_refs[0][...]
    for ref in norm_refs[1:]:
        norm = norm + ref[...]
    sums_ref[...] = norm + jnp.where(first, 0.0, total)


def run_tiles(count, norms, keep, got, weight):
    more = len(norms)
    return pl.pallas_call(
        lambda *refs: tiles_kernel(refs[0], refs[1 : 1 + more], *refs[1 + more :]),
        in_specs=[scalars()] + [resident()] * (more + 3),
        out_specs=[resident()] * 2,
        out_shape=[
            jax.ShapeDtypeStruct(keep.shape, F32),
            jax.ShapeDtypeStruct((8, 128), F32),
        ],
        compiler_params=params(8),
        name="tiles",
    )(count, *norms, keep, got, weight)


def turn_kernel(matrix_ref, out_ref):
    for pair in range(matrix_ref.shape[0]):
        for part in range(2):
            value = matrix_ref[pair, part].astype(F32)
            out_ref[pair, part] = jnp.transpose(value).astype(BF16)


def transposed(matrix):
    pairs, parts, rows, depth = matrix.shape
    step = min(pairs, 8)
    steps = pairs // step
    return pl.pallas_call(
        turn_kernel,
        grid=() if steps == 1 else (steps,),
        in_specs=[blocks((step, parts, rows, depth), lambda q: (q, 0, 0, 0), steps)],
        out_specs=blocks((step, 2, depth, rows), lambda q: (q, 0, 0, 0), steps),
        out_shape=jax.ShapeDtypeStruct((pairs, 2, depth, rows), BF16),
        compiler_params=params(12),
        name="transposed",
    )(matrix)


def back_rows(matrix, rows):
    value = [jnp.concatenate([mine, got], axis=0) for mine, got in zip(rows[::2], rows[1::2])]
    high, low = split(jnp.concatenate(value, axis=1), 2)
    left = jnp.concatenate([matrix[0], matrix[1], matrix[0]], axis=1)
    return dot(left, jnp.concatenate([high, high, low], axis=0))


def combine(back, plane, step, sens_ref, dir_ref, res_ref, out_ref):
    _, coils, rows, _, width = sens_ref.shape
    planes = plane.stop - plane.start
    half = rows * planes
    total = [DAMPING * dir_ref[ri, :, plane].reshape(half, width) for ri in range(2)]
    for coil in range(coils):
        lanes = slice(coil * width, (coil + 1) * width)
        v_re, v_im = back[:half, lanes], back[half:, lanes]
        s_re = sens_ref[0, coil, :, plane].reshape(half, width)
        s_im = sens_ref[1, coil, :, plane].reshape(half, width)
        total[0] += s_re * v_re + s_im * v_im
        total[1] += s_re * v_im - s_im * v_re
    squares = 0.0
    for ri in range(2):
        value = res_ref[ri, :, plane].reshape(half, width) - step * total[ri]
        value = value.reshape(rows, planes, width)
        out_ref[ri, :, plane] = value
        squares = squares + jnp.sum(value * value, axis=0)
    return squares


def finish_kernel(planes, me_ref, sums_ref, sens_ref, dir_ref, res_ref, matrix_ref, *refs):
    coils, rows, total, width = sens_ref.shape[1:]
    row_refs = refs[: 2 * coils]
    out_hbm, out_ref, norm_ref, sem = refs[2 * coils :]
    step = sums_ref[0:1, 0:1] / sums_ref[1:2, 0:1]
    squares = jnp.zeros((planes, width), F32)
    copies = []
    for group in range(total // planes):
        pair = lax.bitwise_xor(group, me_ref[0] // 2)
        back = back_rows(
            [matrix_ref[pair, part] for part in range(2)], [ref[pair] for ref in row_refs]
        )
        plane = slice(group * planes, (group + 1) * planes)
        squares += combine(back, plane, step, sens_ref, dir_ref, res_ref, out_ref)
        at = pl.ds(group * planes, planes)
        copies.append(
            pltpu.make_async_copy(out_ref.at[:, :, at], out_hbm.at[:, :, at], sem.at[group])
        )
        copies[-1].start()
    for copy in copies:
        copy.wait()
    norm_ref[...] = jnp.broadcast_to(jnp.sum(squares, keepdims=True), norm_ref.shape)


def finish(me, sums, rows, sens, direction, residual, matrix, planes):
    kept = jax.ShapeDtypeStruct(residual.shape, F32)
    return pl.pallas_call(
        lambda *refs: finish_kernel(planes, *refs),
        in_specs=[scalars()] + [resident()] * (5 + len(rows)),
        out_specs=[in_hbm(), resident(), resident()],
        out_shape=[kept, kept, jax.ShapeDtypeStruct(sums.shape, F32)],
        scratch_shapes=[pltpu.SemaphoreType.DMA((residual.shape[2] // planes,))],
        compiler_params=params(16),
        name="finish",
    )(me, sums, sens, direction, residual, matrix, *rows)


def finish_deep_kernel(planes, me_ref, sums_ref, sens_ref, dir_ref, res_ref, matrix_ref, *refs):
    coils = sens_ref.shape[1]
    row_refs = refs[: 2 * coils]
    out_ref, norm_ref, squares_ref, sum_ref = refs[2 * coils :]
    group, pair = pl.program_id(0), pl.program_id(1)
    back = back_rows([matrix_ref[0, part] for part in range(2)], [ref[0] for ref in row_refs])

    @pl.when((group == 0) & (pair == 0))
    def _():
        squares_ref[...] = jnp.zeros(squares_ref.shape, F32)

    @pl.when(pair == 0)
    def _():
        sum_ref[...] = back

    @pl.when(pair > 0)
    def _():
        sum_ref[...] += back

    @pl.when(pair == pl.num_programs(1) - 1)
    def _():
        step = sums_ref[0:1, 0:1] / sums_ref[1:2, 0:1]
        squares_ref[...] += combine(
            sum_ref[...], slice(0, planes), step, sens_ref, dir_ref, res_ref, out_ref
        )
        total = jnp.sum(squares_ref[...], keepdims=True)
        norm_ref[...] = jnp.broadcast_to(total, norm_ref.shape)


def finish_deep(me, sums, rows, sens, direction, residual, matrix, planes, slabs_group):
    _, coils, height, total, width = sens.shape
    double = rows[0].shape[1]
    groups, deep = total // planes, slabs_group // 2

    def pair(i, j, me):
        return lax.bitwise_xor(i, me[0] // slabs_group) * deep + j

    row_block = pl.BlockSpec((1, double, width), lambda i, j, me: (pair(i, j, me), 0, 0))
    image = pl.BlockSpec((2, height, planes, width), lambda i, j, me: (0, 0, i, 0))
    small = pl.BlockSpec(sums.shape, lambda i, j, me: (0, 0))
    out, norm = pl.pallas_call(
        lambda *refs: finish_deep_kernel(planes, *refs),
        grid_spec=pltpu.PrefetchScalarGridSpec(
            num_scalar_prefetch=1,
            grid=(groups, deep),
            in_specs=[
                small,
                pl.BlockSpec(
                    (2, coils, height, planes, width), lambda i, j, me: (0, 0, 0, i, 0)
                ),
                image,
                image,
                pl.BlockSpec((1,) + matrix.shape[1:], lambda i, j, me: (pair(i, j, me), 0, 0, 0)),
            ]
            + [row_block] * len(rows),
            out_specs=[image, small],
            scratch_shapes=[
                pltpu.VMEM((planes, width), F32),
                pltpu.VMEM((2 * height * planes, coils * width), F32),
            ],
        ),
        out_shape=[
            jax.ShapeDtypeStruct(residual.shape, F32),
            jax.ShapeDtypeStruct(sums.shape, F32),
        ],
        compiler_params=params(32),
        name="finish_deep",
    )(me, sums, sens, direction, residual, matrix, *rows)
    return out, out, norm


def swap(value, bit, slabs):
    return lax.ppermute(value, "slab", [(i, i ^ bit) for i in range(slabs)])


def sum_scatter(keep, send, bits, slabs):
    dims = keep.shape[1:]
    left = sorted(bits, reverse=True)
    for number, bit in enumerate(bits):
        axis = left.index(bit)
        left.pop(axis)
        if number > 0:
            value = (keep + got).reshape((2,) * (len(left) + 1) + dims)
            keep = lax.index_in_dim(value, 0, axis, keepdims=False)
            send = lax.index_in_dim(value, 1, axis, keepdims=False)
        got = swap(send, bit, slabs)
    return keep, got


def gather(value, bits, slabs):
    have = []
    for bit in bits:
        other = swap(value, bit, slabs)
        value = jnp.stack([value, other], axis=sum(1 for b in have if b > bit))
        have.append(bit)
    return value


def body(x_image, residual, direction, sensitivity, tile_block, tile_count, tile_weight):
    _, coils, rows, plane_count, ny = sensitivity.shape
    tiles, _, cells = tile_weight.shape
    slabs = lax.axis_size("slab")
    me = lax.axis_index("slab")
    lines = plane_count * GY // slabs
    segment = min(lines, GY)
    per_gx = lines // segment
    unit = math.gcd(cells, segment)
    segments = -(-(segment - unit + cells) // segment)
    planes = 8 if rows % 2 == 0 else 16
    slabs_group = planes * GY // lines
    pairs = slabs // 2
    bits = [1 << i for i in range(slabs.bit_length() - 1)]

    first = tile_block * cells
    start = first % segment
    base = (me * lines) % GY
    info = []
    for k in range(segments):
        row = jnp.minimum(first // segment + k, GX * per_gx - 1)
        plane = (me * lines + (row % per_gx) * segment) // GY
        turn = (base + start - segment * k) % GY // unit
        fields = [row // per_gx, plane % planes, turn, segment * k - start]
        info.append(jnp.stack(fields + [jnp.zeros_like(row)] * (FIELDS - len(fields)), axis=1))
    info = jnp.concatenate(info, axis=0)

    norms, have = [], []
    for number, bit in enumerate(reversed(bits)):
        other = swap(info, bit, slabs)
        if number == 0:
            norms.append(squares(residual))
        info = jnp.stack([info, other], axis=sum(1 for b in have if b > bit))
        have.append(bit)
        info, *norms = lax.optimization_barrier((info, *norms))
    info = info.reshape(pairs, 2, segments * tiles, FIELDS)

    x_cos, x_sin = dft(np.arange(GX), np.repeat(np.arange(rows), planes), GX)
    angle = (jnp.arange(GX, dtype=jnp.int32) * (me * rows) % GX).astype(F32) * (2 * math.pi / GX)
    turn_cos, turn_sin = jnp.cos(angle)[:, None], jnp.sin(angle)[:, None]
    x_upper = jnp.asarray(np.hstack([x_cos, x_sin]).astype(np.float32))
    x_lower = jnp.asarray(np.hstack([-x_sin, x_cos]).astype(np.float32))
    x_table = jnp.stack(
        [x_upper * turn_cos + x_lower * turn_sin, x_lower * turn_cos - x_upper * turn_sin]
    )
    x_parts = []
    for _ in range(3):
        part = lax.reduce_precision(x_table, 8, 7)
        x_parts.append(part.astype(BF16))
        x_table = x_table - part
    x_table = jnp.stack(x_parts)
    y_cos, y_sin = dft(np.arange(ny), np.arange(cells), GY)
    y_forward = jnp.asarray(table_parts(np.vstack([y_cos, y_sin]), 3))
    y_back = jnp.asarray(table_parts(np.vstack([y_cos.T, y_sin.T]), 2))
    start_table = np.hstack(dft(np.arange(GY // unit) * unit, np.arange(ny), GY, False))
    start_table = np.pad(start_table, ((0, -start_table.shape[0] % 8), (0, 0)))
    start_table = jnp.asarray(start_table.astype(np.float32))
    me_array = me.astype(jnp.int32)[None]

    keep, send, x_matrix, norm = partial_rows(
        me_array, info, sensitivity, direction, x_table, planes, slabs_group
    )
    norms.append(norm)
    got = [swap(value, 1, slabs) for value in send]
    grid = [
        row_cells(keep[c], got[c], info, start_table, y_forward, tiles, segment, c % 2)
        for c in range(coils)
    ]
    grid[-1], x_matrix = lax.optimization_barrier((grid[-1], x_matrix))
    x_matrix = transposed(x_matrix)
    high_bits = bits[1:]
    orders = [high_bits[c % 2 :] + high_bits[: c % 2] for c in range(coils)]
    grid = [sum_scatter(*value, order, slabs) for value, order in zip(grid, orders)]
    grid[-1], x_matrix = lax.optimization_barrier((grid[-1], x_matrix))

    rows_back, loaded = [], []
    for c, order in enumerate(orders):
        spread, sums = run_tiles(tile_count, norms, *grid[c], tile_weight)
        norms = [sums]
        dims = spread.shape
        have = []
        for number, bit in enumerate(order[::-1]):
            if c == coils - 1:
                sums = sums + swap(sums, high_bits[-1 - number], slabs)
            other = swap(spread, bit, slabs)
            if c == coils - 1 and number < 3:
                loaded.append(load((sensitivity, direction, residual)[number]))
            if bit != order[0]:
                spread = jnp.stack([spread, other], axis=sum(1 for b in have if b > bit))
                have.append(bit)
                if c == coils - 1:
                    sums, spread, sensitivity, direction, residual, *loaded = lax.optimization_barrier(
                        (sums, spread, sensitivity, direction, residual, *loaded)
                    )
        spread, other = spread.reshape((-1,) + dims), other.reshape((-1,) + dims)
        if c == coils - 1:
            sums, spread, other, *loaded = lax.optimization_barrier((sums, spread, other, *loaded))
        mine = adjoint_rows(spread, other, info, start_table, y_back, segment, c % 2)
        rows_back += [mine, swap(mine, 1, slabs)]
    sums = sums + swap(sums, 1, slabs)
    sens, move, residual = loaded
    if slabs_group == 2:
        residual_next, res, norm = finish(
            me_array, sums, rows_back, sens, move, residual, x_matrix, planes
        )
    else:
        residual_next, res, norm = finish_deep(
            me_array, sums, rows_back, sens, move, residual, x_matrix, planes, slabs_group
        )

    pieces = 3
    x_next = None
    for number, bit in enumerate(reversed(bits)):
        norm, x_image = lax.optimization_barrier((norm, x_image))
        other = swap(norm, bit, slabs)
        if number < pieces:
            x_next = x_update(sums, x_image, move, number, pieces, x_next)
            x_next, x_image = lax.optimization_barrier((x_next, x_image))
        if bit > 1:
            norm, x_next = lax.optimization_barrier((norm + other, x_next))
    direction_next = direction_update(sums, norm, other, res, move)
    return (x_next, residual_next, direction_next)


def solution(mesh):
    image = P(None, "slab", "frames", None)
    placed = (image, image, image, P(None, None, "slab", None, None)) + (
        P("slab"),
        P("slab"),
        P("slab", None, None),
    )
    return jax.shard_map(
        body, mesh=mesh, in_specs=placed, out_specs=(image, image, image), check_vma=False
    )
```

time: 137 us -> 115 us (0.84)
  Pallas kernels: 60.5 us -> 49.5 us
  waiting for transfers between devices: 32.6 us -> 29.2 us
  starting transfers between devices: 33.2 us -> 29.9 us
  other arithmetic: 5.34 us -> 2.06 us
    pallas_call x12 -> x17, Pallas kernels: 60.5 us -> 49.5 us  [the longest x1 11.2 us: partial_rows(): pl.pallas_call(lambda *refs: rows_kernel(planes, slabs_group, steps, *ref...]
    ppermute x26 -> x28, starting transfers between devices: 33.2 us -> 29.9 us  [swap(): return lax.ppermute(value, 'slab', [(i, i ^ bit) for i in range(slabs)])]
    ppermute x26 -> x28, waiting for transfers between devices: 32.6 us -> 29.2 us  [swap(): return lax.ppermute(value, 'slab', [(i, i ^ bit) for i in range(slabs)])]
    unnamed x34 -> x20, local copies, waits for them, and re-layouts: 3.54 us -> 2.62 us
  transfers between devices with their start and end apart: 26 -> 28, of which waited for: 14 -> 17; matrix products, arithmetic and copies ran while one was open for 3% -> 1% of each run, Pallas kernels for 10% -> 26%
where the time goes in v3:
time: 115 us
  Pallas kernels  49.5 us (43%)
  starting transfers between devices  29.9 us (26%)
  waiting for transfers between devices  29.2 us (25%)
  local copies, waits for them, and re-layouts  2.86 us (2%)
  other arithmetic  2.06 us (2%)
    ppermute x28, starting transfers between devices, swap(): return lax.ppermute(value, 'slab', [(i, i ^ bit) for i in range(slabs)])  29.9 us
    ppermute x28, waiting for transfers between devices, swap(): return lax.ppermute(value, 'slab', [(i, i ^ bit) for i in range(slabs)])  29.2 us
    pallas_call x1, Pallas kernels, partial_rows(): pl.pallas_call(lambda *refs: rows_kernel(planes, slabs_group, steps, *ref...  11.2 us
    pallas_call x3, Pallas kernels, load(): pl.pallas_call(load_kernel, in_specs=[in_hbm()], out_specs=resident(), ou...  8.7 us
    pallas_call x2, Pallas kernels, row_cells(): pl.pallas_call(lambda *refs: cells_kernel(tiles, segment, bit, *refs), gr...  7.65 us
    pallas_call x1, Pallas kernels, finish(): pl.pallas_call(lambda *refs: finish_kernel(planes, *refs), in_specs=[scal...  5.65 us
    pallas_call x2, Pallas kernels, adjoint_rows(): pl.pallas_call(lambda *refs: adjoint_kernel(segment, bit, *refs), grid=()...  5.27 us
    pallas_call x3, Pallas kernels, x_update(): pl.pallas_call(lambda *refs: x_kernel(piece * rows, *refs), grid=(2,), in...  3.85 us
  transfers between devices with their start and end apart: 28, of which 17 were waited for; matrix products, arithmetic and copies ran while one was open for 1% of the time, Pallas kernels for 26%

profile of v3, /device:TPU:0, one launch (start us, length us, event | category | flops | bytes accessed | tf_op | source)
XLA Modules:
  0.0 114.6 jit_solution(9884972017232302476)
XLA Ops:
  1.6 4.0 %collective-permute-start = (s32[32,8]{0,1:T(8,128)S(1)}, s32[32,8]{0,1:T(8,128)S(1)}, u32[]{:S(2)}, u32[]{:S(2)}) collective-permute-start(s32[32,8]{0,1:T(8,128)S(1)} %pad_add_fusion.4), channel_id=1, source_target_pairs={{0,8},{1,9},{2,10},{3,11},{4,12},{5,13},{6,14},{7,15},{8,0},{9,1},... | collective-permute-start | bytes 3080 | tf_op jit(solution)/shard_map/ppermute | solution.py:683
  5.7 2.3 %copy-done = f32[2,24,64,384]{3,2,1,0:T(8,128)S(1)} copy-done((f32[2,24,64,384]{3,2,1,0:T(8,128)S(1)}, f32[2,24,64,384]{3,2,1,0:T(8,128)}, u32[]{:S(2)}) %copy-start) | copy-done | bytes 4718616
  8.7 1.6 %collective-permute-start.1 = (s32[2,32,8]{1,2,0:T(8,128)S(1)}, s32[2,32,8]{1,2,0:T(8,128)S(1)}, u32[]{:S(2)}, u32[]{:S(2)}) collective-permute-start(s32[2,32,8]{1,2,0:T(8,128)S(1)} %pad_add_fusion.3), channel_id=1, source_target_pairs={{0,4},{1,5},{2,6},{3,7},{4,0},{5,1},{6,2},{7,3},{8,12},{9,13},{10,... | collective-permute-start | bytes 6152 | tf_op jit(solution)/shard_map/ppermute | solution.py:683
  10.6 1.8 %collective-permute-done.1 = s32[2,32,8]{1,2,0:T(8,128)S(1)} collective-permute-done((s32[2,32,8]{1,2,0:T(8,128)S(1)}, s32[2,32,8]{1,2,0:T(8,128)S(1)}, u32[]{:S(2)}, u32[]{:S(2)}) %collective-permute-start.1) | collective-permute-done | bytes 2080 | tf_op jit(solution)/shard_map/ppermute | solution.py:683
  14.3 1.8 %collective-permute-done.2 = s32[2,2,32,8]{2,3,1,0:T(8,128)S(1)} collective-permute-done((s32[2,2,32,8]{2,3,1,0:T(8,128)S(1)}, s32[2,2,32,8]{2,3,1,0:T(8,128)S(1)}, u32[]{:S(2)}, u32[]{:S(2)}) %collective-permute-start.2) | collective-permute-done | bytes 4128 | tf_op jit(solution)/shard_map/ppermute | solution.py:683
  17.5 11.2 %partial_rows.1 = (f32[8,64,384]{2,1,0:T(8,128)S(1)}, f32[8,64,384]{2,1,0:T(8,128)S(1)}, f32[8,64,384]{2,1,0:T(8,128)S(1)}, f32[8,64,384]{2,1,0:T(8,128)S(1)}, b...) custom-call(s32[1]{0:T(128)} %bitcast.refs_0_, s32[8,2,32,8]{3,2,1,0:T(8,128)S(1)} %bitcast.98, ...), custom_call_target="tpu_custom_call" | custom-call | tf_op jit(solution)/shard_map/partial_rows/pallas_call | solution.py:325
  29.3 1.8 %collective-permute-done.4.refs_1_ = f32[8,64,384]{2,1,0:T(8,128)S(1)} collective-permute-done((f32[8,64,384]{2,1,0:T(8,128)S(1)}, f32[8,64,384]{2,1,0:T(8,128)S(1)}, u32[]{:S(2)}, u32[]{:S(2)}) %collective-permute-start.4) | collective-permute-done | bytes 786464 | tf_op jit(solution)/shard_map/ppermute | solution.py:683
  31.1 3.8 %row_cells.2 = (f32[4,16,1024]{2,1,0:T(8,128)S(1)}, f32[4,16,1024]{2,1,0:T(8,128)S(1)}) custom-call(f32[8,64,384]{2,1,0:T(8,128)S(1)} %get-tuple-element.76.refs_0_, f32[8,64,384]{2,1,0:T(8,128)S(1)} %collective-permute-done.4.refs_1_, s32[8,2,32,8]{3,2,1,0:T(8,128)S(1)} %bitcast.99, f32[16,768]{1,0:T(8,128)S(1)} %copy-done.4, bf16[3,768,512]{2,1,0:T(8,128)(2,1)S(1)} %copy-done.1), custom_call_target="tpu_custom_call" | custom-call | tf_op jit(solution)/shard_map/row_cells/pallas_call | solution.py:414
  36.5 3.8 %row_cells.3 = (f32[4,16,1024]{2,1,0:T(8,128)S(1)}, f32[4,16,1024]{2,1,0:T(8,128)S(1)}) custom-call(f32[8,64,384]{2,1,0:T(8,128)S(1)} %get-tuple-element.81.refs_0_, f32[8,64,384]{2,1,0:T(8,128)S(1)} %collective-permute-done.8.refs_1_, s32[8,2,32,8]{3,2,1,0:T(8,128)S(1)} %bitcast.100, f32[16,768]{1,0:T(8,128)S(1)} %copy-done.4, ...), custom_call_target="tpu_custom_call" | custom-call | tf_op jit(solution)/shard_map/row_cells/pallas_call | solution.py:414
  40.4 1.6 %collective-permute-start.9 = (f32[4,16,1024]{2,1,0:T(8,128)S(1)}, f32[4,16,1024]{2,1,0:T(8,128)S(1)}, u32[]{:S(2)}, u32[]{:S(2)}) collective-permute-start(f32[4,16,1024]{2,1,0:T(8,128)S(1)} %get-tuple-element.87), channel_id=1, source_target_pairs={{0,4},{1,5},{2,6},{3,7},{4,0},{5,1},{6,2},{7,3},{8,12},{9,13},{10,... | collective-permute-start | bytes 786440 | tf_op jit(solution)/shard_map/ppermute | solution.py:683
  43.4 1.6 %collective-permute-start.6 = (f32[2,16,1024]{2,1,0:T(8,128)S(1)}, f32[2,16,1024]{2,1,0:T(8,128)S(1)}, u32[]{:S(2)}, u32[]{:S(2)}) collective-permute-start(f32[2,16,1024]{2,1,0:T(8,128)S(1)} %slice_bitcast_fusion), channel_id=1, source_target_pairs={{0,4},{1,5},{2,6},{3,7},{4,0},{5,1},{6,2},{7,3},{8,12},{9,13},{10,... | collective-permute-start | bytes 393224 | tf_op jit(solution)/shard_map/ppermute | solution.py:683
  45.1 4.6 %collective-permute-done.9 = f32[4,16,1024]{2,1,0:T(8,128)S(1)} collective-permute-done((f32[4,16,1024]{2,1,0:T(8,128)S(1)}, f32[4,16,1024]{2,1,0:T(8,128)S(1)}, u32[]{:S(2)}, u32[]{:S(2)}) %collective-permute-start.9) | collective-permute-done | bytes 262176 | tf_op jit(solution)/shard_map/ppermute | solution.py:683
  52.8 6.1 %collective-permute-done.10 = f32[2,16,1024]{2,1,0:T(8,128)S(1)} collective-permute-done((f32[2,16,1024]{2,1,0:T(8,128)S(1)}, f32[2,16,1024]{2,1,0:T(8,128)S(1)}, u32[]{:S(2)}, u32[]{:S(2)}) %collective-permute-start.10) | collective-permute-done | bytes 131104 | tf_op jit(solution)/shard_map/ppermute | solution.py:683
  68.5 3.8 %load.3 = f32[4,24,64,384]{3,2,1,0:T(8,128)S(1)} custom-call(f32[4,24,64,384]{3,2,1,0:T(8,128)} %bitcast.111), custom_call_target="tpu_custom_call" | custom-call | tf_op jit(solution)/shard_map/load/pallas_call | solution.py:94
  72.3 2.4 %collective-permute-start.15 = (f32[2,16,1024]{2,1,0:T(8,128)S(1)}, f32[2,16,1024]{2,1,0:T(8,128)S(1)}, u32[]{:S(2)}, u32[]{:S(2)}) collective-permute-start(f32[2,16,1024]{2,1,0:T(8,128)S(1)} %pad_maximum_fusion.4), channel_id=1, source_target_pairs={{0,8},{1,9},{2,10},{3,11},{4,12},{5,13},{6,14},{7,15},{8,0},{9,1},... | collective-permute-start | bytes 393224 | tf_op jit(solution)/shard_map/ppermute | solution.py:683
  74.8 2.4 %load.4.refs_3_ = f32[2,24,64,384]{3,2,1,0:T(8,128)S(1)} custom-call(f32[2,24,64,384]{3,2,1,0:T(8,128)} %from_hbm), custom_call_target="tpu_custom_call" | custom-call | tf_op jit(solution)/shard_map/load/pallas_call | solution.py:94
  79.3 1.8 %collective-permute-start.17 = (f32[2,2,16,1024]{3,2,1,0:T(8,128)S(1)}, f32[2,2,16,1024]{3,2,1,0:T(8,128)S(1)}, u32[]{:S(2)}, u32[]{:S(2)}) collective-permute-start(f32[2,2,16,1024]{3,2,1,0:T(8,128)S(1)} %pad_maximum_fusion.2), channel_id=1, source_target_pairs={{0,4},{1,5},{2,6},{3,7},{4,0},{5,1},{6,2},{7,3},{8,12},{9,13},{10,... | collective-permute-start | bytes 786440 | tf_op jit(solution)/shard_map/ppermute | solution.py:683
  82.4 2.5 %load.5.refs_4_ = f32[2,24,64,384]{3,2,1,0:T(8,128)S(1)} custom-call(f32[2,24,64,384]{3,2,1,0:T(8,128)} %from_hbm.1), custom_call_target="tpu_custom_call" | custom-call | tf_op jit(solution)/shard_map/load/pallas_call | solution.py:94
  85.2 2.5 %adjoint_rows.2.refs_6_ = f32[8,64,384]{2,1,0:T(8,128)S(1)} custom-call(f32[4,16,1024]{2,1,0:T(8,128)S(1)} %bitcast.105, f32[4,16,1024]{2,1,0:T(8,128)S(1)} %bitcast.106, s32[8,2,32,8]{3,2,1,0:T(8,128)S(1)} %bitcast.101, f32[16,768]{1,0:T(8,128)S(1)} %copy-done.4, bf16[2,1024,384]{2,1,0:T(8,128)(2,1)S(1)} %copy-done.3), custom_call_target="tpu_custom_call" | custom-call | tf_op jit(solution)/shard_map/adjoint_rows/pallas_call | solution.py:463
  87.8 2.8 %adjoint_rows.3.refs_8_ = f32[8,64,384]{2,1,0:T(8,128)S(1)} custom-call(f32[4,16,1024]{2,1,0:T(8,128)S(1)} %bitcast.104, f32[4,16,1024]{2,1,0:T(8,128)S(1)} %bitcast.107, s32[8,2,32,8]{3,2,1,0:T(8,128)S(1)} %bitcast.102, f32[16,768]{1,0:T(8,128)S(1)} %copy-done.4, bf16[2,1024,384]{2,1,0:T(8,128)(2,1)S(1)} %copy-done.3), custom_call_target="tpu_custom_call" | custom-call | tf_op jit(solution)/shard_map/adjoint_rows/pallas_call | solution.py:463
  91.2 1.8 %collective-permute-done.18 = f32[8,128]{1,0:T(8,128)S(1)} collective-permute-done((f32[8,128]{1,0:T(8,128)S(1)}, f32[8,128]{1,0:T(8,128)S(1)}, u32[]{:S(2)}, u32[]{:S(2)}) %collective-permute-start.18) | collective-permute-done | bytes 4128 | tf_op jit(solution)/shard_map/ppermute | solution.py:683
  93.1 5.6 %finish.1 = (f32[2,24,64,384]{3,2,1,0:T(8,128)}, f32[2,24,64,384]{3,2,1,0:T(8,128)S(1)}, f32[8,128]{1,0:T(8,128)S(1)}) custom-call(s32[1]{0:T(128)} %bitcast.refs_0_, f32[8,128]{1,0:T(8,128)S(1)} %add.135.refs_1_.refs_0_.sums_ref, f32[2,2,24,64,384]{4,3,2,1,0:T(8,128)S(1)} %bitcast.97, f32[2,24,64,384]{3,2,1,0:T(8,128)S(1)} %load.4.refs_3_, ...), custom_call_target="tpu_custom_call" | custom-call | tf_op jit(solution)/shard_map/finish/pallas_call | solution.py:600
  98.7 2.1 %collective-permute-start.24 = (f32[8,128]{1,0:T(8,128)S(1)}, f32[8,128]{1,0:T(8,128)S(1)}, u32[]{:S(2)}, u32[]{:S(2)}) collective-permute-start(f32[8,128]{1,0:T(8,128)S(1)} %get-tuple-element.112), channel_id=1, source_target_pairs={{0,8},{1,9},{2,10},{3,11},{4,12},{5,13},{6,14},{7,15},{8,0},{9,1},... | collective-permute-start | bytes 12296 | tf_op jit(solution)/shard_map/ppermute | solution.py:683
  111.7 2.9 %direction_update.1 = f32[48,64,384]{2,1,0:T(8,128)} custom-call(f32[8,128]{1,0:T(8,128)S(1)} %add.135.refs_1_.refs_0_.sums_ref, f32[8,128]{1,0:T(8,128)S(1)} %add.138.one_ref, f32[8,128]{1,0:T(8,128)S(1)} %collective-permute-done.27.two_ref, f32[48,64,384]{2,1,0:T(8,128)S(1)} %bitcast.103, f32[48,64,384]{2,1,0:T(8,128)S(1)} %bitcast.91), custom_call_target="tpu_custom_call" | custom-call | tf_op jit(solution)/shard_map/direction_update/pallas_call | solution.py:168
  (108 shorter events, 36.6 us)
Async XLA Ops:
  1.6 7.1 %collective-permute-start = (s32[32,8]{0,1:T(8,128)S(1)}, s32[32,8]{0,1:T(8,128)S(1)}, u32[]{:S(2)}, u32[]{:S(2)}) collective-permute-start(s32[32,8]{0,1:T(8,128)S(1)} %pad_add_fusion.4), channel_id=1, source_target_pairs={{0,8},{1,9},{2,10},{3,11},{4,12},{5,13},{6,14},{7,15},{8,0},{9,1},... | collective-permute-start | bytes 3080 | tf_op jit(solution)/shard_map/ppermute | solution.py:683
  8.7 3.7 %collective-permute-start.1 = (s32[2,32,8]{1,2,0:T(8,128)S(1)}, s32[2,32,8]{1,2,0:T(8,128)S(1)}, u32[]{:S(2)}, u32[]{:S(2)}) collective-permute-start(s32[2,32,8]{1,2,0:T(8,128)S(1)} %pad_add_fusion.3), channel_id=1, source_target_pairs={{0,4},{1,5},{2,6},{3,7},{4,0},{5,1},{6,2},{7,3},{8,12},{9,13},{10,... | collective-permute-start | bytes 6152 | tf_op jit(solution)/shard_map/ppermute | solution.py:683
  12.4 3.7 %collective-permute-start.2 = (s32[2,2,32,8]{2,3,1,0:T(8,128)S(1)}, s32[2,2,32,8]{2,3,1,0:T(8,128)S(1)}, u32[]{:S(2)}, u32[]{:S(2)}) collective-permute-start(s32[2,2,32,8]{2,3,1,0:T(8,128)S(1)} %pad_add_fusion.2), channel_id=1, source_target_pairs={{0,2},{1,3},{2,0},{3,1},{4,6},{5,7},{6,4},{7,5},{8,10},{9,11},{10,... | collective-permute-start | bytes 12296 | tf_op jit(solution)/shard_map/ppermute | solution.py:683
  29.0 7.6 %collective-permute-start.8 = (f32[8,64,384]{2,1,0:T(8,128)S(1)}, f32[8,64,384]{2,1,0:T(8,128)S(1)}, u32[]{:S(2)}, u32[]{:S(2)}) collective-permute-start(f32[8,64,384]{2,1,0:T(8,128)S(1)} %get-tuple-element.82), channel_id=1, source_target_pairs={{0,1},{1,0},{2,3},{3,2},{4,5},{5,4},{6,7},{7,6},{8,9},{9,8},{10,11... | collective-permute-start | bytes 2359304 | tf_op jit(solution)/shard_map/ppermute | solution.py:683
  34.9 8.4 %collective-permute-start.5 = (f32[4,16,1024]{2,1,0:T(8,128)S(1)}, f32[4,16,1024]{2,1,0:T(8,128)S(1)}, u32[]{:S(2)}, u32[]{:S(2)}) collective-permute-start(f32[4,16,1024]{2,1,0:T(8,128)S(1)} %get-tuple-element.79), channel_id=1, source_target_pairs={{0,2},{1,3},{2,0},{3,1},{4,6},{5,7},{6,4},{7,5},{8,10},{9,11},{10,... | collective-permute-start | bytes 786440 | tf_op jit(solution)/shard_map/ppermute | solution.py:683
  40.4 9.3 %collective-permute-start.9 = (f32[4,16,1024]{2,1,0:T(8,128)S(1)}, f32[4,16,1024]{2,1,0:T(8,128)S(1)}, u32[]{:S(2)}, u32[]{:S(2)}) collective-permute-start(f32[4,16,1024]{2,1,0:T(8,128)S(1)} %get-tuple-element.87), channel_id=1, source_target_pairs={{0,4},{1,5},{2,6},{3,7},{4,0},{5,1},{6,2},{7,3},{8,12},{9,13},{10,... | collective-permute-start | bytes 786440 | tf_op jit(solution)/shard_map/ppermute | solution.py:683
  43.4 9.0 %collective-permute-start.6 = (f32[2,16,1024]{2,1,0:T(8,128)S(1)}, f32[2,16,1024]{2,1,0:T(8,128)S(1)}, u32[]{:S(2)}, u32[]{:S(2)}) collective-permute-start(f32[2,16,1024]{2,1,0:T(8,128)S(1)} %slice_bitcast_fusion), channel_id=1, source_target_pairs={{0,4},{1,5},{2,6},{3,7},{4,0},{5,1},{6,2},{7,3},{8,12},{9,13},{10,... | collective-permute-start | bytes 393224 | tf_op jit(solution)/shard_map/ppermute | solution.py:683
  49.7 9.2 %collective-permute-start.10 = (f32[2,16,1024]{2,1,0:T(8,128)S(1)}, f32[2,16,1024]{2,1,0:T(8,128)S(1)}, u32[]{:S(2)}, u32[]{:S(2)}) collective-permute-start(f32[2,16,1024]{2,1,0:T(8,128)S(1)} %slice.39), channel_id=1, source_target_pairs={{0,8},{1,9},{2,10},{3,11},{4,12},{5,13},{6,14},{7,15},{8,0},{9,1},... | collective-permute-start | bytes 393224 | tf_op jit(solution)/shard_map/ppermute | solution.py:683
  52.5 7.2 %collective-permute-start.7 = (f32[16,1024]{1,0:T(8,128)S(1)}, f32[16,1024]{1,0:T(8,128)S(1)}, u32[]{:S(2)}, u32[]{:S(2)}) collective-permute-start(f32[16,1024]{1,0:T(8,128)S(1)} %get-tuple-element.146), channel_id=1, source_target_pairs={{0,8},{1,9},{2,10},{3,11},{4,12},{5,13},{6,14},{7,15},{8,0},{9,1},... | collective-permute-start | bytes 196616 | tf_op jit(solution)/shard_map/ppermute | solution.py:683
  59.0 4.3 %collective-permute-start.11 = (f32[16,1024]{1,0:T(8,128)S(1)}, f32[16,1024]{1,0:T(8,128)S(1)}, u32[]{:S(2)}, u32[]{:S(2)}) collective-permute-start(f32[16,1024]{1,0:T(8,128)S(1)} %get-tuple-element.144), channel_id=1, source_target_pairs={{0,2},{1,3},{2,0},{3,1},{4,6},{5,7},{6,4},{7,5},{8,10},{9,11},{10,... | collective-permute-start | bytes 196616 | tf_op jit(solution)/shard_map/ppermute | solution.py:683
  61.2 6.6 %collective-permute-start.19 = (f32[16,1024]{1,0:T(8,128)S(1)}, f32[16,1024]{1,0:T(8,128)S(1)}, u32[]{:S(2)}, u32[]{:S(2)}) collective-permute-start(f32[16,1024]{1,0:T(8,128)S(1)} %get-tuple-element.108), channel_id=1, source_target_pairs={{0,8},{1,9},{2,10},{3,11},{4,12},{5,13},{6,14},{7,15},{8,0},{9,1},... | collective-permute-start | bytes 196616 | tf_op jit(solution)/shard_map/ppermute | solution.py:683
  64.9 7.4 %collective-permute-start.12 = (f32[8,128]{1,0:T(8,128)S(1)}, f32[8,128]{1,0:T(8,128)S(1)}, u32[]{:S(2)}, u32[]{:S(2)}) collective-permute-start(f32[8,128]{1,0:T(8,128)S(1)} %get-tuple-element.91), channel_id=1, source_target_pairs={{0,8},{1,9},{2,10},{3,11},{4,12},{5,13},{6,14},{7,15},{8,0},{9,1},... | collective-permute-start | bytes 12296 | tf_op jit(solution)/shard_map/ppermute | solution.py:683
  66.4 5.9 %collective-permute-start.13 = (f32[16,1024]{1,0:T(8,128)S(1)}, f32[16,1024]{1,0:T(8,128)S(1)}, u32[]{:S(2)}, u32[]{:S(2)}) collective-permute-start(f32[16,1024]{1,0:T(8,128)S(1)} %get-tuple-element.92), channel_id=1, source_target_pairs={{0,2},{1,3},{2,0},{3,1},{4,6},{5,7},{6,4},{7,5},{8,10},{9,11},{10,... | collective-permute-start | bytes 196616 | tf_op jit(solution)/shard_map/ppermute | solution.py:683
  67.9 10.5 %collective-permute-start.20 = (f32[2,16,1024]{2,1,0:T(8,128)S(1)}, f32[2,16,1024]{2,1,0:T(8,128)S(1)}, u32[]{:S(2)}, u32[]{:S(2)}) collective-permute-start(f32[2,16,1024]{2,1,0:T(8,128)S(1)} %get-tuple-element.143), channel_id=1, source_target_pairs={{0,4},{1,5},{2,6},{3,7},{4,0},{5,1},{6,2},{7,3},{8,12},{9,13},{10,... | collective-permute-start | bytes 393224 | tf_op jit(solution)/shard_map/ppermute | solution.py:683
  72.3 7.0 %collective-permute-start.15 = (f32[2,16,1024]{2,1,0:T(8,128)S(1)}, f32[2,16,1024]{2,1,0:T(8,128)S(1)}, u32[]{:S(2)}, u32[]{:S(2)}) collective-permute-start(f32[2,16,1024]{2,1,0:T(8,128)S(1)} %pad_maximum_fusion.4), channel_id=1, source_target_pairs={{0,8},{1,9},{2,10},{3,11},{4,12},{5,13},{6,14},{7,15},{8,0},{9,1},... | collective-permute-start | bytes 393224 | tf_op jit(solution)/shard_map/ppermute | solution.py:683
  74.8 3.6 %collective-permute-start.14 = (f32[8,128]{1,0:T(8,128)S(1)}, f32[8,128]{1,0:T(8,128)S(1)}, u32[]{:S(2)}, u32[]{:S(2)}) collective-permute-start(f32[8,128]{1,0:T(8,128)S(1)} %add.132), channel_id=1, source_target_pairs={{0,4},{1,5},{2,6},{3,7},{4,0},{5,1},{6,2},{7,3},{8,12},{9,13},{10,... | collective-permute-start | bytes 12296 | tf_op jit(solution)/shard_map/ppermute | solution.py:683
  78.4 6.5 %collective-permute-start.21 = (f32[2,2,16,1024]{3,2,0,1:T(8,128)S(1)}, f32[2,2,16,1024]{3,2,0,1:T(8,128)S(1)}, u32[]{:S(2)}, u32[]{:S(2)}) collective-permute-start(f32[2,2,16,1024]{3,2,0,1:T(8,128)S(1)} %pad_maximum_fusion.3), channel_id=1, source_target_pairs={{0,2},{1,3},{2,0},{3,1},{4,6},{5,7},{6,4},{7,5},{8,10},{9,11},{10,... | collective-permute-start | bytes 786440 | tf_op jit(solution)/shard_map/ppermute | solution.py:683
  79.3 8.5 %collective-permute-start.17 = (f32[2,2,16,1024]{3,2,1,0:T(8,128)S(1)}, f32[2,2,16,1024]{3,2,1,0:T(8,128)S(1)}, u32[]{:S(2)}, u32[]{:S(2)}) collective-permute-start(f32[2,2,16,1024]{3,2,1,0:T(8,128)S(1)} %pad_maximum_fusion.2), channel_id=1, source_target_pairs={{0,4},{1,5},{2,6},{3,7},{4,0},{5,1},{6,2},{7,3},{8,12},{9,13},{10,... | collective-permute-start | bytes 786440 | tf_op jit(solution)/shard_map/ppermute | solution.py:683
  81.1 3.8 %collective-permute-start.16 = (f32[8,128]{1,0:T(8,128)S(1)}, f32[8,128]{1,0:T(8,128)S(1)}, u32[]{:S(2)}, u32[]{:S(2)}) collective-permute-start(f32[8,128]{1,0:T(8,128)S(1)} %add.133), channel_id=1, source_target_pairs={{0,2},{1,3},{2,0},{3,1},{4,6},{5,7},{6,4},{7,5},{8,10},{9,11},{10,... | collective-permute-start | bytes 12296 | tf_op jit(solution)/shard_map/ppermute | solution.py:683
  87.7 5.3 %collective-permute-start.22 = (f32[8,64,384]{2,1,0:T(8,128)S(1)}, f32[8,64,384]{2,1,0:T(8,128)S(1)}, u32[]{:S(2)}, u32[]{:S(2)}) collective-permute-start(f32[8,64,384]{2,1,0:T(8,128)S(1)} %adjoint_rows.2.refs_6_), channel_id=1, source_target_pairs={{0,1},{1,0},{2,3},{3,2},{4,5},{5,4},{6,7},{7,6},{8,9},{9,8},{10,11... | collective-permute-start | bytes 2359304 | tf_op jit(solution)/shard_map/ppermute | solution.py:683
  90.6 2.5 %collective-permute-start.23 = (f32[8,64,384]{2,1,0:T(8,128)S(1)}, f32[8,64,384]{2,1,0:T(8,128)S(1)}, u32[]{:S(2)}, u32[]{:S(2)}) collective-permute-start(f32[8,64,384]{2,1,0:T(8,128)S(1)} %adjoint_rows.3.refs_8_), channel_id=1, source_target_pairs={{0,1},{1,0},{2,3},{3,2},{4,5},{5,4},{6,7},{7,6},{8,9},{9,8},{10,11... | collective-permute-start | bytes 2359304 | tf_op jit(solution)/shard_map/ppermute | solution.py:683
  98.7 4.6 %collective-permute-start.24 = (f32[8,128]{1,0:T(8,128)S(1)}, f32[8,128]{1,0:T(8,128)S(1)}, u32[]{:S(2)}, u32[]{:S(2)}) collective-permute-start(f32[8,128]{1,0:T(8,128)S(1)} %get-tuple-element.112), channel_id=1, source_target_pairs={{0,8},{1,9},{2,10},{3,11},{4,12},{5,13},{6,14},{7,15},{8,0},{9,1},... | collective-permute-start | bytes 12296 | tf_op jit(solution)/shard_map/ppermute | solution.py:683
  103.3 3.6 %collective-permute-start.25 = (f32[8,128]{1,0:T(8,128)S(1)}, f32[8,128]{1,0:T(8,128)S(1)}, u32[]{:S(2)}, u32[]{:S(2)}) collective-permute-start(f32[8,128]{1,0:T(8,128)S(1)} %add.136), channel_id=1, source_target_pairs={{0,4},{1,5},{2,6},{3,7},{4,0},{5,1},{6,2},{7,3},{8,12},{9,13},{10,... | collective-permute-start | bytes 12296 | tf_op jit(solution)/shard_map/ppermute | solution.py:683
  106.9 3.6 %collective-permute-start.26 = (f32[8,128]{1,0:T(8,128)S(1)}, f32[8,128]{1,0:T(8,128)S(1)}, u32[]{:S(2)}, u32[]{:S(2)}) collective-permute-start(f32[8,128]{1,0:T(8,128)S(1)} %add.137), channel_id=1, source_target_pairs={{0,2},{1,3},{2,0},{3,1},{4,6},{5,7},{6,4},{7,5},{8,10},{9,11},{10,... | collective-permute-start | bytes 12296 | tf_op jit(solution)/shard_map/ppermute | solution.py:683
  (14 other events, 97.7 us)

commit v4 on v3

--- a/solution.py
+++ b/solution.py
@@ -153,24 +153,30 @@
     return out.reshape(dims)
 
 
-def direction_kernel(sums_ref, one_ref, two_ref, res_ref, dir_ref, out_ref):
-    rows = out_ref.shape[0]
+def direction_kernel(sums_ref, one_ref, two_ref, res_ref, dir_ref, out_hbm, out_ref, sem):
+    pieces = sem.shape[0]
+    rows = out_ref.shape[0] // pieces
     ratio = (one_ref[0:1, 0:1] + two_ref[0:1, 0:1]) / sums_ref[0:1, 0:1]
-    at = pl.ds(pl.program_id(0) * rows, rows)
-    out_ref[...] = res_ref[at] + ratio * dir_ref[at]
+    copies = []
+    for piece in range(pieces):
+        at = pl.ds(piece * rows, rows)
+        out_ref[at] = res_ref[at] + ratio * dir_ref[at]
+        copies.append(pltpu.make_async_copy(out_ref.at[at], out_hbm.at[at], sem.at[piece]))
+        copies[-1].start()
+    for copy in copies:
+        copy.wait()
 
 
 def direction_update(sums, one, two, residual, direction):
     dims = residual.shape
     flat = (-1,) + dims[2:]
-    rows = dims[0] * dims[1]
-    steps = 3
+    shape = (dims[0] * dims[1],) + dims[2:]
     out = pl.pallas_call(
         direction_kernel,
-        grid=(steps,),
         in_specs=[resident()] * 5,
-        out_specs=pl.BlockSpec((rows // steps,) + dims[2:], lambda i: (i, 0, 0)),
-        out_shape=jax.ShapeDtypeStruct((rows,) + dims[2:], F32),
+        out_specs=in_hbm(),
+        out_shape=jax.ShapeDtypeStruct(shape, F32),
+        scratch_shapes=[pltpu.VMEM(shape, F32), pltpu.SemaphoreType.DMA((6,))],
         compiler_params=params(16),
         name="direction_update",
     )(sums, one, two, residual.reshape(flat), direction.reshape(flat))
@@ -197,25 +203,43 @@
     return matrix
 
 
+def half_turn(value):
+    return pltpu.roll(value, 4, 1)
+
+
+def low_half(shape):
+    return lax.broadcasted_iota(jnp.int32, shape, 1) < 4
+
+
 def coil_parts(start, planes, sens_ref, dir_ref, out_ref):
     _, coils, rows, _, width = sens_ref.shape
-    half = rows * planes
-    chunk = max(16 // planes, 1)
+    sides = out_ref.shape[0]
+    own = planes // sides
+    half = rows * own
+    chunk = max(16 // own, 1)
     plane = pl.ds(start, planes)
     squares = jnp.zeros((planes, width), F32)
     for index in range(0, rows, chunk):
         at = slice(index, index + chunk)
-        to = index * planes
+        to = index * own
         d_re, d_im = dir_ref[0, at, plane], dir_ref[1, at, plane]
         squares += jnp.sum(d_re * d_re + d_im * d_im, axis=0)
         for coil in range(coils):
             s_re, s_im = sens_ref[0, coil, at, plane], sens_ref[1, coil, at, plane]
             pair = (s_re * d_re - s_im * d_im, s_re * d_im + s_im * d_re)
             for ri, value in enumerate(pair):
-                value = value.reshape(chunk * planes, width)
-                where = slice(ri * half + to, ri * half + to + chunk * planes)
-                for number, part in enumerate(split(value, 3)):
-                    out_ref[number, where, coil * width : (coil + 1) * width] = part
+                if sides == 2:
+                    value = value.reshape(chunk // 2, 2, planes, width)
+                    one, two = value[:, 0], value[:, 1]
+                    low = low_half(one.shape)
+                    values = [jnp.where(low, one, half_turn(two)), jnp.where(low, half_turn(one), two)]
+                else:
+                    values = [value]
+                where = slice(ri * half + to, ri * half + to + chunk * own)
+                for side, value in enumerate(values):
+                    value = value.reshape(chunk * own, width)
+                    for number, part in enumerate(split(value, 3)):
+                        out_ref[side, number, where, coil * width : (coil + 1) * width] = part
     return squares
 
 
@@ -249,7 +273,8 @@
     else:
         pl.when(pl.program_id(0) == 0)(start_copies)
     info = info_ref[...].reshape(pairs, 2 * count, FIELDS)
-    for part, value in enumerate(row_matrix(info, table_ref, planes, 3)):
+    own = planes // one_ref.shape[0]
+    for part, value in enumerate(row_matrix(info, table_ref, own, 3)):
         matrix_ref[:, part] = value
 
     def coil_images(group, ref):
@@ -257,12 +282,13 @@
         return coil_parts(start, planes, sens_ref, dir_ref, ref)
 
     def products(pair, image_ref):
-        matrix = [matrix_ref[pair, part] for part in range(3)]
-        out = six_products(matrix, [image_ref[part] for part in range(3)])
-        for coil in range(coils):
-            mine = out[:, coil * width : (coil + 1) * width]
-            keep_refs[coil][pair] = mine[: 2 * count]
-            send_refs[coil][pair] = mine[2 * count :]
+        for side, out_refs in enumerate((keep_refs, send_refs)):
+            rows = slice(2 * side * count, 2 * (side + 1) * count)
+            matrix = [matrix_ref[pair, part, rows] for part in range(3)]
+            slab = lax.rem(me_ref[0] + side, 2) if slabs_group == 2 else 0
+            out = six_products(matrix, [image_ref[slab, part] for part in range(3)])
+            for coil in range(coils):
+                out_refs[coil][pair] = out[:, coil * width : (coil + 1) * width]
 
     squares = jnp.zeros((planes, width), F32)
     if slabs_group == 2:
@@ -315,7 +341,7 @@
 def partial_rows(me, info, sens, direction, table, planes, slabs_group):
     pairs, _, count, _ = info.shape
     _, coils, rows, total, width = sens.shape
-    depth = 2 * rows * planes
+    depth = table.shape[3]
     step = min(pairs, 512 // (2 * count))
     steps = pairs // step
     shape = (2 * count, width)
@@ -342,7 +368,7 @@
             jax.ShapeDtypeStruct((pairs,) + shape, BF16),
             jax.ShapeDtypeStruct((8, 128), F32),
         ],
-        scratch_shapes=[pltpu.VMEM((3, depth, coils * width), BF16)] * 2
+        scratch_shapes=[pltpu.VMEM((2 if slabs_group == 2 else 1, 3, depth, coils * width), BF16)] * 2
         + [
             pltpu.VMEM(sens.shape, F32),
             pltpu.VMEM(direction.shape, F32),
@@ -522,32 +548,48 @@
 
 
 def turn_kernel(matrix_ref, out_ref):
+    sides = out_ref.shape[1]
+    rows = matrix_ref.shape[2] // sides
     for pair in range(matrix_ref.shape[0]):
-        for part in range(2):
-            value = matrix_ref[pair, part].astype(F32)
-            out_ref[pair, part] = jnp.transpose(value).astype(BF16)
-
-
-def transposed(matrix):
+        for side in range(sides):
+            high, low = [
+                matrix_ref[pair, part, side * rows : (side + 1) * rows].astype(F32) for part in range(2)
+            ]
+            value = jnp.concatenate([high, low, high], axis=0)
+            out_ref[pair, side] = jnp.transpose(value).astype(BF16)
+
+
+def transposed(matrix, sides):
     pairs, parts, rows, depth = matrix.shape
     step = min(pairs, 8)
     steps = pairs // step
+    shape = (sides, depth, 3 * rows // sides)
     return pl.pallas_call(
         turn_kernel,
         grid=() if steps == 1 else (steps,),
         in_specs=[blocks((step, parts, rows, depth), lambda q: (q, 0, 0, 0), steps)],
-        out_specs=blocks((step, 2, depth, rows), lambda q: (q, 0, 0, 0), steps),
-        out_shape=jax.ShapeDtypeStruct((pairs, 2, depth, rows), BF16),
+        out_specs=blocks((step,) + shape, lambda q: (q, 0, 0, 0), steps),
+        out_shape=jax.ShapeDtypeStruct((pairs,) + shape, BF16),
         compiler_params=params(12),
         name="transposed",
     )(matrix)
 
 
 def back_rows(matrix, rows):
-    value = [jnp.concatenate([mine, got], axis=0) for mine, got in zip(rows[::2], rows[1::2])]
-    high, low = split(jnp.concatenate(value, axis=1), 2)
-    left = jnp.concatenate([matrix[0], matrix[1], matrix[0]], axis=1)
-    return dot(left, jnp.concatenate([high, high, low], axis=0))
+    high, low = split(rows, 2)
+    return dot(matrix, jnp.concatenate([high, high, low], axis=0))
+
+
+def back_group(odd, matrix, mine, got):
+    first = back_rows(matrix(odd), jnp.where(odd == 0, mine, got))
+    second = back_rows(matrix(1 - odd), jnp.where(odd == 0, got, mine))
+    shape = (first.shape[0] // 8, 8, first.shape[1])
+    first, second = first.reshape(shape), second.reshape(shape)
+    low = low_half(shape)
+    one = jnp.where(low, first, half_turn(second))
+    two = jnp.where(low, half_turn(first), second)
+    value = jnp.concatenate([one[:, None], two[:, None]], axis=1)
+    return value.reshape(16 * shape[0], shape[2])
 
 
 def combine(back, plane, step, sens_ref, dir_ref, res_ref, out_ref):
@@ -579,10 +621,10 @@
     squares = jnp.zeros((planes, width), F32)
     copies = []
     for group in range(total // planes):
-        pair = lax.bitwise_xor(group, me_ref[0] // 2)
-        back = back_rows(
-            [matrix_ref[pair, part] for part in range(2)], [ref[pair] for ref in row_refs]
-        )
+        pair, odd = lax.bitwise_xor(group, me_ref[0] // 2), lax.rem(me_ref[0], 2)
+        mine = jnp.concatenate([ref[pair] for ref in row_refs[::2]], axis=1)
+        got = jnp.concatenate([ref[pair] for ref in row_refs[1::2]], axis=1)
+        back = back_group(odd, lambda side: matrix_ref[pair, side], mine, got)
         plane = slice(group * planes, (group + 1) * planes)
         squares += combine(back, plane, step, sens_ref, dir_ref, res_ref, out_ref)
         at = pl.ds(group * planes, planes)
@@ -613,7 +655,8 @@
     row_refs = refs[: 2 * coils]
     out_ref, norm_ref, squares_ref, sum_ref = refs[2 * coils :]
     group, pair = pl.program_id(0), pl.program_id(1)
-    back = back_rows([matrix_ref[0, part] for part in range(2)], [ref[0] for ref in row_refs])
+    rows = [jnp.concatenate([ref[0] for ref in row_refs[k::2]], axis=1) for k in range(2)]
+    back = back_rows(matrix_ref[0, 0], jnp.concatenate(rows, axis=0))
 
     @pl.when((group == 0) & (pair == 0))
     def _():
@@ -718,6 +761,7 @@
     segments = -(-(segment - unit + cells) // segment)
     planes = 8 if rows % 2 == 0 else 16
     slabs_group = planes * GY // lines
+    own = planes // 2 if slabs_group == 2 else planes
     pairs = slabs // 2
     bits = [1 << i for i in range(slabs.bit_length() - 1)]
 
@@ -729,21 +773,18 @@
         row = jnp.minimum(first // segment + k, GX * per_gx - 1)
         plane = (me * lines + (row % per_gx) * segment) // GY
         turn = (base + start - segment * k) % GY // unit
-        fields = [row // per_gx, plane % planes, turn, segment * k - start]
+        fields = [row // per_gx, plane % own, turn, segment * k - start]
         info.append(jnp.stack(fields + [jnp.zeros_like(row)] * (FIELDS - len(fields)), axis=1))
     info = jnp.concatenate(info, axis=0)
 
-    norms, have = [], []
+    have = []
     for number, bit in enumerate(reversed(bits)):
         other = swap(info, bit, slabs)
-        if number == 0:
-            norms.append(squares(residual))
         info = jnp.stack([info, other], axis=sum(1 for b in have if b > bit))
         have.append(bit)
-        info, *norms = lax.optimization_barrier((info, *norms))
     info = info.reshape(pairs, 2, segments * tiles, FIELDS)
 
-    x_cos, x_sin = dft(np.arange(GX), np.repeat(np.arange(rows), planes), GX)
+    x_cos, x_sin = dft(np.arange(GX), np.repeat(np.arange(rows), own), GX)
     angle = (jnp.arange(GX, dtype=jnp.int32) * (me * rows) % GX).astype(F32) * (2 * math.pi / GX)
     turn_cos, turn_sin = jnp.cos(angle)[:, None], jnp.sin(angle)[:, None]
     x_upper = jnp.asarray(np.hstack([x_cos, x_sin]).astype(np.float32))
@@ -768,18 +809,19 @@
     keep, send, x_matrix, norm = partial_rows(
         me_array, info, sensitivity, direction, x_table, planes, slabs_group
     )
-    norms.append(norm)
     got = [swap(value, 1, slabs) for value in send]
     grid = [
         row_cells(keep[c], got[c], info, start_table, y_forward, tiles, segment, c % 2)
         for c in range(coils)
     ]
-    grid[-1], x_matrix = lax.optimization_barrier((grid[-1], x_matrix))
-    x_matrix = transposed(x_matrix)
+    grid[-1], x_matrix, residual = lax.optimization_barrier((grid[-1], x_matrix, residual))
+    x_matrix = transposed(x_matrix, planes // own)
+    norms = [norm, squares(residual)]
     high_bits = bits[1:]
     orders = [high_bits[c % 2 :] + high_bits[: c % 2] for c in range(coils)]
-    grid = [sum_scatter(*value, order, slabs) for value, order in zip(grid, orders)]
-    grid[-1], x_matrix = lax.optimization_barrier((grid[-1], x_matrix))
+    ways = [high_bits[c % 2 :] + high_bits[: c % 2] for c in range(coils)]
+    grid = [sum_scatter(*value, ways[c % 2], slabs) for c, value in enumerate(grid)]
+    grid[-1], x_matrix, norms = lax.optimization_barrier((grid[-1], x_matrix, norms))
 
     rows_back, loaded = [], []
     for c, order in enumerate(orders):

time: 115 us -> 112 us (0.974)
  starting transfers between devices: 29.9 us -> 35.5 us
  waiting for transfers between devices: 29.2 us -> 24.7 us
  Pallas kernels: 49.5 us -> 46.8 us
  local copies, waits for them, and re-layouts: 2.86 us -> 0.35 us
    ppermute x28, starting transfers between devices: 29.9 us -> 35.5 us  [swap(): return lax.ppermute(value, 'slab', [(i, i ^ bit) for i in range(slabs)])]
    ppermute x28, waiting for transfers between devices: 29.2 us -> 24.7 us  [swap(): return lax.ppermute(value, 'slab', [(i, i ^ bit) for i in range(slabs)])]
    pallas_call x1, Pallas kernels: 11.2 us -> 8.61 us  [partial_rows(): pl.pallas_call(lambda *refs: rows_kernel(planes, slabs_group, steps, *ref...]
    unnamed x20 -> x18, local copies, waits for them, and re-layouts: 2.62 us -> 0.05 us
  transfers between devices with their start and end apart: 28 -> 28, of which waited for: 17 -> 18; matrix products, arithmetic and copies ran while one was open for 1% -> 2% of each run, Pallas kernels for 26% -> 25%
where the time goes in v4:
time: 112 us
  Pallas kernels  46.8 us (42%)
  starting transfers between devices  35.5 us (32%)
  waiting for transfers between devices  24.7 us (22%)
  other arithmetic  3.13 us (3%)
  between operations  1.2 us (1%)
    ppermute x28, starting transfers between devices, swap(): return lax.ppermute(value, 'slab', [(i, i ^ bit) for i in range(slabs)])  35.5 us
    ppermute x28, waiting for transfers between devices, swap(): return lax.ppermute(value, 'slab', [(i, i ^ bit) for i in range(slabs)])  24.7 us
    pallas_call x3, Pallas kernels, load(): pl.pallas_call(load_kernel, in_specs=[in_hbm()], out_specs=resident(), ou...  8.7 us
    pallas_call x1, Pallas kernels, partial_rows(): pl.pallas_call(lambda *refs: rows_kernel(planes, slabs_group, steps, *ref...  8.61 us
    pallas_call x2, Pallas kernels, row_cells(): pl.pallas_call(lambda *refs: cells_kernel(tiles, segment, bit, *refs), gr...  7.69 us
    pallas_call x1, Pallas kernels, finish(): pl.pallas_call(lambda *refs: finish_kernel(planes, *refs), in_specs=[scal...  5.99 us
    pallas_call x2, Pallas kernels, adjoint_rows(): pl.pallas_call(lambda *refs: adjoint_kernel(segment, bit, *refs), grid=()...  5.04 us
    pallas_call x3, Pallas kernels, x_update(): pl.pallas_call(lambda *refs: x_kernel(piece * rows, *refs), grid=(2,), in...  3.85 us
  transfers between devices with their start and end apart: 28, of which 18 were waited for; matrix products, arithmetic and copies ran while one was open for 2% of the time, Pallas kernels for 25%

profile of v4, /device:TPU:0, one launch (start us, length us, event | category | flops | bytes accessed | tf_op | source)
XLA Modules:
  0.0 111.7 jit_solution(10455940034560972982)
XLA Ops:
  1.6 4.0 %collective-permute-start = (s32[32,8]{0,1:T(8,128)S(1)}, s32[32,8]{0,1:T(8,128)S(1)}, u32[]{:S(2)}, u32[]{:S(2)}) collective-permute-start(s32[32,8]{0,1:T(8,128)S(1)} %pad_add_fusion.4), channel_id=1, source_target_pairs={{0,8},{1,9},{2,10},{3,11},{4,12},{5,13},{6,14},{7,15},{8,0},{9,1},... | collective-permute-start | bytes 3080 | tf_op jit(solution)/shard_map/ppermute | solution.py:726
  7.2 1.9 %collective-permute-start.1 = (s32[2,32,8]{1,2,0:T(8,128)S(1)}, s32[2,32,8]{1,2,0:T(8,128)S(1)}, u32[]{:S(2)}, u32[]{:S(2)}) collective-permute-start(s32[2,32,8]{1,2,0:T(8,128)S(1)} %get-tuple-element.141), channel_id=1, source_target_pairs={{0,4},{1,5},{2,6},{3,7},{4,0},{5,1},{6,2},{7,3},{8,12},{9,13},{10,... | collective-permute-start | bytes 6152 | tf_op jit(solution)/shard_map/ppermute | solution.py:726
  10.8 1.8 %collective-permute-start.2 = (s32[2,2,32,8]{2,3,1,0:T(8,128)S(1)}, s32[2,2,32,8]{2,3,1,0:T(8,128)S(1)}, u32[]{:S(2)}, u32[]{:S(2)}) collective-permute-start(s32[2,2,32,8]{2,3,1,0:T(8,128)S(1)} %get-tuple-element.139), channel_id=1, source_target_pairs={{0,2},{1,3},{2,0},{3,1},{4,6},{5,7},{6,4},{7,5},{8,10},{9,11},{10,... | collective-permute-start | bytes 12296 | tf_op jit(solution)/shard_map/ppermute | solution.py:726
  12.9 1.7 %collective-permute-done.2 = s32[2,2,32,8]{2,3,1,0:T(8,128)S(1)} collective-permute-done((s32[2,2,32,8]{2,3,1,0:T(8,128)S(1)}, s32[2,2,32,8]{2,3,1,0:T(8,128)S(1)}, u32[]{:S(2)}, u32[]{:S(2)}) %collective-permute-start.2) | collective-permute-done | bytes 4128 | tf_op jit(solution)/shard_map/ppermute | solution.py:726
  15.9 8.6 %partial_rows.1 = (f32[8,64,384]{2,1,0:T(8,128)S(1)}, f32[8,64,384]{2,1,0:T(8,128)S(1)}, f32[8,64,384]{2,1,0:T(8,128)S(1)}, f32[8,64,384]{2,1,0:T(8,128)S(1)}, b...) custom-call(s32[1]{0:T(128)} %bitcast.refs_0_, s32[8,2,32,8]{3,2,1,0:T(8,128)S(1)} %pad_add_fusion.refs_1_.refs_2_, ...), custom_call_target="tpu_custom_call" | custom-call | tf_op jit(solution)/shard_map/partial_rows/pallas_call | solution.py:351
  25.1 1.8 %collective-permute-done.4.refs_1_ = f32[8,64,384]{2,1,0:T(8,128)S(1)} collective-permute-done((f32[8,64,384]{2,1,0:T(8,128)S(1)}, f32[8,64,384]{2,1,0:T(8,128)S(1)}, u32[]{:S(2)}, u32[]{:S(2)}) %collective-permute-start.4) | collective-permute-done | bytes 786464 | tf_op jit(solution)/shard_map/ppermute | solution.py:726
  26.9 3.9 %row_cells.2 = (f32[4,16,1024]{2,1,0:T(8,128)S(1)}, f32[4,16,1024]{2,1,0:T(8,128)S(1)}) custom-call(f32[8,64,384]{2,1,0:T(8,128)S(1)} %get-tuple-element.62.refs_0_, f32[8,64,384]{2,1,0:T(8,128)S(1)} %collective-permute-done.4.refs_1_, s32[8,2,32,8]{3,2,1,0:T(8,128)S(1)} %pad_add_fusion.refs_1_.refs_2_, f32[16,768]{1,0:T(8,128)S(1)} %copy-done.3, ...), custom_call_target="tpu_custom_call" | custom-call | tf_op jit(solution)/shard_map/row_cells/pallas_call | solution.py:440
  30.8 2.0 %collective-permute-start.5 = (f32[4,16,1024]{2,1,0:T(8,128)S(1)}, f32[4,16,1024]{2,1,0:T(8,128)S(1)}, u32[]{:S(2)}, u32[]{:S(2)}) collective-permute-start(f32[4,16,1024]{2,1,0:T(8,128)S(1)} %get-tuple-element.68), channel_id=1, source_target_pairs={{0,4},{1,5},{2,6},{3,7},{4,0},{5,1},{6,2},{7,3},{8,12},{9,13},{10,... | collective-permute-start | bytes 786440 | tf_op jit(solution)/shard_map/ppermute | solution.py:726
  32.8 3.8 %row_cells.3 = (f32[4,16,1024]{2,1,0:T(8,128)S(1)}, f32[4,16,1024]{2,1,0:T(8,128)S(1)}) custom-call(f32[8,64,384]{2,1,0:T(8,128)S(1)} %get-tuple-element.74.refs_0_, f32[8,64,384]{2,1,0:T(8,128)S(1)} %collective-permute-done.8.refs_1_, s32[8,2,32,8]{3,2,1,0:T(8,128)S(1)} %pad_add_fusion.refs_1_.refs_2_, f32[16,768]{1,0:T(8,128)S(1)} %copy-done.3, ...), custom_call_target="tpu_custom_call" | custom-call | tf_op jit(solution)/shard_map/row_cells/pallas_call | solution.py:440
  39.5 2.8 %collective-permute-start.6 = (f32[2,16,1024]{2,1,0:T(8,128)S(1)}, f32[2,16,1024]{2,1,0:T(8,128)S(1)}, u32[]{:S(2)}, u32[]{:S(2)}) collective-permute-start(f32[2,16,1024]{2,1,0:T(8,128)S(1)} %slice.35), channel_id=1, source_target_pairs={{0,8},{1,9},{2,10},{3,11},{4,12},{5,13},{6,14},{7,15},{8,0},{9,1},... | collective-permute-start | bytes 393224 | tf_op jit(solution)/shard_map/ppermute | solution.py:726
  42.3 2.5 %collective-permute-done.9 = f32[4,16,1024]{2,1,0:T(8,128)S(1)} collective-permute-done((f32[4,16,1024]{2,1,0:T(8,128)S(1)}, f32[4,16,1024]{2,1,0:T(8,128)S(1)}, u32[]{:S(2)}, u32[]{:S(2)}) %collective-permute-start.9) | collective-permute-done | bytes 262176 | tf_op jit(solution)/shard_map/ppermute | solution.py:726
  45.2 3.0 %collective-permute-done.6 = f32[2,16,1024]{2,1,0:T(8,128)S(1)} collective-permute-done((f32[2,16,1024]{2,1,0:T(8,128)S(1)}, f32[2,16,1024]{2,1,0:T(8,128)S(1)}, u32[]{:S(2)}, u32[]{:S(2)}) %collective-permute-start.6) | collective-permute-done | bytes 131104 | tf_op jit(solution)/shard_map/ppermute | solution.py:726
  53.9 3.5 %collective-permute-done.11.refs_4_ = f32[16,1024]{1,0:T(8,128)S(1)} collective-permute-done((f32[16,1024]{1,0:T(8,128)S(1)}, f32[16,1024]{1,0:T(8,128)S(1)}, u32[]{:S(2)}, u32[]{:S(2)}) %collective-permute-start.11) | collective-permute-done | bytes 65568 | tf_op jit(solution)/shard_map/ppermute | solution.py:726
  61.2 2.5 %collective-permute-start.12 = (f32[8,128]{1,0:T(8,128)S(1)}, f32[8,128]{1,0:T(8,128)S(1)}, u32[]{:S(2)}, u32[]{:S(2)}) collective-permute-start(f32[8,128]{1,0:T(8,128)S(1)} %get-tuple-element.81), channel_id=1, source_target_pairs={{0,8},{1,9},{2,10},{3,11},{4,12},{5,13},{6,14},{7,15},{8,0},{9,1},... | collective-permute-start | bytes 12296 | tf_op jit(solution)/shard_map/ppermute | solution.py:726
  65.6 3.8 %load.3 = f32[4,24,64,384]{3,2,1,0:T(8,128)S(1)} custom-call(f32[4,24,64,384]{3,2,1,0:T(8,128)} %bitcast.101), custom_call_target="tpu_custom_call" | custom-call | tf_op jit(solution)/shard_map/load/pallas_call | solution.py:94
  69.4 2.9 %collective-permute-start.15 = (f32[2,16,1024]{2,1,0:T(8,128)S(1)}, f32[2,16,1024]{2,1,0:T(8,128)S(1)}, u32[]{:S(2)}, u32[]{:S(2)}) collective-permute-start(f32[2,16,1024]{2,1,0:T(8,128)S(1)} %pad_maximum_fusion.4), channel_id=1, source_target_pairs={{0,8},{1,9},{2,10},{3,11},{4,12},{5,13},{6,14},{7,15},{8,0},{9,1},... | collective-permute-start | bytes 393224 | tf_op jit(solution)/shard_map/ppermute | solution.py:726
  72.4 2.4 %load.4.refs_3_ = f32[2,24,64,384]{3,2,1,0:T(8,128)S(1)} custom-call(f32[2,24,64,384]{3,2,1,0:T(8,128)} %from_hbm), custom_call_target="tpu_custom_call" | custom-call | tf_op jit(solution)/shard_map/load/pallas_call | solution.py:94
  79.7 2.5 %load.5.refs_4_ = f32[2,24,64,384]{3,2,1,0:T(8,128)S(1)} custom-call(f32[2,24,64,384]{3,2,1,0:T(8,128)} %from_hbm.1), custom_call_target="tpu_custom_call" | custom-call | tf_op jit(solution)/shard_map/load/pallas_call | solution.py:94
  82.5 2.5 %adjoint_rows.2.refs_6_ = f32[8,64,384]{2,1,0:T(8,128)S(1)} custom-call(f32[4,16,1024]{2,1,0:T(8,128)S(1)} %bitcast.95, f32[4,16,1024]{2,1,0:T(8,128)S(1)} %bitcast.96, s32[8,2,32,8]{3,2,1,0:T(8,128)S(1)} %pad_add_fusion.refs_1_.refs_2_, f32[16,768]{1,0:T(8,128)S(1)} %copy-done.3, bf16[2,1024,384]{2,1,0:T(8,128)(2,1)S(1)} %copy-done.2), custom_call_target="tpu_custom_call" | custom-call | tf_op jit(solution)/shard_map/adjoint_rows/pallas_call | solution.py:489
  85.1 2.5 %adjoint_rows.3.refs_8_ = f32[8,64,384]{2,1,0:T(8,128)S(1)} custom-call(f32[4,16,1024]{2,1,0:T(8,128)S(1)} %bitcast.94, f32[4,16,1024]{2,1,0:T(8,128)S(1)} %bitcast.97, s32[8,2,32,8]{3,2,1,0:T(8,128)S(1)} %pad_add_fusion.refs_1_.refs_2_, f32[16,768]{1,0:T(8,128)S(1)} %copy-done.3, bf16[2,1024,384]{2,1,0:T(8,128)(2,1)S(1)} %copy-done.2), custom_call_target="tpu_custom_call" | custom-call | tf_op jit(solution)/shard_map/adjoint_rows/pallas_call | solution.py:489
  88.3 1.8 %collective-permute-done.18 = f32[8,128]{1,0:T(8,128)S(1)} collective-permute-done((f32[8,128]{1,0:T(8,128)S(1)}, f32[8,128]{1,0:T(8,128)S(1)}, u32[]{:S(2)}, u32[]{:S(2)}) %collective-permute-start.18) | collective-permute-done | bytes 4128 | tf_op jit(solution)/shard_map/ppermute | solution.py:726
  90.1 6.0 %finish.1 = (f32[2,24,64,384]{3,2,1,0:T(8,128)}, f32[2,24,64,384]{3,2,1,0:T(8,128)S(1)}, f32[8,128]{1,0:T(8,128)S(1)}) custom-call(s32[1]{0:T(128)} %bitcast.refs_0_, f32[8,128]{1,0:T(8,128)S(1)} %add.135.refs_1_.refs_0_.sums_ref, f32[2,2,24,64,384]{4,3,2,1,0:T(8,128)S(1)} %bitcast.90, f32[2,24,64,384]{3,2,1,0:T(8,128)S(1)} %load.4.refs_3_, ...), custom_call_target="tpu_custom_call" | custom-call | tf_op jit(solution)/shard_map/finish/pallas_call | solution.py:642
  96.1 2.4 %collective-permute-start.24 = (f32[8,128]{1,0:T(8,128)S(1)}, f32[8,128]{1,0:T(8,128)S(1)}, u32[]{:S(2)}, u32[]{:S(2)}) collective-permute-start(f32[8,128]{1,0:T(8,128)S(1)} %get-tuple-element.102), channel_id=1, source_target_pairs={{0,8},{1,9},{2,10},{3,11},{4,12},{5,13},{6,14},{7,15},{8,0},{9,1},... | collective-permute-start | bytes 12296 | tf_op jit(solution)/shard_map/ppermute | solution.py:726
  109.1 2.4 %direction_update.1 = f32[48,64,384]{2,1,0:T(8,128)} custom-call(f32[8,128]{1,0:T(8,128)S(1)} %add.135.refs_1_.refs_0_.sums_ref, f32[8,128]{1,0:T(8,128)S(1)} %add.138.one_ref, f32[8,128]{1,0:T(8,128)S(1)} %collective-permute-done.27.two_ref, f32[48,64,384]{2,1,0:T(8,128)S(1)} %bitcast.93, f32[48,64,384]{2,1,0:T(8,128)S(1)} %bitcast.84), custom_call_target="tpu_custom_call" | custom-call | tf_op jit(solution)/shard_map/direction_update/pallas_call | solution.py:174
  (108 shorter events, 37.3 us)
Async XLA Ops:
  1.6 5.6 %collective-permute-start = (s32[32,8]{0,1:T(8,128)S(1)}, s32[32,8]{0,1:T(8,128)S(1)}, u32[]{:S(2)}, u32[]{:S(2)}) collective-permute-start(s32[32,8]{0,1:T(8,128)S(1)} %pad_add_fusion.4), channel_id=1, source_target_pairs={{0,8},{1,9},{2,10},{3,11},{4,12},{5,13},{6,14},{7,15},{8,0},{9,1},... | collective-permute-start | bytes 3080 | tf_op jit(solution)/shard_map/ppermute | solution.py:726
  7.2 3.7 %collective-permute-start.1 = (s32[2,32,8]{1,2,0:T(8,128)S(1)}, s32[2,32,8]{1,2,0:T(8,128)S(1)}, u32[]{:S(2)}, u32[]{:S(2)}) collective-permute-start(s32[2,32,8]{1,2,0:T(8,128)S(1)} %get-tuple-element.141), channel_id=1, source_target_pairs={{0,4},{1,5},{2,6},{3,7},{4,0},{5,1},{6,2},{7,3},{8,12},{9,13},{10,... | collective-permute-start | bytes 6152 | tf_op jit(solution)/shard_map/ppermute | solution.py:726
  10.8 3.7 %collective-permute-start.2 = (s32[2,2,32,8]{2,3,1,0:T(8,128)S(1)}, s32[2,2,32,8]{2,3,1,0:T(8,128)S(1)}, u32[]{:S(2)}, u32[]{:S(2)}) collective-permute-start(s32[2,2,32,8]{2,3,1,0:T(8,128)S(1)} %get-tuple-element.139), channel_id=1, source_target_pairs={{0,2},{1,3},{2,0},{3,1},{4,6},{5,7},{6,4},{7,5},{8,10},{9,11},{10,... | collective-permute-start | bytes 12296 | tf_op jit(solution)/shard_map/ppermute | solution.py:726
  24.8 7.9 %collective-permute-start.8 = (f32[8,64,384]{2,1,0:T(8,128)S(1)}, f32[8,64,384]{2,1,0:T(8,128)S(1)}, u32[]{:S(2)}, u32[]{:S(2)}) collective-permute-start(f32[8,64,384]{2,1,0:T(8,128)S(1)} %get-tuple-element.75), channel_id=1, source_target_pairs={{0,1},{1,0},{2,3},{3,2},{4,5},{5,4},{6,7},{7,6},{8,9},{9,8},{10,11... | collective-permute-start | bytes 2359304 | tf_op jit(solution)/shard_map/ppermute | solution.py:726
  30.8 8.6 %collective-permute-start.5 = (f32[4,16,1024]{2,1,0:T(8,128)S(1)}, f32[4,16,1024]{2,1,0:T(8,128)S(1)}, u32[]{:S(2)}, u32[]{:S(2)}) collective-permute-start(f32[4,16,1024]{2,1,0:T(8,128)S(1)} %get-tuple-element.68), channel_id=1, source_target_pairs={{0,4},{1,5},{2,6},{3,7},{4,0},{5,1},{6,2},{7,3},{8,12},{9,13},{10,... | collective-permute-start | bytes 786440 | tf_op jit(solution)/shard_map/ppermute | solution.py:726
  36.6 8.2 %collective-permute-start.9 = (f32[4,16,1024]{2,1,0:T(8,128)S(1)}, f32[4,16,1024]{2,1,0:T(8,128)S(1)}, u32[]{:S(2)}, u32[]{:S(2)}) collective-permute-start(f32[4,16,1024]{2,1,0:T(8,128)S(1)} %get-tuple-element.77), channel_id=1, source_target_pairs={{0,2},{1,3},{2,0},{3,1},{4,6},{5,7},{6,4},{7,5},{8,10},{9,11},{10,... | collective-permute-start | bytes 786440 | tf_op jit(solution)/shard_map/ppermute | solution.py:726
  39.5 8.8 %collective-permute-start.6 = (f32[2,16,1024]{2,1,0:T(8,128)S(1)}, f32[2,16,1024]{2,1,0:T(8,128)S(1)}, u32[]{:S(2)}, u32[]{:S(2)}) collective-permute-start(f32[2,16,1024]{2,1,0:T(8,128)S(1)} %slice.35), channel_id=1, source_target_pairs={{0,8},{1,9},{2,10},{3,11},{4,12},{5,13},{6,14},{7,15},{8,0},{9,1},... | collective-permute-start | bytes 393224 | tf_op jit(solution)/shard_map/ppermute | solution.py:726
  44.9 6.1 %collective-permute-start.10 = (f32[2,16,1024]{2,1,0:T(8,128)S(1)}, f32[2,16,1024]{2,1,0:T(8,128)S(1)}, u32[]{:S(2)}, u32[]{:S(2)}) collective-permute-start(f32[2,16,1024]{2,1,0:T(8,128)S(1)} %slice_bitcast_fusion), channel_id=1, source_target_pairs={{0,4},{1,5},{2,6},{3,7},{4,0},{5,1},{6,2},{7,3},{8,12},{9,13},{10,... | collective-permute-start | bytes 393224 | tf_op jit(solution)/shard_map/ppermute | solution.py:726
  48.3 5.6 %collective-permute-start.7 = (f32[16,1024]{1,0:T(8,128)S(1)}, f32[16,1024]{1,0:T(8,128)S(1)}, u32[]{:S(2)}, u32[]{:S(2)}) collective-permute-start(f32[16,1024]{1,0:T(8,128)S(1)} %get-tuple-element.136), channel_id=1, source_target_pairs={{0,2},{1,3},{2,0},{3,1},{4,6},{5,7},{6,4},{7,5},{8,10},{9,11},{10,... | collective-permute-start | bytes 196616 | tf_op jit(solution)/shard_map/ppermute | solution.py:726
  51.0 6.4 %collective-permute-start.11 = (f32[16,1024]{1,0:T(8,128)S(1)}, f32[16,1024]{1,0:T(8,128)S(1)}, u32[]{:S(2)}, u32[]{:S(2)}) collective-permute-start(f32[16,1024]{1,0:T(8,128)S(1)} %get-tuple-element.134), channel_id=1, source_target_pairs={{0,8},{1,9},{2,10},{3,11},{4,12},{5,13},{6,14},{7,15},{8,0},{9,1},... | collective-permute-start | bytes 196616 | tf_op jit(solution)/shard_map/ppermute | solution.py:726
  59.0 6.1 %collective-permute-start.19 = (f32[16,1024]{1,0:T(8,128)S(1)}, f32[16,1024]{1,0:T(8,128)S(1)}, u32[]{:S(2)}, u32[]{:S(2)}) collective-permute-start(f32[16,1024]{1,0:T(8,128)S(1)} %get-tuple-element.98), channel_id=1, source_target_pairs={{0,8},{1,9},{2,10},{3,11},{4,12},{5,13},{6,14},{7,15},{8,0},{9,1},... | collective-permute-start | bytes 196616 | tf_op jit(solution)/shard_map/ppermute | solution.py:726
  61.2 8.2 %collective-permute-start.12 = (f32[8,128]{1,0:T(8,128)S(1)}, f32[8,128]{1,0:T(8,128)S(1)}, u32[]{:S(2)}, u32[]{:S(2)}) collective-permute-start(f32[8,128]{1,0:T(8,128)S(1)} %get-tuple-element.81), channel_id=1, source_target_pairs={{0,8},{1,9},{2,10},{3,11},{4,12},{5,13},{6,14},{7,15},{8,0},{9,1},... | collective-permute-start | bytes 12296 | tf_op jit(solution)/shard_map/ppermute | solution.py:726
  63.7 5.7 %collective-permute-start.13 = (f32[16,1024]{1,0:T(8,128)S(1)}, f32[16,1024]{1,0:T(8,128)S(1)}, u32[]{:S(2)}, u32[]{:S(2)}) collective-permute-start(f32[16,1024]{1,0:T(8,128)S(1)} %get-tuple-element.82), channel_id=1, source_target_pairs={{0,2},{1,3},{2,0},{3,1},{4,6},{5,7},{6,4},{7,5},{8,10},{9,11},{10,... | collective-permute-start | bytes 196616 | tf_op jit(solution)/shard_map/ppermute | solution.py:726
  65.2 10.8 %collective-permute-start.20 = (f32[2,16,1024]{2,1,0:T(8,128)S(1)}, f32[2,16,1024]{2,1,0:T(8,128)S(1)}, u32[]{:S(2)}, u32[]{:S(2)}) collective-permute-start(f32[2,16,1024]{2,1,0:T(8,128)S(1)} %get-tuple-element.133), channel_id=1, source_target_pairs={{0,4},{1,5},{2,6},{3,7},{4,0},{5,1},{6,2},{7,3},{8,12},{9,13},{10,... | collective-permute-start | bytes 393224 | tf_op jit(solution)/shard_map/ppermute | solution.py:726
  69.4 7.8 %collective-permute-start.15 = (f32[2,16,1024]{2,1,0:T(8,128)S(1)}, f32[2,16,1024]{2,1,0:T(8,128)S(1)}, u32[]{:S(2)}, u32[]{:S(2)}) collective-permute-start(f32[2,16,1024]{2,1,0:T(8,128)S(1)} %pad_maximum_fusion.4), channel_id=1, source_target_pairs={{0,8},{1,9},{2,10},{3,11},{4,12},{5,13},{6,14},{7,15},{8,0},{9,1},... | collective-permute-start | bytes 393224 | tf_op jit(solution)/shard_map/ppermute | solution.py:726
  72.3 3.6 %collective-permute-start.14 = (f32[8,128]{1,0:T(8,128)S(1)}, f32[8,128]{1,0:T(8,128)S(1)}, u32[]{:S(2)}, u32[]{:S(2)}) collective-permute-start(f32[8,128]{1,0:T(8,128)S(1)} %add.132), channel_id=1, source_target_pairs={{0,4},{1,5},{2,6},{3,7},{4,0},{5,1},{6,2},{7,3},{8,12},{9,13},{10,... | collective-permute-start | bytes 12296 | tf_op jit(solution)/shard_map/ppermute | solution.py:726
  76.0 6.5 %collective-permute-start.21 = (f32[2,2,16,1024]{3,2,0,1:T(8,128)S(1)}, f32[2,2,16,1024]{3,2,0,1:T(8,128)S(1)}, u32[]{:S(2)}, u32[]{:S(2)}) collective-permute-start(f32[2,2,16,1024]{3,2,0,1:T(8,128)S(1)} %pad_maximum_fusion.3), channel_id=1, source_target_pairs={{0,2},{1,3},{2,0},{3,1},{4,6},{5,7},{6,4},{7,5},{8,10},{9,11},{10,... | collective-permute-start | bytes 786440 | tf_op jit(solution)/shard_map/ppermute | solution.py:726
  77.3 7.8 %collective-permute-start.17 = (f32[2,2,16,1024]{3,2,1,0:T(8,128)S(1)}, f32[2,2,16,1024]{3,2,1,0:T(8,128)S(1)}, u32[]{:S(2)}, u32[]{:S(2)}) collective-permute-start(f32[2,2,16,1024]{3,2,1,0:T(8,128)S(1)} %pad_maximum_fusion.2), channel_id=1, source_target_pairs={{0,4},{1,5},{2,6},{3,7},{4,0},{5,1},{6,2},{7,3},{8,12},{9,13},{10,... | collective-permute-start | bytes 786440 | tf_op jit(solution)/shard_map/ppermute | solution.py:726
  78.4 4.1 %collective-permute-start.16 = (f32[8,128]{1,0:T(8,128)S(1)}, f32[8,128]{1,0:T(8,128)S(1)}, u32[]{:S(2)}, u32[]{:S(2)}) collective-permute-start(f32[8,128]{1,0:T(8,128)S(1)} %add.133), channel_id=1, source_target_pairs={{0,2},{1,3},{2,0},{3,1},{4,6},{5,7},{6,4},{7,5},{8,10},{9,11},{10,... | collective-permute-start | bytes 12296 | tf_op jit(solution)/shard_map/ppermute | solution.py:726
  85.0 5.1 %collective-permute-start.22 = (f32[8,64,384]{2,1,0:T(8,128)S(1)}, f32[8,64,384]{2,1,0:T(8,128)S(1)}, u32[]{:S(2)}, u32[]{:S(2)}) collective-permute-start(f32[8,64,384]{2,1,0:T(8,128)S(1)} %adjoint_rows.2.refs_6_), channel_id=1, source_target_pairs={{0,1},{1,0},{2,3},{3,2},{4,5},{5,4},{6,7},{7,6},{8,9},{9,8},{10,11... | collective-permute-start | bytes 2359304 | tf_op jit(solution)/shard_map/ppermute | solution.py:726
  87.6 2.5 %collective-permute-start.23 = (f32[8,64,384]{2,1,0:T(8,128)S(1)}, f32[8,64,384]{2,1,0:T(8,128)S(1)}, u32[]{:S(2)}, u32[]{:S(2)}) collective-permute-start(f32[8,64,384]{2,1,0:T(8,128)S(1)} %adjoint_rows.3.refs_8_), channel_id=1, source_target_pairs={{0,1},{1,0},{2,3},{3,2},{4,5},{5,4},{6,7},{7,6},{8,9},{9,8},{10,11... | collective-permute-start | bytes 2359304 | tf_op jit(solution)/shard_map/ppermute | solution.py:726
  96.1 4.6 %collective-permute-start.24 = (f32[8,128]{1,0:T(8,128)S(1)}, f32[8,128]{1,0:T(8,128)S(1)}, u32[]{:S(2)}, u32[]{:S(2)}) collective-permute-start(f32[8,128]{1,0:T(8,128)S(1)} %get-tuple-element.102), channel_id=1, source_target_pairs={{0,8},{1,9},{2,10},{3,11},{4,12},{5,13},{6,14},{7,15},{8,0},{9,1},... | collective-permute-start | bytes 12296 | tf_op jit(solution)/shard_map/ppermute | solution.py:726
  100.7 3.6 %collective-permute-start.25 = (f32[8,128]{1,0:T(8,128)S(1)}, f32[8,128]{1,0:T(8,128)S(1)}, u32[]{:S(2)}, u32[]{:S(2)}) collective-permute-start(f32[8,128]{1,0:T(8,128)S(1)} %add.136), channel_id=1, source_target_pairs={{0,4},{1,5},{2,6},{3,7},{4,0},{5,1},{6,2},{7,3},{8,12},{9,13},{10,... | collective-permute-start | bytes 12296 | tf_op jit(solution)/shard_map/ppermute | solution.py:726
  104.3 3.6 %collective-permute-start.26 = (f32[8,128]{1,0:T(8,128)S(1)}, f32[8,128]{1,0:T(8,128)S(1)}, u32[]{:S(2)}, u32[]{:S(2)}) collective-permute-start(f32[8,128]{1,0:T(8,128)S(1)} %add.137), channel_id=1, source_target_pairs={{0,2},{1,3},{2,0},{3,1},{4,6},{5,7},{6,4},{7,5},{8,10},{9,11},{10,... | collective-permute-start | bytes 12296 | tf_op jit(solution)/shard_map/ppermute | solution.py:726
  (13 other events, 119.0 us)

commit v5 on v4

--- a/solution.py
+++ b/solution.py
@@ -89,18 +89,15 @@
 
 
 def load(value):
-    flat = (-1,) + value.shape[-3:]
-    out = pltpu.with_memory_space_constraint(value.reshape(flat), pltpu.HBM)
-    out = pl.pallas_call(
+    return pl.pallas_call(
         load_kernel,
         in_specs=[in_hbm()],
         out_specs=resident(),
-        out_shape=jax.ShapeDtypeStruct(out.shape, F32),
-        scratch_shapes=[pltpu.SemaphoreType.DMA((out.shape[0],))],
+        out_shape=jax.ShapeDtypeStruct(value.shape, F32),
+        scratch_shapes=[pltpu.SemaphoreType.DMA((value.shape[0],))],
         compiler_params=params(2),
         name="load",
-    )(out)
-    return out.reshape(value.shape)
+    )(pltpu.with_memory_space_constraint(value, pltpu.HBM))
 
 
 def squares_kernel(res_ref, norm_ref):
@@ -386,11 +383,18 @@
     return values[:coils], values[coils:], matrix, norm
 
 
-def start_turn(info_ref, start_ref):
-    chunk, _, count, _ = info_ref.shape
-    info = info_ref[:, 0].reshape(chunk * count, FIELDS)
+def side_of(pair, bit):
+    return (pair >> bit) & 1, ((pair >> (bit + 1)) << bit) | (pair & ((1 << bit) - 1))
+
+
+def of_side(pairs, bit, side):
+    return [pair for pair in range(pairs) if side_of(pair, bit)[0] == side]
+
+
+def start_turn(pairs, info_ref, start_ref):
+    info = jnp.concatenate([info_ref[pair, 0] for pair in pairs], axis=0)
     starts = start_ref.shape[0]
-    hot = lax.broadcasted_iota(jnp.int32, (chunk * count, starts), 1) == info[:, 2:3]
+    hot = lax.broadcasted_iota(jnp.int32, (info.shape[0], starts), 1) == info[:, 2:3]
     turn = jnp.dot(
         jnp.where(hot, 1.0, 0.0), start_ref[...], precision=HIGHEST, preferred_element_type=F32
     )
@@ -403,19 +407,16 @@
     return (at >= info[:, 3:4]) & (at < info[:, 3:4] + segment)
 
 
-def side_of(value, bit):
-    step = 2**bit
-    return value // step % 2, value // (2 * step) * step + value % step
-
-
-def cells_kernel(tiles, segment, bit, keep_ref, got_ref, info_ref, start_ref, table_ref, *out_refs):
-    pairs, count, width = keep_ref.shape
-    count = count // 2
+def cells_kernel(
+    tiles, segment, bit, side, keep_ref, got_ref, info_ref, start_ref, table_ref, out_ref
+):
+    chosen = of_side(keep_ref.shape[0], bit, side)
+    pairs, count = len(chosen), keep_ref.shape[1] // 2
     cells = table_ref.shape[2]
-    info, cos, sin = start_turn(info_ref, start_ref)
-    both = keep_ref[...] + got_ref[...]
-    re = both[:, :count].reshape(pairs * count, width)
-    im = both[:, count:].reshape(pairs * count, width)
+    info, cos, sin = start_turn(chosen, info_ref, start_ref)
+    both = [keep_ref[pair] + got_ref[pair] for pair in chosen]
+    re = jnp.concatenate([value[:count] for value in both], axis=0)
+    im = jnp.concatenate([value[count:] for value in both], axis=0)
     re, im = cos * re + sin * im, cos * im - sin * re
     value = [jnp.concatenate([re, im], axis=1), jnp.concatenate([im, -re], axis=1)]
     value = split(jnp.concatenate(value, axis=0), 3)
@@ -424,21 +425,17 @@
     for ri in range(2):
         mine = out[ri * pairs * count : (ri + 1) * pairs * count]
         mine = jnp.where(mask, mine, 0.0).reshape(pairs, count // tiles, tiles, cells)
-        mine = jnp.sum(mine, axis=1)
-        for pair in range(pairs):
-            side, place = side_of(pair, bit)
-            out_refs[side][place, :, ri * cells : (ri + 1) * cells] = mine[pair]
-
-
-def row_cells(keep, got, info, start, table, tiles, segment, bit):
+        out_ref[:, :, ri * cells : (ri + 1) * cells] = jnp.sum(mine, axis=1)
+
+
+def row_cells(keep, got, info, start, table, tiles, segment, bit, side):
     pairs, double, width = keep.shape
     lines = 2 * table.shape[2]
     chunk = pairs if pairs <= 8 else 4
     steps = pairs // chunk
     rows = blocks((chunk, double, width), lambda i: (i, 0, 0), steps)
-    half = jax.ShapeDtypeStruct((pairs // 2, tiles, lines), F32)
     return pl.pallas_call(
-        lambda *refs: cells_kernel(tiles, segment, bit, *refs),
+        lambda *refs: cells_kernel(tiles, segment, bit, side, *refs),
         grid=() if steps == 1 else (steps,),
         in_specs=[
             rows,
@@ -447,26 +444,47 @@
             resident(),
             resident(),
         ],
-        out_specs=[blocks((chunk // 2, tiles, lines), lambda i: (i, 0, 0), steps)] * 2,
-        out_shape=[half] * 2,
+        out_specs=blocks((chunk // 2, tiles, lines), lambda i: (i, 0, 0), steps),
+        out_shape=jax.ShapeDtypeStruct((pairs // 2, tiles, lines), F32),
         compiler_params=params(24),
         name="row_cells",
     )(keep, got, info, start, table)
 
 
-def adjoint_kernel(segment, bit, had_ref, got_ref, info_ref, start_ref, table_ref, out_ref):
-    chunk, _, count, _ = info_ref.shape
-    _, tiles, cells = had_ref.shape
-    cells = cells // 2
-    info, cos, sin = start_turn(info_ref, start_ref)
+def adjoint_kernel(
+    segment, bit, side, part, steps, cell_ref, info_ref, start_ref, table_ref, *refs
+):
+    out_ref = refs[-3] if part is not None else refs[0]
+    if part is not None:
+        from_hbm, to_ref, sem = refs[0], refs[-2], refs[-1]
+        copies = [
+            pltpu.make_async_copy(from_hbm.at[part, piece], to_ref.at[piece], sem.at[piece])
+            for piece in range(to_ref.shape[0])
+        ]
+
+        def start_copies():
+            for copy in copies:
+                copy.start()
+
+        def wait_copies():
+            for copy in copies:
+                copy.wait()
+
+        if steps == 1:
+            start_copies()
+        else:
+            pl.when(pl.program_id(0) == 0)(start_copies)
+    chosen = of_side(info_ref.shape[0], bit, side)
+    chunk, count = len(chosen), info_ref.shape[2]
+    tiles = cell_ref.shape[1]
+    cells = table_ref.shape[1] // 2
+    info, cos, sin = start_turn(chosen, info_ref, start_ref)
     mask = segment_mask(info, cells, segment)
     both = []
     for ri in range(2):
         wide = []
-        for pair in range(chunk):
-            side, place = side_of(pair, bit)
-            value = (had_ref, got_ref)[side][place, :, ri * cells : (ri + 1) * cells]
-            wide += [value] * (count // tiles)
+        for place in range(chunk):
+            wide += [cell_ref[place, :, ri * cells : (ri + 1) * cells]] * (count // tiles)
         both.append(jnp.where(mask, jnp.concatenate(wide, axis=0), 0.0))
     re, im = both
     value = [jnp.concatenate([re, -im], axis=1), jnp.concatenate([im, re], axis=1)]
@@ -477,42 +495,59 @@
     re, im = out[:rows], out[rows:]
     out_ref[:, :count] = (cos * re - sin * im).reshape(chunk, count, -1)
     out_ref[:, count:] = (cos * im + sin * re).reshape(chunk, count, -1)
-
-
-def adjoint_rows(had, got, info, start, table, segment, bit):
-    half, tiles, lines = had.shape
+    if part is not None:
+        if steps == 1:
+            wait_copies()
+        else:
+            pl.when(pl.program_id(0) == steps - 1)(wait_copies)
+
+
+def adjoint_rows(value, info, start, table, segment, bit, side, large=None, part=None):
+    half, tiles, lines = value.shape
     pairs, _, count, _ = info.shape
     width = table.shape[2]
     chunk = pairs if pairs <= 8 else 4
     steps = pairs // chunk
-    cells = blocks((chunk // 2, tiles, lines), lambda i: (i, 0, 0), steps)
+    more = large is not None
     return pl.pallas_call(
-        lambda *refs: adjoint_kernel(segment, bit, *refs),
+        lambda *refs: adjoint_kernel(segment, bit, side, part, steps, *refs),
         grid=() if steps == 1 else (steps,),
         in_specs=[
-            cells,
-            cells,
+            blocks((chunk // 2, tiles, lines), lambda i: (i, 0, 0), steps),
             blocks((chunk, 1, count, FIELDS), lambda i: (i, 0, 0, 0), steps),
             resident(),
             resident(),
-        ],
-        out_specs=blocks((chunk, 2 * count, width), lambda i: (i, 0, 0), steps),
-        out_shape=jax.ShapeDtypeStruct((pairs, 2 * count, width), F32),
+        ]
+        + [in_hbm()] * more,
+        out_specs=[blocks((chunk // 2, 2 * count, width), lambda i: (i, 0, 0), steps)]
+        + [resident()] * more,
+        out_shape=[jax.ShapeDtypeStruct((half, 2 * count, width), F32)]
+        + ([jax.ShapeDtypeStruct(large.shape[1:], F32)] if more else []),
+        scratch_shapes=[pltpu.SemaphoreType.DMA((large.shape[1],))] if more else [],
         compiler_params=params(24),
         name="adjoint_rows",
-    )(had, got, info, start, table)
-
-
-def tiles_kernel(count_ref, norm_refs, keep_ref, got_ref, weight_ref, out_ref, sums_ref):
+    )(
+        value,
+        info,
+        start,
+        table,
+        *([pltpu.with_memory_space_constraint(large, pltpu.HBM)] if more else []),
+    )
+
+
+def tiles_kernel(coils, count_ref, norm_refs, weight_ref, *refs):
     tiles, _, cells = weight_ref.shape
-    grid = keep_ref[...] + got_ref[...]
-    rows = [grid[:, ri * cells : (ri + 1) * cells] for ri in range(2)]
+    cell_refs, out_refs, sums_refs = refs[: 2 * coils], refs[2 * coils : 3 * coils], refs[3 * coils :]
+    rows = []
+    for keep, got in zip(cell_refs[::2], cell_refs[1::2]):
+        grid = keep[...] + got[...]
+        rows += [grid[:, ri * cells : (ri + 1) * cells] for ri in range(2)]
     found = []
     for tile in range(tiles):
-        both = jnp.concatenate([row[tile : tile + 1] for row in rows], axis=0).astype(BF16)
+        grid = jnp.concatenate([row[tile : tile + 1] for row in rows], axis=0).astype(BF16)
         found.append(
             lax.dot_general(
-                both, weight_ref[tile], (((1,), (1,)), ((), ())), preferred_element_type=F32
+                grid, weight_ref[tile], (((1,), (1,)), ((), ())), preferred_element_type=F32
             )
         )
     spread = []
@@ -520,31 +555,36 @@
         live = lax.broadcasted_iota(jnp.int32, found[tile].shape, 1) < count_ref[tile]
         spread.append(dot(jnp.where(live, found[tile], 0.0).astype(BF16), weight_ref[tile]))
     total = 0.0
-    for ri, row in enumerate(rows):
-        value = jnp.concatenate([piece[ri : ri + 1] for piece in spread], axis=0)
+    for number, row in enumerate(rows):
+        value = jnp.concatenate([piece[number : number + 1] for piece in spread], axis=0)
         total = total + row * value
-        out_ref[:, ri * cells : (ri + 1) * cells] = value
+        ri = number % 2
+        out_refs[number // 2][:, ri * cells : (ri + 1) * cells] = value
     total = jnp.sum(total, keepdims=True)
-    first = lax.broadcasted_iota(jnp.int32, sums_ref.shape, 0) == 0
-    norm = norm_refs[0][...]
-    for ref in norm_refs[1:]:
-        norm = norm + ref[...]
-    sums_ref[...] = norm + jnp.where(first, 0.0, total)
-
-
-def run_tiles(count, norms, keep, got, weight):
-    more = len(norms)
-    return pl.pallas_call(
-        lambda *refs: tiles_kernel(refs[0], refs[1 : 1 + more], *refs[1 + more :]),
-        in_specs=[scalars()] + [resident()] * (more + 3),
-        out_specs=[resident()] * 2,
-        out_shape=[
-            jax.ShapeDtypeStruct(keep.shape, F32),
-            jax.ShapeDtypeStruct((8, 128), F32),
-        ],
+    norm = norm_refs[0][...] + norm_refs[1][...]
+    first = lax.broadcasted_iota(jnp.int32, norm.shape, 0) == 0
+    norm = norm + jnp.where(first, 0.0, total)
+    if sums_refs:
+        sums_refs[0][...] = norm
+    else:
+        out_refs[-1][:, 2 * cells :] = jnp.concatenate([norm] * (tiles // norm.shape[0]), axis=0)
+
+
+def run_tiles(count, norms, cells, weight, carry):
+    coils = len(cells)
+    tiles, lines = cells[0][0].shape
+    shapes = [(tiles, lines + 128 * (carry and c == coils - 1)) for c in range(coils)]
+    if not carry:
+        shapes.append((8, 128))
+    out = pl.pallas_call(
+        lambda *refs: tiles_kernel(coils, refs[0], refs[1:3], *refs[3:]),
+        in_specs=[scalars()] + [resident()] * (2 * coils + 3),
+        out_specs=[resident()] * len(shapes),
+        out_shape=[jax.ShapeDtypeStruct(shape, F32) for shape in shapes],
         compiler_params=params(8),
         name="tiles",
-    )(count, *norms, keep, got, weight)
+    )(count, *norms, weight, *[value for pair in cells for value in pair])
+    return list(out[:coils]), list(out[coils:])
 
 
 def turn_kernel(matrix_ref, out_ref):
@@ -592,16 +632,15 @@
     return value.reshape(16 * shape[0], shape[2])
 
 
-def combine(back, plane, step, sens_ref, dir_ref, res_ref, out_ref):
-    _, coils, rows, _, width = sens_ref.shape
+def combine(back, plane, step, sens_refs, dir_ref, res_ref, out_ref):
+    coils, rows, _, width = sens_refs[0].shape
     planes = plane.stop - plane.start
     half = rows * planes
     total = [DAMPING * dir_ref[ri, :, plane].reshape(half, width) for ri in range(2)]
     for coil in range(coils):
         lanes = slice(coil * width, (coil + 1) * width)
         v_re, v_im = back[:half, lanes], back[half:, lanes]
-        s_re = sens_ref[0, coil, :, plane].reshape(half, width)
-        s_im = sens_ref[1, coil, :, plane].reshape(half, width)
+        s_re, s_im = [ref[coil, :, plane].reshape(half, width) for ref in sens_refs]
         total[0] += s_re * v_re + s_im * v_im
         total[1] += s_re * v_im - s_im * v_re
     squares = 0.0
@@ -613,20 +652,26 @@
     return squares
 
 
-def finish_kernel(planes, me_ref, sums_ref, sens_ref, dir_ref, res_ref, matrix_ref, *refs):
-    coils, rows, total, width = sens_ref.shape[1:]
-    row_refs = refs[: 2 * coils]
-    out_hbm, out_ref, norm_ref, sem = refs[2 * coils :]
+def finish_kernel(planes, me_ref, sums_ref, re_ref, im_ref, dir_ref, res_ref, matrix_ref, *refs):
+    coils, rows, total, width = re_ref.shape
+    row_refs = refs[: 4 * coils]
+    out_hbm, out_ref, norm_ref, sem = refs[4 * coils :]
     step = sums_ref[0:1, 0:1] / sums_ref[1:2, 0:1]
     squares = jnp.zeros((planes, width), F32)
     copies = []
     for group in range(total // planes):
         pair, odd = lax.bitwise_xor(group, me_ref[0] // 2), lax.rem(me_ref[0], 2)
-        mine = jnp.concatenate([ref[pair] for ref in row_refs[::2]], axis=1)
-        got = jnp.concatenate([ref[pair] for ref in row_refs[1::2]], axis=1)
+        values = []
+        for coil in range(coils):
+            side, place = side_of(pair, coil % 2)
+            for k in range(2):
+                one, two = row_refs[4 * coil + k], row_refs[4 * coil + 2 + k]
+                values.append(jnp.where(side == 0, one[place], two[place]))
+        mine = jnp.concatenate(values[::2], axis=1)
+        got = jnp.concatenate(values[1::2], axis=1)
         back = back_group(odd, lambda side: matrix_ref[pair, side], mine, got)
         plane = slice(group * planes, (group + 1) * planes)
-        squares += combine(back, plane, step, sens_ref, dir_ref, res_ref, out_ref)
+        squares += combine(back, plane, step, (re_ref, im_ref), dir_ref, res_ref, out_ref)
         at = pl.ds(group * planes, planes)
         copies.append(
             pltpu.make_async_copy(out_ref.at[:, :, at], out_hbm.at[:, :, at], sem.at[group])
@@ -641,17 +686,19 @@
     kept = jax.ShapeDtypeStruct(residual.shape, F32)
     return pl.pallas_call(
         lambda *refs: finish_kernel(planes, *refs),
-        in_specs=[scalars()] + [resident()] * (5 + len(rows)),
+        in_specs=[scalars()] + [resident()] * (6 + len(rows)),
         out_specs=[in_hbm(), resident(), resident()],
         out_shape=[kept, kept, jax.ShapeDtypeStruct(sums.shape, F32)],
         scratch_shapes=[pltpu.SemaphoreType.DMA((residual.shape[2] // planes,))],
         compiler_params=params(16),
         name="finish",
-    )(me, sums, sens, direction, residual, matrix, *rows)
-
-
-def finish_deep_kernel(planes, me_ref, sums_ref, sens_ref, dir_ref, res_ref, matrix_ref, *refs):
-    coils = sens_ref.shape[1]
+    )(me, sums, *sens, direction, residual, matrix, *rows)
+
+
+def finish_deep_kernel(
+    planes, me_ref, sums_ref, re_ref, im_ref, dir_ref, res_ref, matrix_ref, *refs
+):
+    coils = re_ref.shape[0]
     row_refs = refs[: 2 * coils]
     out_ref, norm_ref, squares_ref, sum_ref = refs[2 * coils :]
     group, pair = pl.program_id(0), pl.program_id(1)
@@ -674,14 +721,14 @@
     def _():
         step = sums_ref[0:1, 0:1] / sums_ref[1:2, 0:1]
         squares_ref[...] += combine(
-            sum_ref[...], slice(0, planes), step, sens_ref, dir_ref, res_ref, out_ref
+            sum_ref[...], slice(0, planes), step, (re_ref, im_ref), dir_ref, res_ref, out_ref
         )
         total = jnp.sum(squares_ref[...], keepdims=True)
         norm_ref[...] = jnp.broadcast_to(total, norm_ref.shape)
 
 
 def finish_deep(me, sums, rows, sens, direction, residual, matrix, planes, slabs_group):
-    _, coils, height, total, width = sens.shape
+    coils, height, total, width = sens[0].shape
     double = rows[0].shape[1]
     groups, deep = total // planes, slabs_group // 2
 
@@ -698,9 +745,8 @@
             grid=(groups, deep),
             in_specs=[
                 small,
-                pl.BlockSpec(
-                    (2, coils, height, planes, width), lambda i, j, me: (0, 0, 0, i, 0)
-                ),
+                pl.BlockSpec((coils, height, planes, width), lambda i, j, me: (0, 0, i, 0)),
+                pl.BlockSpec((coils, height, planes, width), lambda i, j, me: (0, 0, i, 0)),
                 image,
                 image,
                 pl.BlockSpec((1,) + matrix.shape[1:], lambda i, j, me: (pair(i, j, me), 0, 0, 0)),
@@ -718,7 +764,7 @@
         ],
         compiler_params=params(32),
         name="finish_deep",
-    )(me, sums, sens, direction, residual, matrix, *rows)
+    )(me, sums, *sens, direction, residual, matrix, *rows)
     return out, out, norm
 
 
@@ -810,45 +856,63 @@
         me_array, info, sensitivity, direction, x_table, planes, slabs_group
     )
     got = [swap(value, 1, slabs) for value in send]
-    grid = [
-        row_cells(keep[c], got[c], info, start_table, y_forward, tiles, segment, c % 2)
-        for c in range(coils)
-    ]
-    grid[-1], x_matrix, residual = lax.optimization_barrier((grid[-1], x_matrix, residual))
+    grid = []
+    for c in range(coils):
+        send, stay = [
+            row_cells(keep[c], got[c], info, start_table, y_forward, tiles, segment, c % 2, side)
+            for side in (1, 0)
+        ]
+        grid.append([stay, send])
+    grid[-1][0], x_matrix, residual = lax.optimization_barrier((grid[-1][0], x_matrix, residual))
     x_matrix = transposed(x_matrix, planes // own)
     norms = [norm, squares(residual)]
     high_bits = bits[1:]
     orders = [high_bits[c % 2 :] + high_bits[: c % 2] for c in range(coils)]
-    ways = [high_bits[c % 2 :] + high_bits[: c % 2] for c in range(coils)]
-    grid = [sum_scatter(*value, ways[c % 2], slabs) for c, value in enumerate(grid)]
+    grid = [sum_scatter(*value, order, slabs) for value, order in zip(grid, orders)]
     grid[-1], x_matrix, norms = lax.optimization_barrier((grid[-1], x_matrix, norms))
 
-    rows_back, loaded = [], []
-    for c, order in enumerate(orders):
-        spread, sums = run_tiles(tile_count, norms, *grid[c], tile_weight)
-        norms = [sums]
-        dims = spread.shape
-        have = []
-        for number, bit in enumerate(order[::-1]):
-            if c == coils - 1:
-                sums = sums + swap(sums, high_bits[-1 - number], slabs)
-            other = swap(spread, bit, slabs)
-            if c == coils - 1 and number < 3:
-                loaded.append(load((sensitivity, direction, residual)[number]))
-            if bit != order[0]:
-                spread = jnp.stack([spread, other], axis=sum(1 for b in have if b > bit))
-                have.append(bit)
-                if c == coils - 1:
-                    sums, spread, sensitivity, direction, residual, *loaded = lax.optimization_barrier(
-                        (sums, spread, sensitivity, direction, residual, *loaded)
-                    )
-        spread, other = spread.reshape((-1,) + dims), other.reshape((-1,) + dims)
-        if c == coils - 1:
-            sums, spread, other, *loaded = lax.optimization_barrier((sums, spread, other, *loaded))
-        mine = adjoint_rows(spread, other, info, start_table, y_back, segment, c % 2)
-        rows_back += [mine, swap(mine, 1, slabs)]
-    sums = sums + swap(sums, 1, slabs)
-    sens, move, residual = loaded
+    spread, sums = run_tiles(tile_count, norms, grid, tile_weight, False)
+    rows_back, sens, loaded, inputs = [], [], [], [direction, residual]
+    dims = [value.shape for value in spread]
+    orders = [high_bits[c % 2 :] + high_bits[: c % 2] for c in range(coils)]
+    have = [[] for _ in range(coils)]
+    for number in range(len(high_bits)):
+        ways = [order[-1 - number] for order in orders]
+        other = [swap(value, bit, slabs) for value, bit in zip(spread, ways)]
+        if not False:
+            sums = [sums[0] + swap(sums[0], high_bits[-1 - number], slabs)]
+        if 1 <= number < 1 + 2:
+            loaded.append(load(inputs[number - 1]))
+        if number == len(high_bits) - 1:
+            for c in range(coils):
+                had = spread[c].reshape((-1,) + dims[c])
+                mine, part = adjoint_rows(
+                    had, info, start_table, y_back, segment, c % 2, 0, sensitivity, c
+                )
+                sens.append(part)
+                rows_back.append([mine, swap(mine, 1, slabs)])
+        else:
+            for c in range(coils):
+                axis = sum(1 for b in have[c] if b > ways[c])
+                spread[c] = jnp.stack([spread[c], other[c]], axis=axis)
+                have[c].append(ways[c])
+        spread, other, sums, loaded, inputs = lax.optimization_barrier((spread, other, sums, loaded, inputs))
+    for c in range(coils):
+        got = other[c].reshape((-1,) + dims[c])
+        (mine,) = adjoint_rows(got, info, start_table, y_back, segment, c % 2, 1)
+        rows_back[c] += [mine, swap(mine, 1, slabs)]
+    sums = sums[0] + swap(sums[0], 1, slabs)
+    move, residual = loaded
+    if slabs_group == 2:
+        rows_back = [value for values in rows_back for value in values]
+    else:
+        both = []
+        for c, (one, near_one, two, near_two) in enumerate(rows_back):
+            shape = (pairs >> (c % 2 + 1), 1 << (c % 2)) + one.shape[1:]
+            for had, got in ((one, two), (near_one, near_two)):
+                value = jnp.stack([had.reshape(shape), got.reshape(shape)], axis=1)
+                both.append(value.reshape((pairs,) + one.shape[1:]))
+        rows_back = both
     if slabs_group == 2:
         residual_next, res, norm = finish(
             me_array, sums, rows_back, sens, move, residual, x_matrix, planes

time: 112 us -> 110 us (0.982)
  starting transfers between devices: 35.5 us -> 30 us
  waiting for transfers between devices: 24.7 us -> 29.5 us
  Pallas kernels: 46.8 us -> 45.4 us
    ppermute x28 -> x30, starting transfers between devices: 35.5 us -> 30 us  [swap(): return lax.ppermute(value, 'slab', [(i, i ^ bit) for i in range(slabs)])]
    ppermute x28 -> x30, waiting for transfers between devices: 24.7 us -> 29.5 us  [swap(): return lax.ppermute(value, 'slab', [(i, i ^ bit) for i in range(slabs)])]
    pallas_call x3 -> x2, Pallas kernels: 8.7 us -> 4.9 us  [load(): pl.pallas_call(load_kernel, in_specs=[in_hbm()], out_specs=resident(), ou...]
    pallas_call x6 -> x9, Pallas kernels: 15.9 us -> 18.2 us  [the longest x4 8.3 us: row_cells(): pl.pallas_call(lambda *refs: cells_kernel(tiles, segment, bit, side, *ref...]
  transfers between devices with their start and end apart: 28 -> 30, of which waited for: 18 -> 17; matrix products, arithmetic and copies ran while one was open for 2% -> 2% of each run, Pallas kernels for 25% -> 24%
where the time goes in v5:
time: 110 us
  Pallas kernels  45.4 us (41%)
  starting transfers between devices  30 us (27%)
  waiting for transfers between devices  29.5 us (27%)
  other arithmetic  3.12 us (3%)
  between operations  1.22 us (1%)
    ppermute x30, starting transfers between devices, swap(): return lax.ppermute(value, 'slab', [(i, i ^ bit) for i in range(slabs)])  30 us
    ppermute x30, waiting for transfers between devices, swap(): return lax.ppermute(value, 'slab', [(i, i ^ bit) for i in range(slabs)])  29.5 us
    pallas_call x1, Pallas kernels, partial_rows(): pl.pallas_call(lambda *refs: rows_kernel(planes, slabs_group, steps, *ref...  8.61 us
    pallas_call x4, Pallas kernels, row_cells(): pl.pallas_call(lambda *refs: cells_kernel(tiles, segment, bit, side, *ref...  8.3 us
    pallas_call x4, Pallas kernels, adjoint_rows(): pl.pallas_call(lambda *refs: adjoint_kernel(segment, bit, side, part, ste...  8.28 us
    pallas_call x1, Pallas kernels, finish(): pl.pallas_call(lambda *refs: finish_kernel(planes, *refs), in_specs=[scal...  6.1 us
    pallas_call x2, Pallas kernels, load(): pl.pallas_call(load_kernel, in_specs=[in_hbm()], out_specs=resident(), ou...  4.9 us
    pallas_call x3, Pallas kernels, x_update(): pl.pallas_call(lambda *refs: x_kernel(piece * rows, *refs), grid=(2,), in...  3.85 us
  transfers between devices with their start and end apart: 30, of which 17 were waited for; matrix products, arithmetic and copies ran while one was open for 2% of the time, Pallas kernels for 24%

profile of v5, /device:TPU:0, one launch (start us, length us, event | category | flops | bytes accessed | tf_op | source)
XLA Modules:
  0.0 109.9 jit_solution(3570190516225306025)
XLA Ops:
  1.6 4.0 %collective-permute-start = (s32[32,8]{0,1:T(8,128)S(1)}, s32[32,8]{0,1:T(8,128)S(1)}, u32[]{:S(2)}, u32[]{:S(2)}) collective-permute-start(s32[32,8]{0,1:T(8,128)S(1)} %pad_add_fusion.4), channel_id=1, source_target_pairs={{0,8},{1,9},{2,10},{3,11},{4,12},{5,13},{6,14},{7,15},{8,0},{9,1},... | collective-permute-start | bytes 3080 | tf_op jit(solution)/shard_map/ppermute | solution.py:772
  7.2 1.9 %collective-permute-start.1 = (s32[2,32,8]{1,2,0:T(8,128)S(1)}, s32[2,32,8]{1,2,0:T(8,128)S(1)}, u32[]{:S(2)}, u32[]{:S(2)}) collective-permute-start(s32[2,32,8]{1,2,0:T(8,128)S(1)} %get-tuple-element.133), channel_id=1, source_target_pairs={{0,4},{1,5},{2,6},{3,7},{4,0},{5,1},{6,2},{7,3},{8,12},{9,13},{10,... | collective-permute-start | bytes 6152 | tf_op jit(solution)/shard_map/ppermute | solution.py:772
  10.8 1.8 %collective-permute-start.2 = (s32[2,2,32,8]{2,3,1,0:T(8,128)S(1)}, s32[2,2,32,8]{2,3,1,0:T(8,128)S(1)}, u32[]{:S(2)}, u32[]{:S(2)}) collective-permute-start(s32[2,2,32,8]{2,3,1,0:T(8,128)S(1)} %get-tuple-element.131), channel_id=1, source_target_pairs={{0,2},{1,3},{2,0},{3,1},{4,6},{5,7},{6,4},{7,5},{8,10},{9,11},{10,... | collective-permute-start | bytes 12296 | tf_op jit(solution)/shard_map/ppermute | solution.py:772
  15.9 8.6 %partial_rows.1 = (f32[8,64,384]{2,1,0:T(8,128)S(1)}, f32[8,64,384]{2,1,0:T(8,128)S(1)}, f32[8,64,384]{2,1,0:T(8,128)S(1)}, f32[8,64,384]{2,1,0:T(8,128)S(1)}, b...) custom-call(s32[1]{0:T(128)} %bitcast.refs_0_, s32[8,2,32,8]{3,2,1,0:T(8,128)S(1)} %pad_add_fusion.refs_1_.refs_2_, ...), custom_call_target="tpu_custom_call" | custom-call | tf_op jit(solution)/shard_map/partial_rows/pallas_call | solution.py:348
  25.1 1.8 %collective-permute-done.4.refs_1_ = f32[8,64,384]{2,1,0:T(8,128)S(1)} collective-permute-done((f32[8,64,384]{2,1,0:T(8,128)S(1)}, f32[8,64,384]{2,1,0:T(8,128)S(1)}, u32[]{:S(2)}, u32[]{:S(2)}) %collective-permute-start.4) | collective-permute-done | bytes 786464 | tf_op jit(solution)/shard_map/ppermute | solution.py:772
  26.9 2.1 %row_cells.5 = f32[4,16,1024]{2,1,0:T(8,128)S(1)} custom-call(f32[8,64,384]{2,1,0:T(8,128)S(1)} %get-tuple-element.59.refs_0_, f32[8,64,384]{2,1,0:T(8,128)S(1)} %collective-permute-done.4.refs_1_, s32[8,2,32,8]{3,2,1,0:T(8,128)S(1)} %pad_add_fusion.refs_1_.refs_2_, f32[16,768]{1,0:T(8,128)S(1)} %copy-done.2, bf16[3,768,512]{2,1,0:T(8,128)(2,1)S(1)} %copy-done), custom_call_target="tpu_custom_call" | custom-call | tf_op jit(solution)/shard_map/row_cells/pallas_call | solution.py:437
  29.0 2.0 %collective-permute-start.5 = (f32[4,16,1024]{2,1,0:T(8,128)S(1)}, f32[4,16,1024]{2,1,0:T(8,128)S(1)}, u32[]{:S(2)}, u32[]{:S(2)}) collective-permute-start(f32[4,16,1024]{2,1,0:T(8,128)S(1)} %row_cells.5), channel_id=1, source_target_pairs={{0,4},{1,5},{2,6},{3,7},{4,0},{5,1},{6,2},{7,3},{8,12},{9,13},{10,... | collective-permute-start | bytes 786440 | tf_op jit(solution)/shard_map/ppermute | solution.py:772
  31.0 2.1 %row_cells.7 = f32[4,16,1024]{2,1,0:T(8,128)S(1)} custom-call(f32[8,64,384]{2,1,0:T(8,128)S(1)} %get-tuple-element.68.refs_0_, f32[8,64,384]{2,1,0:T(8,128)S(1)} %collective-permute-done.8.refs_1_, s32[8,2,32,8]{3,2,1,0:T(8,128)S(1)} %pad_add_fusion.refs_1_.refs_2_, f32[16,768]{1,0:T(8,128)S(1)} %copy-done.2, bf16[3,768,512]{2,1,0:T(8,128)(2,1)S(1)} %copy-done), custom_call_target="tpu_custom_call" | custom-call | tf_op jit(solution)/shard_map/row_cells/pallas_call | solution.py:437
  34.6 2.1 %row_cells.4 = f32[4,16,1024]{2,1,0:T(8,128)S(1)} custom-call(f32[8,64,384]{2,1,0:T(8,128)S(1)} %get-tuple-element.59.refs_0_, f32[8,64,384]{2,1,0:T(8,128)S(1)} %collective-permute-done.4.refs_1_, s32[8,2,32,8]{3,2,1,0:T(8,128)S(1)} %pad_add_fusion.refs_1_.refs_2_, f32[16,768]{1,0:T(8,128)S(1)} %copy-done.2, bf16[3,768,512]{2,1,0:T(8,128)(2,1)S(1)} %copy-done), custom_call_target="tpu_custom_call" | custom-call | tf_op jit(solution)/shard_map/row_cells/pallas_call | solution.py:437
  36.7 2.1 %row_cells.6 = f32[4,16,1024]{2,1,0:T(8,128)S(1)} custom-call(f32[8,64,384]{2,1,0:T(8,128)S(1)} %get-tuple-element.68.refs_0_, f32[8,64,384]{2,1,0:T(8,128)S(1)} %collective-permute-done.8.refs_1_, s32[8,2,32,8]{3,2,1,0:T(8,128)S(1)} %pad_add_fusion.refs_1_.refs_2_, f32[16,768]{1,0:T(8,128)S(1)} %copy-done.2, bf16[3,768,512]{2,1,0:T(8,128)(2,1)S(1)} %copy-done), custom_call_target="tpu_custom_call" | custom-call | tf_op jit(solution)/shard_map/row_cells/pallas_call | solution.py:437
  38.9 2.7 %collective-permute-start.6 = (f32[2,16,1024]{2,1,0:T(8,128)S(1)}, f32[2,16,1024]{2,1,0:T(8,128)S(1)}, u32[]{:S(2)}, u32[]{:S(2)}) collective-permute-start(f32[2,16,1024]{2,1,0:T(8,128)S(1)} %slice.35), channel_id=1, source_target_pairs={{0,8},{1,9},{2,10},{3,11},{4,12},{5,13},{6,14},{7,15},{8,0},{9,1},... | collective-permute-start | bytes 393224 | tf_op jit(solution)/shard_map/ppermute | solution.py:772
  42.2 5.5 %collective-permute-done.6 = f32[2,16,1024]{2,1,0:T(8,128)S(1)} collective-permute-done((f32[2,16,1024]{2,1,0:T(8,128)S(1)}, f32[2,16,1024]{2,1,0:T(8,128)S(1)}, u32[]{:S(2)}, u32[]{:S(2)}) %collective-permute-start.6) | collective-permute-done | bytes 131104 | tf_op jit(solution)/shard_map/ppermute | solution.py:772
  52.1 2.7 %collective-permute-done.11.refs_5_ = f32[16,1024]{1,0:T(8,128)S(1)} collective-permute-done((f32[16,1024]{1,0:T(8,128)S(1)}, f32[16,1024]{1,0:T(8,128)S(1)}, u32[]{:S(2)}, u32[]{:S(2)}) %collective-permute-start.11) | collective-permute-done | bytes 65568 | tf_op jit(solution)/shard_map/ppermute | solution.py:772
  56.5 2.9 %collective-permute-start.14 = (f32[8,128]{1,0:T(8,128)S(1)}, f32[8,128]{1,0:T(8,128)S(1)}, u32[]{:S(2)}, u32[]{:S(2)}) collective-permute-start(f32[8,128]{1,0:T(8,128)S(1)} %get-tuple-element.74), channel_id=1, source_target_pairs={{0,8},{1,9},{2,10},{3,11},{4,12},{5,13},{6,14},{7,15},{8,0},{9,1},... | collective-permute-start | bytes 12296 | tf_op jit(solution)/shard_map/ppermute | solution.py:772
  60.0 1.7 %collective-permute-done.14 = f32[8,128]{1,0:T(8,128)S(1)} collective-permute-done((f32[8,128]{1,0:T(8,128)S(1)}, f32[8,128]{1,0:T(8,128)S(1)}, u32[]{:S(2)}, u32[]{:S(2)}) %collective-permute-start.14) | collective-permute-done | bytes 4128 | tf_op jit(solution)/shard_map/ppermute | solution.py:772
  61.8 1.9 %collective-permute-done.13 = f32[16,1024]{1,0:T(8,128)S(1)} collective-permute-done((f32[16,1024]{1,0:T(8,128)S(1)}, f32[16,1024]{1,0:T(8,128)S(1)}, u32[]{:S(2)}, u32[]{:S(2)}) %collective-permute-start.13) | collective-permute-done | bytes 65568 | tf_op jit(solution)/shard_map/ppermute | solution.py:772
  63.8 2.6 %collective-permute-start.16 = (f32[2,16,1024]{2,1,0:T(8,128)S(1)}, f32[2,16,1024]{2,1,0:T(8,128)S(1)}, u32[]{:S(2)}, u32[]{:S(2)}) collective-permute-start(f32[2,16,1024]{2,1,0:T(8,128)S(1)} %pad_maximum_fusion.5), channel_id=1, source_target_pairs={{0,8},{1,9},{2,10},{3,11},{4,12},{5,13},{6,14},{7,15},{8,0},{9,1},... | collective-permute-start | bytes 393224 | tf_op jit(solution)/shard_map/ppermute | solution.py:772
  66.5 2.4 %load.2.refs_4_ = f32[2,24,64,384]{3,2,1,0:T(8,128)S(1)} custom-call(f32[2,24,64,384]{3,2,1,0:T(8,128)} %from_hbm), custom_call_target="tpu_custom_call" | custom-call | tf_op jit(solution)/shard_map/load/pallas_call | solution.py:92
  74.0 2.5 %load.3.refs_5_ = f32[2,24,64,384]{3,2,1,0:T(8,128)S(1)} custom-call(f32[2,24,64,384]{3,2,1,0:T(8,128)} %from_hbm.1), custom_call_target="tpu_custom_call" | custom-call | tf_op jit(solution)/shard_map/load/pallas_call | solution.py:92
  76.8 2.5 %adjoint_rows.4 = (f32[4,64,384]{2,1,0:T(8,128)S(1)}, f32[2,24,64,384]{3,2,1,0:T(8,128)S(1)}) custom-call(f32[4,16,1024]{2,1,0:T(8,128)S(1)} %bitcast.91, s32[8,2,32,8]{3,2,1,0:T(8,128)S(1)} %pad_add_fusion.refs_1_.refs_2_, f32[16,768]{1,0:T(8,128)S(1)} %copy-done.2, bf16[2,1024,384]{2,1,0:T(8,128)(2,1)S(1)} %copy-done.1, f32[2,2,24,64,384]{4,3,2,1,0:T(8,128)} %refs_4_.7), custom_call_target="tpu_custom_call" | custom-call | tf_op jit(solution)/shard_map/adjoint_rows/pallas_call | solution.py:512
  79.5 3.0 %adjoint_rows.5 = (f32[4,64,384]{2,1,0:T(8,128)S(1)}, f32[2,24,64,384]{3,2,1,0:T(8,128)S(1)}) custom-call(f32[4,16,1024]{2,1,0:T(8,128)S(1)} %bitcast.90, s32[8,2,32,8]{3,2,1,0:T(8,128)S(1)} %pad_add_fusion.refs_1_.refs_2_, f32[16,768]{1,0:T(8,128)S(1)} %copy-done.2, bf16[2,1024,384]{2,1,0:T(8,128)(2,1)S(1)} %copy-done.1, f32[2,2,24,64,384]{4,3,2,1,0:T(8,128)} %refs_4_.7), custom_call_target="tpu_custom_call" | custom-call | tf_op jit(solution)/shard_map/adjoint_rows/pallas_call | solution.py:512
  88.3 6.1 %finish.1 = (f32[2,24,64,384]{3,2,1,0:T(8,128)}, f32[2,24,64,384]{3,2,1,0:T(8,128)S(1)}, f32[8,128]{1,0:T(8,128)S(1)}) custom-call(s32[1]{0:T(128)} %bitcast.refs_0_, f32[8,128]{1,0:T(8,128)S(1)} %add.135.refs_1_.refs_0_.sums_ref, f32[2,24,64,384]{3,2,1,0:T(8,128)S(1)} %get-tuple-element.86.refs_2_, f32[2,24,64,384]{3,2,1,0:T(8,128)S(1)} %get-tuple-element.87.refs_3_, ...), custom_call_target="tpu_custom_call" | custom-call | tf_op jit(solution)/shard_map/finish/pallas_call | solution.py:687
  97.0 2.0 %collective-permute-done.26 = f32[8,128]{1,0:T(8,128)S(1)} collective-permute-done((f32[8,128]{1,0:T(8,128)S(1)}, f32[8,128]{1,0:T(8,128)S(1)}, u32[]{:S(2)}, u32[]{:S(2)}) %collective-permute-start.26) | collective-permute-done | bytes 4128 | tf_op jit(solution)/shard_map/ppermute | solution.py:772
  107.3 2.4 %direction_update.1 = f32[48,64,384]{2,1,0:T(8,128)} custom-call(f32[8,128]{1,0:T(8,128)S(1)} %add.135.refs_1_.refs_0_.sums_ref, f32[8,128]{1,0:T(8,128)S(1)} %add.138.one_ref, f32[8,128]{1,0:T(8,128)S(1)} %collective-permute-done.29.two_ref, f32[48,64,384]{2,1,0:T(8,128)S(1)} %bitcast.89, f32[48,64,384]{2,1,0:T(8,128)S(1)} %bitcast.81), custom_call_target="tpu_custom_call" | custom-call | tf_op jit(solution)/shard_map/direction_update/pallas_call | solution.py:171
  (114 shorter events, 39.3 us)
Async XLA Ops:
  1.6 5.6 %collective-permute-start = (s32[32,8]{0,1:T(8,128)S(1)}, s32[32,8]{0,1:T(8,128)S(1)}, u32[]{:S(2)}, u32[]{:S(2)}) collective-permute-start(s32[32,8]{0,1:T(8,128)S(1)} %pad_add_fusion.4), channel_id=1, source_target_pairs={{0,8},{1,9},{2,10},{3,11},{4,12},{5,13},{6,14},{7,15},{8,0},{9,1},... | collective-permute-start | bytes 3080 | tf_op jit(solution)/shard_map/ppermute | solution.py:772
  7.2 3.7 %collective-permute-start.1 = (s32[2,32,8]{1,2,0:T(8,128)S(1)}, s32[2,32,8]{1,2,0:T(8,128)S(1)}, u32[]{:S(2)}, u32[]{:S(2)}) collective-permute-start(s32[2,32,8]{1,2,0:T(8,128)S(1)} %get-tuple-element.133), channel_id=1, source_target_pairs={{0,4},{1,5},{2,6},{3,7},{4,0},{5,1},{6,2},{7,3},{8,12},{9,13},{10,... | collective-permute-start | bytes 6152 | tf_op jit(solution)/shard_map/ppermute | solution.py:772
  10.8 3.7 %collective-permute-start.2 = (s32[2,2,32,8]{2,3,1,0:T(8,128)S(1)}, s32[2,2,32,8]{2,3,1,0:T(8,128)S(1)}, u32[]{:S(2)}, u32[]{:S(2)}) collective-permute-start(s32[2,2,32,8]{2,3,1,0:T(8,128)S(1)} %get-tuple-element.131), channel_id=1, source_target_pairs={{0,2},{1,3},{2,0},{3,1},{4,6},{5,7},{6,4},{7,5},{8,10},{9,11},{10,... | collective-permute-start | bytes 12296 | tf_op jit(solution)/shard_map/ppermute | solution.py:772
  24.8 6.2 %collective-permute-start.8 = (f32[8,64,384]{2,1,0:T(8,128)S(1)}, f32[8,64,384]{2,1,0:T(8,128)S(1)}, u32[]{:S(2)}, u32[]{:S(2)}) collective-permute-start(f32[8,64,384]{2,1,0:T(8,128)S(1)} %get-tuple-element.69), channel_id=1, source_target_pairs={{0,1},{1,0},{2,3},{3,2},{4,5},{5,4},{6,7},{7,6},{8,9},{9,8},{10,11... | collective-permute-start | bytes 2359304 | tf_op jit(solution)/shard_map/ppermute | solution.py:772
  29.0 9.8 %collective-permute-start.5 = (f32[4,16,1024]{2,1,0:T(8,128)S(1)}, f32[4,16,1024]{2,1,0:T(8,128)S(1)}, u32[]{:S(2)}, u32[]{:S(2)}) collective-permute-start(f32[4,16,1024]{2,1,0:T(8,128)S(1)} %row_cells.5), channel_id=1, source_target_pairs={{0,4},{1,5},{2,6},{3,7},{4,0},{5,1},{6,2},{7,3},{8,12},{9,13},{10,... | collective-permute-start | bytes 786440 | tf_op jit(solution)/shard_map/ppermute | solution.py:772
  33.1 8.5 %collective-permute-start.9 = (f32[4,16,1024]{2,1,0:T(8,128)S(1)}, f32[4,16,1024]{2,1,0:T(8,128)S(1)}, u32[]{:S(2)}, u32[]{:S(2)}) collective-permute-start(f32[4,16,1024]{2,1,0:T(8,128)S(1)} %row_cells.7), channel_id=1, source_target_pairs={{0,2},{1,3},{2,0},{3,1},{4,6},{5,7},{6,4},{7,5},{8,10},{9,11},{10,... | collective-permute-start | bytes 786440 | tf_op jit(solution)/shard_map/ppermute | solution.py:772
  38.9 8.8 %collective-permute-start.6 = (f32[2,16,1024]{2,1,0:T(8,128)S(1)}, f32[2,16,1024]{2,1,0:T(8,128)S(1)}, u32[]{:S(2)}, u32[]{:S(2)}) collective-permute-start(f32[2,16,1024]{2,1,0:T(8,128)S(1)} %slice.35), channel_id=1, source_target_pairs={{0,8},{1,9},{2,10},{3,11},{4,12},{5,13},{6,14},{7,15},{8,0},{9,1},... | collective-permute-start | bytes 393224 | tf_op jit(solution)/shard_map/ppermute | solution.py:772
  41.6 7.5 %collective-permute-start.10 = (f32[2,16,1024]{2,1,0:T(8,128)S(1)}, f32[2,16,1024]{2,1,0:T(8,128)S(1)}, u32[]{:S(2)}, u32[]{:S(2)}) collective-permute-start(f32[2,16,1024]{2,1,0:T(8,128)S(1)} %slice_bitcast_fusion), channel_id=1, source_target_pairs={{0,4},{1,5},{2,6},{3,7},{4,0},{5,1},{6,2},{7,3},{8,12},{9,13},{10,... | collective-permute-start | bytes 393224 | tf_op jit(solution)/shard_map/ppermute | solution.py:772
  47.7 4.3 %collective-permute-start.7 = (f32[16,1024]{1,0:T(8,128)S(1)}, f32[16,1024]{1,0:T(8,128)S(1)}, u32[]{:S(2)}, u32[]{:S(2)}) collective-permute-start(f32[16,1024]{1,0:T(8,128)S(1)} %get-tuple-element.128), channel_id=1, source_target_pairs={{0,2},{1,3},{2,0},{3,1},{4,6},{5,7},{6,4},{7,5},{8,10},{9,11},{10,... | collective-permute-start | bytes 196616 | tf_op jit(solution)/shard_map/ppermute | solution.py:772
  49.2 5.6 %collective-permute-start.11 = (f32[16,1024]{1,0:T(8,128)S(1)}, f32[16,1024]{1,0:T(8,128)S(1)}, u32[]{:S(2)}, u32[]{:S(2)}) collective-permute-start(f32[16,1024]{1,0:T(8,128)S(1)} %get-tuple-element.126), channel_id=1, source_target_pairs={{0,8},{1,9},{2,10},{3,11},{4,12},{5,13},{6,14},{7,15},{8,0},{9,1},... | collective-permute-start | bytes 196616 | tf_op jit(solution)/shard_map/ppermute | solution.py:772
  56.4 5.4 %collective-permute-start.12 = (f32[16,1024]{1,0:T(8,128)S(1)}, f32[16,1024]{1,0:T(8,128)S(1)}, u32[]{:S(2)}, u32[]{:S(2)}) collective-permute-start(f32[16,1024]{1,0:T(8,128)S(1)} %get-tuple-element.72), channel_id=1, source_target_pairs={{0,8},{1,9},{2,10},{3,11},{4,12},{5,13},{6,14},{7,15},{8,0},{9,1},... | collective-permute-start | bytes 196616 | tf_op jit(solution)/shard_map/ppermute | solution.py:772
  56.5 5.3 %collective-permute-start.14 = (f32[8,128]{1,0:T(8,128)S(1)}, f32[8,128]{1,0:T(8,128)S(1)}, u32[]{:S(2)}, u32[]{:S(2)}) collective-permute-start(f32[8,128]{1,0:T(8,128)S(1)} %get-tuple-element.74), channel_id=1, source_target_pairs={{0,8},{1,9},{2,10},{3,11},{4,12},{5,13},{6,14},{7,15},{8,0},{9,1},... | collective-permute-start | bytes 12296 | tf_op jit(solution)/shard_map/ppermute | solution.py:772
  59.4 4.3 %collective-permute-start.13 = (f32[16,1024]{1,0:T(8,128)S(1)}, f32[16,1024]{1,0:T(8,128)S(1)}, u32[]{:S(2)}, u32[]{:S(2)}) collective-permute-start(f32[16,1024]{1,0:T(8,128)S(1)} %get-tuple-element.73), channel_id=1, source_target_pairs={{0,2},{1,3},{2,0},{3,1},{4,6},{5,7},{6,4},{7,5},{8,10},{9,11},{10,... | collective-permute-start | bytes 196616 | tf_op jit(solution)/shard_map/ppermute | solution.py:772
  63.7 7.0 %collective-permute-start.15 = (f32[2,16,1024]{2,1,0:T(8,128)S(1)}, f32[2,16,1024]{2,1,0:T(8,128)S(1)}, u32[]{:S(2)}, u32[]{:S(2)}) collective-permute-start(f32[2,16,1024]{2,1,0:T(8,128)S(1)} %pad_maximum_fusion.4), channel_id=1, source_target_pairs={{0,4},{1,5},{2,6},{3,7},{4,0},{5,1},{6,2},{7,3},{8,12},{9,13},{10,... | collective-permute-start | bytes 393224 | tf_op jit(solution)/shard_map/ppermute | solution.py:772
  63.8 6.9 %collective-permute-start.16 = (f32[2,16,1024]{2,1,0:T(8,128)S(1)}, f32[2,16,1024]{2,1,0:T(8,128)S(1)}, u32[]{:S(2)}, u32[]{:S(2)}) collective-permute-start(f32[2,16,1024]{2,1,0:T(8,128)S(1)} %pad_maximum_fusion.5), channel_id=1, source_target_pairs={{0,8},{1,9},{2,10},{3,11},{4,12},{5,13},{6,14},{7,15},{8,0},{9,1},... | collective-permute-start | bytes 393224 | tf_op jit(solution)/shard_map/ppermute | solution.py:772
  66.5 4.2 %collective-permute-start.17 = (f32[8,128]{1,0:T(8,128)S(1)}, f32[8,128]{1,0:T(8,128)S(1)}, u32[]{:S(2)}, u32[]{:S(2)}) collective-permute-start(f32[8,128]{1,0:T(8,128)S(1)} %add.132), channel_id=1, source_target_pairs={{0,4},{1,5},{2,6},{3,7},{4,0},{5,1},{6,2},{7,3},{8,12},{9,13},{10,... | collective-permute-start | bytes 12296 | tf_op jit(solution)/shard_map/ppermute | solution.py:772
  70.7 12.3 %collective-permute-start.18 = (f32[2,2,16,1024]{3,2,0,1:T(8,128)S(1)}, f32[2,2,16,1024]{3,2,0,1:T(8,128)S(1)}, u32[]{:S(2)}, u32[]{:S(2)}) collective-permute-start(f32[2,2,16,1024]{3,2,0,1:T(8,128)S(1)} %pad_maximum_fusion.2), channel_id=1, source_target_pairs={{0,2},{1,3},{2,0},{3,1},{4,6},{5,7},{6,4},{7,5},{8,10},{9,11},{10,... | collective-permute-start | bytes 786440 | tf_op jit(solution)/shard_map/ppermute | solution.py:772
  72.2 10.8 %collective-permute-start.19 = (f32[2,2,16,1024]{3,2,1,0:T(8,128)S(1)}, f32[2,2,16,1024]{3,2,1,0:T(8,128)S(1)}, u32[]{:S(2)}, u32[]{:S(2)}) collective-permute-start(f32[2,2,16,1024]{3,2,1,0:T(8,128)S(1)} %pad_maximum_fusion.3), channel_id=1, source_target_pairs={{0,4},{1,5},{2,6},{3,7},{4,0},{5,1},{6,2},{7,3},{8,12},{9,13},{10,... | collective-permute-start | bytes 786440 | tf_op jit(solution)/shard_map/ppermute | solution.py:772
  72.6 10.4 %collective-permute-start.20 = (f32[8,128]{1,0:T(8,128)S(1)}, f32[8,128]{1,0:T(8,128)S(1)}, u32[]{:S(2)}, u32[]{:S(2)}) collective-permute-start(f32[8,128]{1,0:T(8,128)S(1)} %add.133), channel_id=1, source_target_pairs={{0,2},{1,3},{2,0},{3,1},{4,6},{5,7},{6,4},{7,5},{8,10},{9,11},{10,... | collective-permute-start | bytes 12296 | tf_op jit(solution)/shard_map/ppermute | solution.py:772
  79.4 8.8 %collective-permute-start.22 = (f32[4,64,384]{2,1,0:T(8,128)S(1)}, f32[4,64,384]{2,1,0:T(8,128)S(1)}, u32[]{:S(2)}, u32[]{:S(2)}) collective-permute-start(f32[4,64,384]{2,1,0:T(8,128)S(1)} %get-tuple-element.91.refs_7_), channel_id=1, source_target_pairs={{0,1},{1,0},{2,3},{3,2},{4,5},{5,4},{6,7},{7,6},{8,9},{9,8},{10,11... | collective-permute-start | bytes 1179656 | tf_op jit(solution)/shard_map/ppermute | solution.py:772
  82.4 5.8 %collective-permute-start.24 = (f32[4,64,384]{2,1,0:T(8,128)S(1)}, f32[4,64,384]{2,1,0:T(8,128)S(1)}, u32[]{:S(2)}, u32[]{:S(2)}) collective-permute-start(f32[4,64,384]{2,1,0:T(8,128)S(1)} %get-tuple-element.93.refs_11_), channel_id=1, source_target_pairs={{0,1},{1,0},{2,3},{3,2},{4,5},{5,4},{6,7},{7,6},{8,9},{9,8},{10,11... | collective-permute-start | bytes 1179656 | tf_op jit(solution)/shard_map/ppermute | solution.py:772
  94.4 4.6 %collective-permute-start.26 = (f32[8,128]{1,0:T(8,128)S(1)}, f32[8,128]{1,0:T(8,128)S(1)}, u32[]{:S(2)}, u32[]{:S(2)}) collective-permute-start(f32[8,128]{1,0:T(8,128)S(1)} %get-tuple-element.96), channel_id=1, source_target_pairs={{0,8},{1,9},{2,10},{3,11},{4,12},{5,13},{6,14},{7,15},{8,0},{9,1},... | collective-permute-start | bytes 12296 | tf_op jit(solution)/shard_map/ppermute | solution.py:772
  98.9 3.6 %collective-permute-start.27 = (f32[8,128]{1,0:T(8,128)S(1)}, f32[8,128]{1,0:T(8,128)S(1)}, u32[]{:S(2)}, u32[]{:S(2)}) collective-permute-start(f32[8,128]{1,0:T(8,128)S(1)} %add.136), channel_id=1, source_target_pairs={{0,4},{1,5},{2,6},{3,7},{4,0},{5,1},{6,2},{7,3},{8,12},{9,13},{10,... | collective-permute-start | bytes 12296 | tf_op jit(solution)/shard_map/ppermute | solution.py:772
  102.5 3.6 %collective-permute-start.28 = (f32[8,128]{1,0:T(8,128)S(1)}, f32[8,128]{1,0:T(8,128)S(1)}, u32[]{:S(2)}, u32[]{:S(2)}) collective-permute-start(f32[8,128]{1,0:T(8,128)S(1)} %add.137), channel_id=1, source_target_pairs={{0,2},{1,3},{2,0},{3,1},{4,6},{5,7},{6,4},{7,5},{8,10},{9,11},{10,... | collective-permute-start | bytes 12296 | tf_op jit(solution)/shard_map/ppermute | solution.py:772
  (15 other events, 108.8 us)

commit v6 on v5

--- a/solution.py
+++ b/solution.py
@@ -881,8 +881,8 @@
         other = [swap(value, bit, slabs) for value, bit in zip(spread, ways)]
         if not False:
             sums = [sums[0] + swap(sums[0], high_bits[-1 - number], slabs)]
-        if 1 <= number < 1 + 2:
-            loaded.append(load(inputs[number - 1]))
+        if number == 1:
+            loaded += [load(value) for value in inputs]
         if number == len(high_bits) - 1:
             for c in range(coils):
                 had = spread[c].reshape((-1,) + dims[c])

time: 110 us -> 109 us (level)
  transfers between devices with their start and end apart: 30 -> 30, of which waited for: 17 -> 16; matrix products, arithmetic and copies ran while one was open for 2% -> 2% of each run, Pallas kernels for 24% -> 25%
where the time goes in v6:
time: 109 us
  Pallas kernels  45.4 us (42%)
  starting transfers between devices  29.4 us (27%)
  waiting for transfers between devices  29.1 us (27%)
  other arithmetic  3.12 us (3%)
  between operations  1.26 us (1%)
    ppermute x30, starting transfers between devices, swap(): return lax.ppermute(value, 'slab', [(i, i ^ bit) for i in range(slabs)])  29.4 us
    ppermute x30, waiting for transfers between devices, swap(): return lax.ppermute(value, 'slab', [(i, i ^ bit) for i in range(slabs)])  29.1 us
    pallas_call x1, Pallas kernels, partial_rows(): pl.pallas_call(lambda *refs: rows_kernel(planes, slabs_group, steps, *ref...  8.61 us
    pallas_call x4, Pallas kernels, row_cells(): pl.pallas_call(lambda *refs: cells_kernel(tiles, segment, bit, side, *ref...  8.3 us
    pallas_call x4, Pallas kernels, adjoint_rows(): pl.pallas_call(lambda *refs: adjoint_kernel(segment, bit, side, part, ste...  8.29 us
    pallas_call x1, Pallas kernels, finish(): pl.pallas_call(lambda *refs: finish_kernel(planes, *refs), in_specs=[scal...  6.09 us
    pallas_call x2, Pallas kernels, load(): pl.pallas_call(load_kernel, in_specs=[in_hbm()], out_specs=resident(), ou...  4.9 us
    pallas_call x3, Pallas kernels, x_update(): pl.pallas_call(lambda *refs: x_kernel(piece * rows, *refs), grid=(2,), in...  3.85 us
  transfers between devices with their start and end apart: 30, of which 16 were waited for; matrix products, arithmetic and copies ran while one was open for 2% of the time, Pallas kernels for 25%

profile of v6, /device:TPU:0, one launch (start us, length us, event | category | flops | bytes accessed | tf_op | source)
XLA Modules:
  0.0 108.7 jit_solution(4792273872373261183)
XLA Ops:
  1.6 4.0 %collective-permute-start = (s32[32,8]{0,1:T(8,128)S(1)}, s32[32,8]{0,1:T(8,128)S(1)}, u32[]{:S(2)}, u32[]{:S(2)}) collective-permute-start(s32[32,8]{0,1:T(8,128)S(1)} %pad_add_fusion.4), channel_id=1, source_target_pairs={{0,8},{1,9},{2,10},{3,11},{4,12},{5,13},{6,14},{7,15},{8,0},{9,1},... | collective-permute-start | bytes 3080 | tf_op jit(solution)/shard_map/ppermute | solution.py:772
  7.2 1.9 %collective-permute-start.1 = (s32[2,32,8]{1,2,0:T(8,128)S(1)}, s32[2,32,8]{1,2,0:T(8,128)S(1)}, u32[]{:S(2)}, u32[]{:S(2)}) collective-permute-start(s32[2,32,8]{1,2,0:T(8,128)S(1)} %get-tuple-element.133), channel_id=1, source_target_pairs={{0,4},{1,5},{2,6},{3,7},{4,0},{5,1},{6,2},{7,3},{8,12},{9,13},{10,... | collective-permute-start | bytes 6152 | tf_op jit(solution)/shard_map/ppermute | solution.py:772
  10.8 1.8 %collective-permute-start.2 = (s32[2,2,32,8]{2,3,1,0:T(8,128)S(1)}, s32[2,2,32,8]{2,3,1,0:T(8,128)S(1)}, u32[]{:S(2)}, u32[]{:S(2)}) collective-permute-start(s32[2,2,32,8]{2,3,1,0:T(8,128)S(1)} %get-tuple-element.131), channel_id=1, source_target_pairs={{0,2},{1,3},{2,0},{3,1},{4,6},{5,7},{6,4},{7,5},{8,10},{9,11},{10,... | collective-permute-start | bytes 12296 | tf_op jit(solution)/shard_map/ppermute | solution.py:772
  15.9 8.6 %partial_rows.1 = (f32[8,64,384]{2,1,0:T(8,128)S(1)}, f32[8,64,384]{2,1,0:T(8,128)S(1)}, f32[8,64,384]{2,1,0:T(8,128)S(1)}, f32[8,64,384]{2,1,0:T(8,128)S(1)}, b...) custom-call(s32[1]{0:T(128)} %bitcast.refs_0_, s32[8,2,32,8]{3,2,1,0:T(8,128)S(1)} %pad_add_fusion.refs_1_.refs_2_, ...), custom_call_target="tpu_custom_call" | custom-call | tf_op jit(solution)/shard_map/partial_rows/pallas_call | solution.py:348
  26.9 2.1 %row_cells.5 = f32[4,16,1024]{2,1,0:T(8,128)S(1)} custom-call(f32[8,64,384]{2,1,0:T(8,128)S(1)} %get-tuple-element.59.refs_0_, f32[8,64,384]{2,1,0:T(8,128)S(1)} %collective-permute-done.4.refs_1_, s32[8,2,32,8]{3,2,1,0:T(8,128)S(1)} %pad_add_fusion.refs_1_.refs_2_, f32[16,768]{1,0:T(8,128)S(1)} %copy-done.2, bf16[3,768,512]{2,1,0:T(8,128)(2,1)S(1)} %copy-done), custom_call_target="tpu_custom_call" | custom-call | tf_op jit(solution)/shard_map/row_cells/pallas_call | solution.py:437
  29.0 2.0 %collective-permute-start.5 = (f32[4,16,1024]{2,1,0:T(8,128)S(1)}, f32[4,16,1024]{2,1,0:T(8,128)S(1)}, u32[]{:S(2)}, u32[]{:S(2)}) collective-permute-start(f32[4,16,1024]{2,1,0:T(8,128)S(1)} %row_cells.5), channel_id=1, source_target_pairs={{0,4},{1,5},{2,6},{3,7},{4,0},{5,1},{6,2},{7,3},{8,12},{9,13},{10,... | collective-permute-start | bytes 786440 | tf_op jit(solution)/shard_map/ppermute | solution.py:772
  31.0 2.1 %row_cells.7 = f32[4,16,1024]{2,1,0:T(8,128)S(1)} custom-call(f32[8,64,384]{2,1,0:T(8,128)S(1)} %get-tuple-element.68.refs_0_, f32[8,64,384]{2,1,0:T(8,128)S(1)} %collective-permute-done.8.refs_1_, s32[8,2,32,8]{3,2,1,0:T(8,128)S(1)} %pad_add_fusion.refs_1_.refs_2_, f32[16,768]{1,0:T(8,128)S(1)} %copy-done.2, bf16[3,768,512]{2,1,0:T(8,128)(2,1)S(1)} %copy-done), custom_call_target="tpu_custom_call" | custom-call | tf_op jit(solution)/shard_map/row_cells/pallas_call | solution.py:437
  34.6 2.1 %row_cells.4 = f32[4,16,1024]{2,1,0:T(8,128)S(1)} custom-call(f32[8,64,384]{2,1,0:T(8,128)S(1)} %get-tuple-element.59.refs_0_, f32[8,64,384]{2,1,0:T(8,128)S(1)} %collective-permute-done.4.refs_1_, s32[8,2,32,8]{3,2,1,0:T(8,128)S(1)} %pad_add_fusion.refs_1_.refs_2_, f32[16,768]{1,0:T(8,128)S(1)} %copy-done.2, bf16[3,768,512]{2,1,0:T(8,128)(2,1)S(1)} %copy-done), custom_call_target="tpu_custom_call" | custom-call | tf_op jit(solution)/shard_map/row_cells/pallas_call | solution.py:437
  36.7 2.1 %row_cells.6 = f32[4,16,1024]{2,1,0:T(8,128)S(1)} custom-call(f32[8,64,384]{2,1,0:T(8,128)S(1)} %get-tuple-element.68.refs_0_, f32[8,64,384]{2,1,0:T(8,128)S(1)} %collective-permute-done.8.refs_1_, s32[8,2,32,8]{3,2,1,0:T(8,128)S(1)} %pad_add_fusion.refs_1_.refs_2_, f32[16,768]{1,0:T(8,128)S(1)} %copy-done.2, bf16[3,768,512]{2,1,0:T(8,128)(2,1)S(1)} %copy-done), custom_call_target="tpu_custom_call" | custom-call | tf_op jit(solution)/shard_map/row_cells/pallas_call | solution.py:437
  38.9 2.7 %collective-permute-start.6 = (f32[2,16,1024]{2,1,0:T(8,128)S(1)}, f32[2,16,1024]{2,1,0:T(8,128)S(1)}, u32[]{:S(2)}, u32[]{:S(2)}) collective-permute-start(f32[2,16,1024]{2,1,0:T(8,128)S(1)} %slice.35), channel_id=1, source_target_pairs={{0,8},{1,9},{2,10},{3,11},{4,12},{5,13},{6,14},{7,15},{8,0},{9,1},... | collective-permute-start | bytes 393224 | tf_op jit(solution)/shard_map/ppermute | solution.py:772
  42.2 5.5 %collective-permute-done.6 = f32[2,16,1024]{2,1,0:T(8,128)S(1)} collective-permute-done((f32[2,16,1024]{2,1,0:T(8,128)S(1)}, f32[2,16,1024]{2,1,0:T(8,128)S(1)}, u32[]{:S(2)}, u32[]{:S(2)}) %collective-permute-start.6) | collective-permute-done | bytes 131104 | tf_op jit(solution)/shard_map/ppermute | solution.py:772
  52.1 2.7 %collective-permute-done.11.refs_5_ = f32[16,1024]{1,0:T(8,128)S(1)} collective-permute-done((f32[16,1024]{1,0:T(8,128)S(1)}, f32[16,1024]{1,0:T(8,128)S(1)}, u32[]{:S(2)}, u32[]{:S(2)}) %collective-permute-start.11) | collective-permute-done | bytes 65568 | tf_op jit(solution)/shard_map/ppermute | solution.py:772
  56.5 2.9 %collective-permute-start.14 = (f32[8,128]{1,0:T(8,128)S(1)}, f32[8,128]{1,0:T(8,128)S(1)}, u32[]{:S(2)}, u32[]{:S(2)}) collective-permute-start(f32[8,128]{1,0:T(8,128)S(1)} %get-tuple-element.74), channel_id=1, source_target_pairs={{0,8},{1,9},{2,10},{3,11},{4,12},{5,13},{6,14},{7,15},{8,0},{9,1},... | collective-permute-start | bytes 12296 | tf_op jit(solution)/shard_map/ppermute | solution.py:772
  61.8 1.9 %collective-permute-done.13 = f32[16,1024]{1,0:T(8,128)S(1)} collective-permute-done((f32[16,1024]{1,0:T(8,128)S(1)}, f32[16,1024]{1,0:T(8,128)S(1)}, u32[]{:S(2)}, u32[]{:S(2)}) %collective-permute-start.13) | collective-permute-done | bytes 65568 | tf_op jit(solution)/shard_map/ppermute | solution.py:772
  63.8 2.6 %collective-permute-start.16 = (f32[2,16,1024]{2,1,0:T(8,128)S(1)}, f32[2,16,1024]{2,1,0:T(8,128)S(1)}, u32[]{:S(2)}, u32[]{:S(2)}) collective-permute-start(f32[2,16,1024]{2,1,0:T(8,128)S(1)} %pad_maximum_fusion.5), channel_id=1, source_target_pairs={{0,8},{1,9},{2,10},{3,11},{4,12},{5,13},{6,14},{7,15},{8,0},{9,1},... | collective-permute-start | bytes 393224 | tf_op jit(solution)/shard_map/ppermute | solution.py:772
  66.5 2.4 %load.2.refs_4_ = f32[2,24,64,384]{3,2,1,0:T(8,128)S(1)} custom-call(f32[2,24,64,384]{3,2,1,0:T(8,128)} %from_hbm), custom_call_target="tpu_custom_call" | custom-call | tf_op jit(solution)/shard_map/load/pallas_call | solution.py:92
  68.9 2.5 %load.3.refs_5_ = f32[2,24,64,384]{3,2,1,0:T(8,128)S(1)} custom-call(f32[2,24,64,384]{3,2,1,0:T(8,128)} %from_hbm.1), custom_call_target="tpu_custom_call" | custom-call | tf_op jit(solution)/shard_map/load/pallas_call | solution.py:92
  72.6 1.9 %collective-permute-start.19 = (f32[2,2,16,1024]{3,2,1,0:T(8,128)S(1)}, f32[2,2,16,1024]{3,2,1,0:T(8,128)S(1)}, u32[]{:S(2)}, u32[]{:S(2)}) collective-permute-start(f32[2,2,16,1024]{3,2,1,0:T(8,128)S(1)} %pad_maximum_fusion.3), channel_id=1, source_target_pairs={{0,4},{1,5},{2,6},{3,7},{4,0},{5,1},{6,2},{7,3},{8,12},{9,13},{10,... | collective-permute-start | bytes 786440 | tf_op jit(solution)/shard_map/ppermute | solution.py:772
  75.6 2.5 %adjoint_rows.4 = (f32[4,64,384]{2,1,0:T(8,128)S(1)}, f32[2,24,64,384]{3,2,1,0:T(8,128)S(1)}) custom-call(f32[4,16,1024]{2,1,0:T(8,128)S(1)} %bitcast.91, s32[8,2,32,8]{3,2,1,0:T(8,128)S(1)} %pad_add_fusion.refs_1_.refs_2_, f32[16,768]{1,0:T(8,128)S(1)} %copy-done.2, bf16[2,1024,384]{2,1,0:T(8,128)(2,1)S(1)} %copy-done.1, f32[2,2,24,64,384]{4,3,2,1,0:T(8,128)} %refs_4_.7), custom_call_target="tpu_custom_call" | custom-call | tf_op jit(solution)/shard_map/adjoint_rows/pallas_call | solution.py:512
  78.3 3.0 %adjoint_rows.5 = (f32[4,64,384]{2,1,0:T(8,128)S(1)}, f32[2,24,64,384]{3,2,1,0:T(8,128)S(1)}) custom-call(f32[4,16,1024]{2,1,0:T(8,128)S(1)} %bitcast.90, s32[8,2,32,8]{3,2,1,0:T(8,128)S(1)} %pad_add_fusion.refs_1_.refs_2_, f32[16,768]{1,0:T(8,128)S(1)} %copy-done.2, bf16[2,1024,384]{2,1,0:T(8,128)(2,1)S(1)} %copy-done.1, f32[2,2,24,64,384]{4,3,2,1,0:T(8,128)} %refs_4_.7), custom_call_target="tpu_custom_call" | custom-call | tf_op jit(solution)/shard_map/adjoint_rows/pallas_call | solution.py:512
  87.1 6.1 %finish.1 = (f32[2,24,64,384]{3,2,1,0:T(8,128)}, f32[2,24,64,384]{3,2,1,0:T(8,128)S(1)}, f32[8,128]{1,0:T(8,128)S(1)}) custom-call(s32[1]{0:T(128)} %bitcast.refs_0_, f32[8,128]{1,0:T(8,128)S(1)} %add.135.refs_1_.refs_0_.sums_ref, f32[2,24,64,384]{3,2,1,0:T(8,128)S(1)} %get-tuple-element.86.refs_2_, f32[2,24,64,384]{3,2,1,0:T(8,128)S(1)} %get-tuple-element.87.refs_3_, ...), custom_call_target="tpu_custom_call" | custom-call | tf_op jit(solution)/shard_map/finish/pallas_call | solution.py:687
  94.8 2.9 %collective-permute-done.26 = f32[8,128]{1,0:T(8,128)S(1)} collective-permute-done((f32[8,128]{1,0:T(8,128)S(1)}, f32[8,128]{1,0:T(8,128)S(1)}, u32[]{:S(2)}, u32[]{:S(2)}) %collective-permute-start.26) | collective-permute-done | bytes 4128 | tf_op jit(solution)/shard_map/ppermute | solution.py:772
  99.1 2.2 %collective-permute-done.27 = f32[8,128]{1,0:T(8,128)S(1)} collective-permute-done((f32[8,128]{1,0:T(8,128)S(1)}, f32[8,128]{1,0:T(8,128)S(1)}, u32[]{:S(2)}, u32[]{:S(2)}) %collective-permute-start.27) | collective-permute-done | bytes 4128 | tf_op jit(solution)/shard_map/ppermute | solution.py:772
  106.1 2.4 %direction_update.1 = f32[48,64,384]{2,1,0:T(8,128)} custom-call(f32[8,128]{1,0:T(8,128)S(1)} %add.135.refs_1_.refs_0_.sums_ref, f32[8,128]{1,0:T(8,128)S(1)} %add.138.one_ref, f32[8,128]{1,0:T(8,128)S(1)} %collective-permute-done.29.two_ref, f32[48,64,384]{2,1,0:T(8,128)S(1)} %bitcast.89, f32[48,64,384]{2,1,0:T(8,128)S(1)} %bitcast.81), custom_call_target="tpu_custom_call" | custom-call | tf_op jit(solution)/shard_map/direction_update/pallas_call | solution.py:171
  (114 shorter events, 36.4 us)
Async XLA Ops:
  1.6 5.6 %collective-permute-start = (s32[32,8]{0,1:T(8,128)S(1)}, s32[32,8]{0,1:T(8,128)S(1)}, u32[]{:S(2)}, u32[]{:S(2)}) collective-permute-start(s32[32,8]{0,1:T(8,128)S(1)} %pad_add_fusion.4), channel_id=1, source_target_pairs={{0,8},{1,9},{2,10},{3,11},{4,12},{5,13},{6,14},{7,15},{8,0},{9,1},... | collective-permute-start | bytes 3080 | tf_op jit(solution)/shard_map/ppermute | solution.py:772
  7.2 3.7 %collective-permute-start.1 = (s32[2,32,8]{1,2,0:T(8,128)S(1)}, s32[2,32,8]{1,2,0:T(8,128)S(1)}, u32[]{:S(2)}, u32[]{:S(2)}) collective-permute-start(s32[2,32,8]{1,2,0:T(8,128)S(1)} %get-tuple-element.133), channel_id=1, source_target_pairs={{0,4},{1,5},{2,6},{3,7},{4,0},{5,1},{6,2},{7,3},{8,12},{9,13},{10,... | collective-permute-start | bytes 6152 | tf_op jit(solution)/shard_map/ppermute | solution.py:772
  10.8 3.7 %collective-permute-start.2 = (s32[2,2,32,8]{2,3,1,0:T(8,128)S(1)}, s32[2,2,32,8]{2,3,1,0:T(8,128)S(1)}, u32[]{:S(2)}, u32[]{:S(2)}) collective-permute-start(s32[2,2,32,8]{2,3,1,0:T(8,128)S(1)} %get-tuple-element.131), channel_id=1, source_target_pairs={{0,2},{1,3},{2,0},{3,1},{4,6},{5,7},{6,4},{7,5},{8,10},{9,11},{10,... | collective-permute-start | bytes 12296 | tf_op jit(solution)/shard_map/ppermute | solution.py:772
  24.8 6.2 %collective-permute-start.8 = (f32[8,64,384]{2,1,0:T(8,128)S(1)}, f32[8,64,384]{2,1,0:T(8,128)S(1)}, u32[]{:S(2)}, u32[]{:S(2)}) collective-permute-start(f32[8,64,384]{2,1,0:T(8,128)S(1)} %get-tuple-element.69), channel_id=1, source_target_pairs={{0,1},{1,0},{2,3},{3,2},{4,5},{5,4},{6,7},{7,6},{8,9},{9,8},{10,11... | collective-permute-start | bytes 2359304 | tf_op jit(solution)/shard_map/ppermute | solution.py:772
  29.0 9.8 %collective-permute-start.5 = (f32[4,16,1024]{2,1,0:T(8,128)S(1)}, f32[4,16,1024]{2,1,0:T(8,128)S(1)}, u32[]{:S(2)}, u32[]{:S(2)}) collective-permute-start(f32[4,16,1024]{2,1,0:T(8,128)S(1)} %row_cells.5), channel_id=1, source_target_pairs={{0,4},{1,5},{2,6},{3,7},{4,0},{5,1},{6,2},{7,3},{8,12},{9,13},{10,... | collective-permute-start | bytes 786440 | tf_op jit(solution)/shard_map/ppermute | solution.py:772
  33.1 8.5 %collective-permute-start.9 = (f32[4,16,1024]{2,1,0:T(8,128)S(1)}, f32[4,16,1024]{2,1,0:T(8,128)S(1)}, u32[]{:S(2)}, u32[]{:S(2)}) collective-permute-start(f32[4,16,1024]{2,1,0:T(8,128)S(1)} %row_cells.7), channel_id=1, source_target_pairs={{0,2},{1,3},{2,0},{3,1},{4,6},{5,7},{6,4},{7,5},{8,10},{9,11},{10,... | collective-permute-start | bytes 786440 | tf_op jit(solution)/shard_map/ppermute | solution.py:772
  38.9 8.8 %collective-permute-start.6 = (f32[2,16,1024]{2,1,0:T(8,128)S(1)}, f32[2,16,1024]{2,1,0:T(8,128)S(1)}, u32[]{:S(2)}, u32[]{:S(2)}) collective-permute-start(f32[2,16,1024]{2,1,0:T(8,128)S(1)} %slice.35), channel_id=1, source_target_pairs={{0,8},{1,9},{2,10},{3,11},{4,12},{5,13},{6,14},{7,15},{8,0},{9,1},... | collective-permute-start | bytes 393224 | tf_op jit(solution)/shard_map/ppermute | solution.py:772
  41.6 7.5 %collective-permute-start.10 = (f32[2,16,1024]{2,1,0:T(8,128)S(1)}, f32[2,16,1024]{2,1,0:T(8,128)S(1)}, u32[]{:S(2)}, u32[]{:S(2)}) collective-permute-start(f32[2,16,1024]{2,1,0:T(8,128)S(1)} %slice_bitcast_fusion), channel_id=1, source_target_pairs={{0,4},{1,5},{2,6},{3,7},{4,0},{5,1},{6,2},{7,3},{8,12},{9,13},{10,... | collective-permute-start | bytes 393224 | tf_op jit(solution)/shard_map/ppermute | solution.py:772
  47.7 4.3 %collective-permute-start.7 = (f32[16,1024]{1,0:T(8,128)S(1)}, f32[16,1024]{1,0:T(8,128)S(1)}, u32[]{:S(2)}, u32[]{:S(2)}) collective-permute-start(f32[16,1024]{1,0:T(8,128)S(1)} %get-tuple-element.128), channel_id=1, source_target_pairs={{0,2},{1,3},{2,0},{3,1},{4,6},{5,7},{6,4},{7,5},{8,10},{9,11},{10,... | collective-permute-start | bytes 196616 | tf_op jit(solution)/shard_map/ppermute | solution.py:772
  49.2 5.6 %collective-permute-start.11 = (f32[16,1024]{1,0:T(8,128)S(1)}, f32[16,1024]{1,0:T(8,128)S(1)}, u32[]{:S(2)}, u32[]{:S(2)}) collective-permute-start(f32[16,1024]{1,0:T(8,128)S(1)} %get-tuple-element.126), channel_id=1, source_target_pairs={{0,8},{1,9},{2,10},{3,11},{4,12},{5,13},{6,14},{7,15},{8,0},{9,1},... | collective-permute-start | bytes 196616 | tf_op jit(solution)/shard_map/ppermute | solution.py:772
  56.4 5.4 %collective-permute-start.12 = (f32[16,1024]{1,0:T(8,128)S(1)}, f32[16,1024]{1,0:T(8,128)S(1)}, u32[]{:S(2)}, u32[]{:S(2)}) collective-permute-start(f32[16,1024]{1,0:T(8,128)S(1)} %get-tuple-element.72), channel_id=1, source_target_pairs={{0,8},{1,9},{2,10},{3,11},{4,12},{5,13},{6,14},{7,15},{8,0},{9,1},... | collective-permute-start | bytes 196616 | tf_op jit(solution)/shard_map/ppermute | solution.py:772
  56.5 5.3 %collective-permute-start.14 = (f32[8,128]{1,0:T(8,128)S(1)}, f32[8,128]{1,0:T(8,128)S(1)}, u32[]{:S(2)}, u32[]{:S(2)}) collective-permute-start(f32[8,128]{1,0:T(8,128)S(1)} %get-tuple-element.74), channel_id=1, source_target_pairs={{0,8},{1,9},{2,10},{3,11},{4,12},{5,13},{6,14},{7,15},{8,0},{9,1},... | collective-permute-start | bytes 12296 | tf_op jit(solution)/shard_map/ppermute | solution.py:772
  59.4 4.3 %collective-permute-start.13 = (f32[16,1024]{1,0:T(8,128)S(1)}, f32[16,1024]{1,0:T(8,128)S(1)}, u32[]{:S(2)}, u32[]{:S(2)}) collective-permute-start(f32[16,1024]{1,0:T(8,128)S(1)} %get-tuple-element.73), channel_id=1, source_target_pairs={{0,2},{1,3},{2,0},{3,1},{4,6},{5,7},{6,4},{7,5},{8,10},{9,11},{10,... | collective-permute-start | bytes 196616 | tf_op jit(solution)/shard_map/ppermute | solution.py:772
  63.7 7.8 %collective-permute-start.15 = (f32[2,16,1024]{2,1,0:T(8,128)S(1)}, f32[2,16,1024]{2,1,0:T(8,128)S(1)}, u32[]{:S(2)}, u32[]{:S(2)}) collective-permute-start(f32[2,16,1024]{2,1,0:T(8,128)S(1)} %pad_maximum_fusion.4), channel_id=1, source_target_pairs={{0,4},{1,5},{2,6},{3,7},{4,0},{5,1},{6,2},{7,3},{8,12},{9,13},{10,... | collective-permute-start | bytes 393224 | tf_op jit(solution)/shard_map/ppermute | solution.py:772
  63.8 7.7 %collective-permute-start.16 = (f32[2,16,1024]{2,1,0:T(8,128)S(1)}, f32[2,16,1024]{2,1,0:T(8,128)S(1)}, u32[]{:S(2)}, u32[]{:S(2)}) collective-permute-start(f32[2,16,1024]{2,1,0:T(8,128)S(1)} %pad_maximum_fusion.5), channel_id=1, source_target_pairs={{0,8},{1,9},{2,10},{3,11},{4,12},{5,13},{6,14},{7,15},{8,0},{9,1},... | collective-permute-start | bytes 393224 | tf_op jit(solution)/shard_map/ppermute | solution.py:772
  66.5 5.0 %collective-permute-start.17 = (f32[8,128]{1,0:T(8,128)S(1)}, f32[8,128]{1,0:T(8,128)S(1)}, u32[]{:S(2)}, u32[]{:S(2)}) collective-permute-start(f32[8,128]{1,0:T(8,128)S(1)} %add.132), channel_id=1, source_target_pairs={{0,4},{1,5},{2,6},{3,7},{4,0},{5,1},{6,2},{7,3},{8,12},{9,13},{10,... | collective-permute-start | bytes 12296 | tf_op jit(solution)/shard_map/ppermute | solution.py:772
  71.6 10.2 %collective-permute-start.18 = (f32[2,2,16,1024]{3,2,0,1:T(8,128)S(1)}, f32[2,2,16,1024]{3,2,0,1:T(8,128)S(1)}, u32[]{:S(2)}, u32[]{:S(2)}) collective-permute-start(f32[2,2,16,1024]{3,2,0,1:T(8,128)S(1)} %pad_maximum_fusion.2), channel_id=1, source_target_pairs={{0,2},{1,3},{2,0},{3,1},{4,6},{5,7},{6,4},{7,5},{8,10},{9,11},{10,... | collective-permute-start | bytes 786440 | tf_op jit(solution)/shard_map/ppermute | solution.py:772
  72.6 9.2 %collective-permute-start.19 = (f32[2,2,16,1024]{3,2,1,0:T(8,128)S(1)}, f32[2,2,16,1024]{3,2,1,0:T(8,128)S(1)}, u32[]{:S(2)}, u32[]{:S(2)}) collective-permute-start(f32[2,2,16,1024]{3,2,1,0:T(8,128)S(1)} %pad_maximum_fusion.3), channel_id=1, source_target_pairs={{0,4},{1,5},{2,6},{3,7},{4,0},{5,1},{6,2},{7,3},{8,12},{9,13},{10,... | collective-permute-start | bytes 786440 | tf_op jit(solution)/shard_map/ppermute | solution.py:772
  74.5 7.3 %collective-permute-start.20 = (f32[8,128]{1,0:T(8,128)S(1)}, f32[8,128]{1,0:T(8,128)S(1)}, u32[]{:S(2)}, u32[]{:S(2)}) collective-permute-start(f32[8,128]{1,0:T(8,128)S(1)} %add.133), channel_id=1, source_target_pairs={{0,2},{1,3},{2,0},{3,1},{4,6},{5,7},{6,4},{7,5},{8,10},{9,11},{10,... | collective-permute-start | bytes 12296 | tf_op jit(solution)/shard_map/ppermute | solution.py:772
  78.2 8.8 %collective-permute-start.22 = (f32[4,64,384]{2,1,0:T(8,128)S(1)}, f32[4,64,384]{2,1,0:T(8,128)S(1)}, u32[]{:S(2)}, u32[]{:S(2)}) collective-permute-start(f32[4,64,384]{2,1,0:T(8,128)S(1)} %get-tuple-element.91.refs_7_), channel_id=1, source_target_pairs={{0,1},{1,0},{2,3},{3,2},{4,5},{5,4},{6,7},{7,6},{8,9},{9,8},{10,11... | collective-permute-start | bytes 1179656 | tf_op jit(solution)/shard_map/ppermute | solution.py:772
  81.2 5.8 %collective-permute-start.24 = (f32[4,64,384]{2,1,0:T(8,128)S(1)}, f32[4,64,384]{2,1,0:T(8,128)S(1)}, u32[]{:S(2)}, u32[]{:S(2)}) collective-permute-start(f32[4,64,384]{2,1,0:T(8,128)S(1)} %get-tuple-element.93.refs_11_), channel_id=1, source_target_pairs={{0,1},{1,0},{2,3},{3,2},{4,5},{5,4},{6,7},{7,6},{8,9},{9,8},{10,11... | collective-permute-start | bytes 1179656 | tf_op jit(solution)/shard_map/ppermute | solution.py:772
  93.2 4.6 %collective-permute-start.26 = (f32[8,128]{1,0:T(8,128)S(1)}, f32[8,128]{1,0:T(8,128)S(1)}, u32[]{:S(2)}, u32[]{:S(2)}) collective-permute-start(f32[8,128]{1,0:T(8,128)S(1)} %get-tuple-element.96), channel_id=1, source_target_pairs={{0,8},{1,9},{2,10},{3,11},{4,12},{5,13},{6,14},{7,15},{8,0},{9,1},... | collective-permute-start | bytes 12296 | tf_op jit(solution)/shard_map/ppermute | solution.py:772
  97.7 3.6 %collective-permute-start.27 = (f32[8,128]{1,0:T(8,128)S(1)}, f32[8,128]{1,0:T(8,128)S(1)}, u32[]{:S(2)}, u32[]{:S(2)}) collective-permute-start(f32[8,128]{1,0:T(8,128)S(1)} %add.136), channel_id=1, source_target_pairs={{0,4},{1,5},{2,6},{3,7},{4,0},{5,1},{6,2},{7,3},{8,12},{9,13},{10,... | collective-permute-start | bytes 12296 | tf_op jit(solution)/shard_map/ppermute | solution.py:772
  101.3 3.6 %collective-permute-start.28 = (f32[8,128]{1,0:T(8,128)S(1)}, f32[8,128]{1,0:T(8,128)S(1)}, u32[]{:S(2)}, u32[]{:S(2)}) collective-permute-start(f32[8,128]{1,0:T(8,128)S(1)} %add.137), channel_id=1, source_target_pairs={{0,2},{1,3},{2,0},{3,1},{4,6},{5,7},{6,4},{7,5},{8,10},{9,11},{10,... | collective-permute-start | bytes 12296 | tf_op jit(solution)/shard_map/ppermute | solution.py:772
  (15 other events, 110.8 us)
